TPU v7x, 512 devices: a whole 4x4x16 slice. The times are simulated.
512 devices in a mesh: blk: 32 (over x, z_lo), head: 16 (over y, z_hi, core).
Axes of the slice: x: 4, y: 4, z: 16 (z_hi: 2, z_lo: 8; z = z_hi * 8 + z_lo), core: 2. Of those that a mesh axis runs over, the one named last changes fastest.
Arguments:
- query: bfloat16 [8192, 4096], P('blk', 'head'), may hold values from -6 to 6
- key: bfloat16 [8192, 256], P('blk'), may hold values from -6 to 6
- value: bfloat16 [8192, 256], P('blk'), may hold values from -6 to 6
- output: bfloat16 [8192, 4096], P('blk', 'head'), may hold values from -6 to 6
- grad_output: bfloat16 [8192, 4096], P('blk', 'head'), may hold values from -0.59765625 to 0.59765625
- log_norm: float32 [32, 8192], P('head', 'blk'), may hold values from 1 to 3
- entropy: float32 [32, 8192], P('head', 'blk'), may hold values from 0.5 to 4
- segment_ids: int32 [8192], replicated, may hold values from 0 to 15, never falling along the last dimension, each value on 1 to 2048 neighbouring positions
- weight_index: int32 [16], replicated, may hold values from 0 to 7
- penalty_weights: float32 [8], replicated, may hold values from 0.3 to 3
Outputs:
- grad_query: bfloat16 [8192, 4096], P('blk', 'head')
- grad_key: bfloat16 [8192, 256], P(('blk', 'head'))
- grad_value: bfloat16 [8192, 256], P(('blk', 'head'))
Inputs may be any that keep to these rules, and one draw needn't show every extreme that they name: `segment_ids`: never falling along the window; every document has 1 to 2048 tokens, and one has exactly 2048.
All inputs are finite; a program needn't handle non-finite values.
Results may differ from a plain program's by a relative error of at most 0.0052.
Values may be sent and summed in bfloat16 or wider, within the bound.
No kernel may reach another device: no remote copies, remote signals or barrier semaphores. Data moves between devices by JAX's collectives and lax.ppermute only.
A program may use at most 64 MiB of HBM per device.

v0:
```python
import jax
import jax.numpy as jnp
from jax import lax
from jax.sharding import PartitionSpec as P

HD = 128


def shifted(value, axis, steps):
    count = lax.axis_size(axis)
    pairs = [(source, (source + steps) % count) for source in range(count)]
    return lax.ppermute(value, axis, pairs)


def local(
    query,
    key,
    value,
    output,
    grad_output,
    log_norm,
    entropy,
    segment_ids,
    weight_index,
    penalty_weights,
):
    score_scale = HD ** (-0.5)
    block_count = lax.axis_size("blk")
    block_rows = query.shape[0]
    heads_here = query.shape[1] // HD
    kv_heads = key.shape[1] // HD
    heads_total = heads_here * lax.axis_size("head")
    kv_index = lax.axis_index("head") * heads_here // (heads_total // kv_heads)
    key_block = lax.dynamic_slice_in_dim(key, kv_index * HD, HD, 1)
    value_block = lax.dynamic_slice_in_dim(value, kv_index * HD, HD, 1)
    q_heads = query.reshape(block_rows, heads_here, HD).transpose(1, 0, 2)
    do_heads = grad_output.reshape(block_rows, heads_here, HD).transpose(1, 0, 2)
    o_heads = output.reshape(block_rows, heads_here, HD).transpose(1, 0, 2)
    row_delta = jnp.einsum("hqd,hqd->hq", do_heads, o_heads, preferred_element_type=jnp.float32)[
        :, :, None
    ]
    lse_rows = log_norm[:, :, None]
    ent_rows = entropy[:, :, None]
    block_owner = lax.axis_index("blk")
    row_start = block_owner * block_rows
    seg_rows = lax.dynamic_slice_in_dim(segment_ids, row_start, block_rows)
    doc_rate = jnp.sum(
        jnp.where(
            weight_index[:, None] == jnp.arange(penalty_weights.shape[0])[None, :],
            penalty_weights[None, :],
            0.0,
        ),
        1,
    )
    row_rate = jnp.sum(
        jnp.where(
            seg_rows[:, None] == jnp.arange(doc_rate.shape[0])[None, :], doc_rate[None, :], 0.0
        ),
        1,
    )[None, :, None]
    query_pos = row_start + jnp.arange(block_rows)

    def block_terms(key_piece, value_piece, visible):
        scores = (
            jnp.einsum("hqd,kd->hqk", q_heads, key_piece, preferred_element_type=jnp.float32)
            * score_scale
        )
        probs = jnp.where(visible[None, :, :], jnp.exp(scores - lse_rows), 0.0)
        dprobs = jnp.einsum(
            "hqd,kd->hqk", do_heads, value_piece, preferred_element_type=jnp.float32
        )
        dscores = probs * (dprobs - row_delta - row_rate * (scores - lse_rows + ent_rows))
        probs_low = probs.astype(jnp.bfloat16)
        dscores_low = dscores.astype(jnp.bfloat16)
        query_add = jnp.einsum(
            "hqk,kd->hqd", dscores_low, key_piece, preferred_element_type=jnp.float32
        )
        key_add = jnp.einsum(
            "hqk,hqd->kd", dscores_low, q_heads, preferred_element_type=jnp.float32
        )
        value_add = jnp.einsum(
            "hqk,hqd->kd", probs_low, do_heads, preferred_element_type=jnp.float32
        )
        return (query_add, key_add, value_add)

    def contribute(key_piece, value_piece, key_start):
        count = key_piece.shape[0]
        seg_keys = lax.dynamic_slice_in_dim(segment_ids, key_start, count)
        key_pos = key_start + jnp.arange(count)
        visible = (seg_rows[:, None] == seg_keys[None, :]) & (
            key_pos[None, :] <= query_pos[:, None]
        )
        return block_terms(key_piece, value_piece, visible)

    query_acc = jnp.zeros((heads_here, block_rows, HD), jnp.float32)
    zeros_acc = jnp.zeros((block_rows, HD), jnp.float32)

    def one_turn(turn_index, carry):
        query_sum, key_piece, value_piece, key_sum, value_sum = carry
        key_piece, value_piece = shifted((key_piece, value_piece), "blk", 1)
        key_sum, value_sum = shifted((key_sum, value_sum), "blk", 1)
        anchor = (block_owner - turn_index - 1) % block_count
        query_add, key_add, value_add = contribute(key_piece, value_piece, anchor * block_rows)
        return (
            query_sum + query_add,
            key_piece,
            value_piece,
            key_sum + key_add,
            value_sum + value_add,
        )

    query_acc, unused_key, unused_value, key_total, value_total = lax.fori_loop(
        0, block_count, one_turn, (query_acc, key_block, value_block, zeros_acc, zeros_acc)
    )
    grad_query = (
        (query_acc * score_scale)
        .astype(jnp.bfloat16)
        .transpose(1, 0, 2)
        .reshape(block_rows, heads_here * HD)
    )
    column_mask = (jnp.arange(kv_heads) == kv_index)[None, :, None]
    key_term = jnp.where(column_mask, (key_total * score_scale)[:, None, :], 0.0).reshape(
        block_rows, kv_heads * HD
    )
    value_term = jnp.where(column_mask, value_total[:, None, :], 0.0).reshape(
        block_rows, kv_heads * HD
    )
    key_sum, value_sum = (
        lax.psum_scatter(key_term, "head", scatter_dimension=0, tiled=True),
        lax.psum_scatter(value_term, "head", scatter_dimension=0, tiled=True),
    )
    return (grad_query, key_sum.astype(jnp.bfloat16), value_sum.astype(jnp.bfloat16))


def solution(mesh):
    in_specs = (
        P("blk", "head"),
        P("blk", None),
        P("blk", None),
        P("blk", "head"),
        P("blk", "head"),
        P("head", "blk"),
        P("head", "blk"),
        P(),
        P(),
        P(),
    )
    out_specs = (P("blk", "head"), P(("blk", "head"), None), P(("blk", "head"), None))
    return jax.shard_map(local, mesh=mesh, in_specs=in_specs, out_specs=out_specs, check_vma=False)
```

profile of v0, /device:TPU:1, one launch (start us, length us, event | category | flops | bytes accessed | tf_op | source)
XLA Modules:
  0.0 921.5 jit_solution(315927452591774976)
XLA Ops:
  12.5 711.5 %while.24 = (s32[]{:T(128)}, f32[2,256,128]{2,1,0:T(8,128)S(1)}, bf16[256,128]{1,0:T(8,128)(2,1)S(1)}, bf16[256,128]{1,0:T(8,128)(2,1)S(1)}, f32[256,128]{1,0:T(...) while((s32[]{:T(128)}, f32[2,256,128]{2,1,0:T(8,128)S(1)}, ...), condition=%wide.region_3.4_spmd.clone, body=%wide.region_2.3_spmd.clone.sunk | while | flops 169673216 | bytes 6700600 | solution.py:112
  32.8 7.4 collective-permute-done.3
  49.5 5.0 collective-permute-done.1
  72.2 5.0 collective-permute-done.1
  94.8 5.0 collective-permute-done.1
  117.2 5.0 collective-permute-done.1
  139.3 5.0 collective-permute-done.1
  161.3 5.0 collective-permute-done.1
  183.1 5.0 collective-permute-done.1
  204.7 5.0 collective-permute-done.1
  226.7 5.0 collective-permute-done.1
  248.7 5.0 collective-permute-done.1
  270.7 5.0 collective-permute-done.1
  292.7 5.0 collective-permute-done.1
  314.7 5.0 collective-permute-done.1
  336.7 5.0 collective-permute-done.1
  358.7 5.0 collective-permute-done.1
  380.7 5.0 collective-permute-done.1
  402.7 5.0 collective-permute-done.1
  424.7 5.0 collective-permute-done.1
  468.7 5.0 collective-permute-done.1
  490.7 5.0 collective-permute-done.1
  726.6 92.9 %reduce-scatter.5.cloned.1.call-done = f32[16,256]{1,0:T(8,128)} async-done(((f32[256,256]{1,0:T(8,128)}), f32[16,256]{1,0:T(8,128)}) %reduce-scatter.5.cloned.1.call-update) | async-done | bytes 16400 | tf_op jit(solution)/shard_map/reduce_scatter | solution.py:130
  820.7 92.6 %reduce-scatter.3.cloned.1.call-done = f32[16,256]{1,0:T(8,128)} async-done(((f32[256,256]{1,0:T(8,128)}), f32[16,256]{1,0:T(8,128)}) %reduce-scatter.3.cloned.1.call-update) | async-done | bytes 16400 | tf_op jit(solution)/shard_map/reduce_scatter | solution.py:129
  (695 shorter events, 609.2 us)
Async XLA Ops:
  7.2 812.3 %reduce-scatter.5.cloned.1.call-start = ((), (), s32[]{:S(2)}) async-start(), calls=%async_computation.3 | async-start | bytes 278528 | tf_op jit(solution)/shard_map/reduce_scatter | solution.py:130
  20.4 20.0 %collective-permute-start.2 = (f32[256,128]{1,0:T(8,128)S(1)}, f32[256,128]{1,0:T(8,128)S(1)}, u32[]{:S(2)}, u32[]{:S(2)}) collective-permute-start(f32[256,128]{1,0:T(8,128)S(1)} %broadcast_select_fusion.4), channel_id=1, source_target_pairs={{0,16},{16,32},{32,48},{48,64},{64,80},{80,96},{96,112},{112,128},... | collective-permute-start | bytes 393224 | tf_op jit(solution)/shard_map/while/body/eval_jaxpr/ppermute | solution.py:12
  44.6 18.6 %collective-permute-start.2 = (f32[256,128]{1,0:T(8,128)S(1)}, f32[256,128]{1,0:T(8,128)S(1)}, u32[]{:S(2)}, u32[]{:S(2)}) collective-permute-start(f32[256,128]{1,0:T(8,128)S(1)} %broadcast_select_fusion.4), channel_id=1, source_target_pairs={{0,16},{16,32},{32,48},{48,64},{64,80},{80,96},{96,112},{112,128},... | collective-permute-start | bytes 393224 | tf_op jit(solution)/shard_map/while/body/eval_jaxpr/ppermute | solution.py:12
  67.4 18.4 %collective-permute-start.2 = (f32[256,128]{1,0:T(8,128)S(1)}, f32[256,128]{1,0:T(8,128)S(1)}, u32[]{:S(2)}, u32[]{:S(2)}) collective-permute-start(f32[256,128]{1,0:T(8,128)S(1)} %broadcast_select_fusion.4), channel_id=1, source_target_pairs={{0,16},{16,32},{32,48},{48,64},{64,80},{80,96},{96,112},{112,128},... | collective-permute-start | bytes 393224 | tf_op jit(solution)/shard_map/while/body/eval_jaxpr/ppermute | solution.py:12
  90.0 18.2 %collective-permute-start.2 = (f32[256,128]{1,0:T(8,128)S(1)}, f32[256,128]{1,0:T(8,128)S(1)}, u32[]{:S(2)}, u32[]{:S(2)}) collective-permute-start(f32[256,128]{1,0:T(8,128)S(1)} %broadcast_select_fusion.4), channel_id=1, source_target_pairs={{0,16},{16,32},{32,48},{48,64},{64,80},{80,96},{96,112},{112,128},... | collective-permute-start | bytes 393224 | tf_op jit(solution)/shard_map/while/body/eval_jaxpr/ppermute | solution.py:12
  112.3 17.9 %collective-permute-start.2 = (f32[256,128]{1,0:T(8,128)S(1)}, f32[256,128]{1,0:T(8,128)S(1)}, u32[]{:S(2)}, u32[]{:S(2)}) collective-permute-start(f32[256,128]{1,0:T(8,128)S(1)} %broadcast_select_fusion.4), channel_id=1, source_target_pairs={{0,16},{16,32},{32,48},{48,64},{64,80},{80,96},{96,112},{112,128},... | collective-permute-start | bytes 393224 | tf_op jit(solution)/shard_map/while/body/eval_jaxpr/ppermute | solution.py:12
  221.8 17.8 %collective-permute-start.2 = (f32[256,128]{1,0:T(8,128)S(1)}, f32[256,128]{1,0:T(8,128)S(1)}, u32[]{:S(2)}, u32[]{:S(2)}) collective-permute-start(f32[256,128]{1,0:T(8,128)S(1)} %broadcast_select_fusion.4), channel_id=1, source_target_pairs={{0,16},{16,32},{32,48},{48,64},{64,80},{80,96},{96,112},{112,128},... | collective-permute-start | bytes 393224 | tf_op jit(solution)/shard_map/while/body/eval_jaxpr/ppermute | solution.py:12
  243.8 17.8 %collective-permute-start.2 = (f32[256,128]{1,0:T(8,128)S(1)}, f32[256,128]{1,0:T(8,128)S(1)}, u32[]{:S(2)}, u32[]{:S(2)}) collective-permute-start(f32[256,128]{1,0:T(8,128)S(1)} %broadcast_select_fusion.4), channel_id=1, source_target_pairs={{0,16},{16,32},{32,48},{48,64},{64,80},{80,96},{96,112},{112,128},... | collective-permute-start | bytes 393224 | tf_op jit(solution)/shard_map/while/body/eval_jaxpr/ppermute | solution.py:12
  265.8 17.8 %collective-permute-start.2 = (f32[256,128]{1,0:T(8,128)S(1)}, f32[256,128]{1,0:T(8,128)S(1)}, u32[]{:S(2)}, u32[]{:S(2)}) collective-permute-start(f32[256,128]{1,0:T(8,128)S(1)} %broadcast_select_fusion.4), channel_id=1, source_target_pairs={{0,16},{16,32},{32,48},{48,64},{64,80},{80,96},{96,112},{112,128},... | collective-permute-start | bytes 393224 | tf_op jit(solution)/shard_map/while/body/eval_jaxpr/ppermute | solution.py:12
  287.8 17.8 %collective-permute-start.2 = (f32[256,128]{1,0:T(8,128)S(1)}, f32[256,128]{1,0:T(8,128)S(1)}, u32[]{:S(2)}, u32[]{:S(2)}) collective-permute-start(f32[256,128]{1,0:T(8,128)S(1)} %broadcast_select_fusion.4), channel_id=1, source_target_pairs={{0,16},{16,32},{32,48},{48,64},{64,80},{80,96},{96,112},{112,128},... | collective-permute-start | bytes 393224 | tf_op jit(solution)/shard_map/while/body/eval_jaxpr/ppermute | solution.py:12
  309.8 17.8 %collective-permute-start.2 = (f32[256,128]{1,0:T(8,128)S(1)}, f32[256,128]{1,0:T(8,128)S(1)}, u32[]{:S(2)}, u32[]{:S(2)}) collective-permute-start(f32[256,128]{1,0:T(8,128)S(1)} %broadcast_select_fusion.4), channel_id=1, source_target_pairs={{0,16},{16,32},{32,48},{48,64},{64,80},{80,96},{96,112},{112,128},... | collective-permute-start | bytes 393224 | tf_op jit(solution)/shard_map/while/body/eval_jaxpr/ppermute | solution.py:12
  331.8 17.8 %collective-permute-start.2 = (f32[256,128]{1,0:T(8,128)S(1)}, f32[256,128]{1,0:T(8,128)S(1)}, u32[]{:S(2)}, u32[]{:S(2)}) collective-permute-start(f32[256,128]{1,0:T(8,128)S(1)} %broadcast_select_fusion.4), channel_id=1, source_target_pairs={{0,16},{16,32},{32,48},{48,64},{64,80},{80,96},{96,112},{112,128},... | collective-permute-start | bytes 393224 | tf_op jit(solution)/shard_map/while/body/eval_jaxpr/ppermute | solution.py:12
  353.8 17.8 %collective-permute-start.2 = (f32[256,128]{1,0:T(8,128)S(1)}, f32[256,128]{1,0:T(8,128)S(1)}, u32[]{:S(2)}, u32[]{:S(2)}) collective-permute-start(f32[256,128]{1,0:T(8,128)S(1)} %broadcast_select_fusion.4), channel_id=1, source_target_pairs={{0,16},{16,32},{32,48},{48,64},{64,80},{80,96},{96,112},{112,128},... | collective-permute-start | bytes 393224 | tf_op jit(solution)/shard_map/while/body/eval_jaxpr/ppermute | solution.py:12
  375.8 17.8 %collective-permute-start.2 = (f32[256,128]{1,0:T(8,128)S(1)}, f32[256,128]{1,0:T(8,128)S(1)}, u32[]{:S(2)}, u32[]{:S(2)}) collective-permute-start(f32[256,128]{1,0:T(8,128)S(1)} %broadcast_select_fusion.4), channel_id=1, source_target_pairs={{0,16},{16,32},{32,48},{48,64},{64,80},{80,96},{96,112},{112,128},... | collective-permute-start | bytes 393224 | tf_op jit(solution)/shard_map/while/body/eval_jaxpr/ppermute | solution.py:12
  397.8 17.8 %collective-permute-start.2 = (f32[256,128]{1,0:T(8,128)S(1)}, f32[256,128]{1,0:T(8,128)S(1)}, u32[]{:S(2)}, u32[]{:S(2)}) collective-permute-start(f32[256,128]{1,0:T(8,128)S(1)} %broadcast_select_fusion.4), channel_id=1, source_target_pairs={{0,16},{16,32},{32,48},{48,64},{64,80},{80,96},{96,112},{112,128},... | collective-permute-start | bytes 393224 | tf_op jit(solution)/shard_map/while/body/eval_jaxpr/ppermute | solution.py:12
  419.9 17.8 %collective-permute-start.2 = (f32[256,128]{1,0:T(8,128)S(1)}, f32[256,128]{1,0:T(8,128)S(1)}, u32[]{:S(2)}, u32[]{:S(2)}) collective-permute-start(f32[256,128]{1,0:T(8,128)S(1)} %broadcast_select_fusion.4), channel_id=1, source_target_pairs={{0,16},{16,32},{32,48},{48,64},{64,80},{80,96},{96,112},{112,128},... | collective-permute-start | bytes 393224 | tf_op jit(solution)/shard_map/while/body/eval_jaxpr/ppermute | solution.py:12
  441.9 17.8 %collective-permute-start.2 = (f32[256,128]{1,0:T(8,128)S(1)}, f32[256,128]{1,0:T(8,128)S(1)}, u32[]{:S(2)}, u32[]{:S(2)}) collective-permute-start(f32[256,128]{1,0:T(8,128)S(1)} %broadcast_select_fusion.4), channel_id=1, source_target_pairs={{0,16},{16,32},{32,48},{48,64},{64,80},{80,96},{96,112},{112,128},... | collective-permute-start | bytes 393224 | tf_op jit(solution)/shard_map/while/body/eval_jaxpr/ppermute | solution.py:12
  463.9 17.8 %collective-permute-start.2 = (f32[256,128]{1,0:T(8,128)S(1)}, f32[256,128]{1,0:T(8,128)S(1)}, u32[]{:S(2)}, u32[]{:S(2)}) collective-permute-start(f32[256,128]{1,0:T(8,128)S(1)} %broadcast_select_fusion.4), channel_id=1, source_target_pairs={{0,16},{16,32},{32,48},{48,64},{64,80},{80,96},{96,112},{112,128},... | collective-permute-start | bytes 393224 | tf_op jit(solution)/shard_map/while/body/eval_jaxpr/ppermute | solution.py:12
  485.9 17.8 %collective-permute-start.2 = (f32[256,128]{1,0:T(8,128)S(1)}, f32[256,128]{1,0:T(8,128)S(1)}, u32[]{:S(2)}, u32[]{:S(2)}) collective-permute-start(f32[256,128]{1,0:T(8,128)S(1)} %broadcast_select_fusion.4), channel_id=1, source_target_pairs={{0,16},{16,32},{32,48},{48,64},{64,80},{80,96},{96,112},{112,128},... | collective-permute-start | bytes 393224 | tf_op jit(solution)/shard_map/while/body/eval_jaxpr/ppermute | solution.py:12
  507.9 17.8 %collective-permute-start.2 = (f32[256,128]{1,0:T(8,128)S(1)}, f32[256,128]{1,0:T(8,128)S(1)}, u32[]{:S(2)}, u32[]{:S(2)}) collective-permute-start(f32[256,128]{1,0:T(8,128)S(1)} %broadcast_select_fusion.4), channel_id=1, source_target_pairs={{0,16},{16,32},{32,48},{48,64},{64,80},{80,96},{96,112},{112,128},... | collective-permute-start | bytes 393224 | tf_op jit(solution)/shard_map/while/body/eval_jaxpr/ppermute | solution.py:12
  529.9 17.8 %collective-permute-start.2 = (f32[256,128]{1,0:T(8,128)S(1)}, f32[256,128]{1,0:T(8,128)S(1)}, u32[]{:S(2)}, u32[]{:S(2)}) collective-permute-start(f32[256,128]{1,0:T(8,128)S(1)} %broadcast_select_fusion.4), channel_id=1, source_target_pairs={{0,16},{16,32},{32,48},{48,64},{64,80},{80,96},{96,112},{112,128},... | collective-permute-start | bytes 393224 | tf_op jit(solution)/shard_map/while/body/eval_jaxpr/ppermute | solution.py:12
  551.9 17.8 %collective-permute-start.2 = (f32[256,128]{1,0:T(8,128)S(1)}, f32[256,128]{1,0:T(8,128)S(1)}, u32[]{:S(2)}, u32[]{:S(2)}) collective-permute-start(f32[256,128]{1,0:T(8,128)S(1)} %broadcast_select_fusion.4), channel_id=1, source_target_pairs={{0,16},{16,32},{32,48},{48,64},{64,80},{80,96},{96,112},{112,128},... | collective-permute-start | bytes 393224 | tf_op jit(solution)/shard_map/while/body/eval_jaxpr/ppermute | solution.py:12
  573.9 17.8 %collective-permute-start.2 = (f32[256,128]{1,0:T(8,128)S(1)}, f32[256,128]{1,0:T(8,128)S(1)}, u32[]{:S(2)}, u32[]{:S(2)}) collective-permute-start(f32[256,128]{1,0:T(8,128)S(1)} %broadcast_select_fusion.4), channel_id=1, source_target_pairs={{0,16},{16,32},{32,48},{48,64},{64,80},{80,96},{96,112},{112,128},... | collective-permute-start | bytes 393224 | tf_op jit(solution)/shard_map/while/body/eval_jaxpr/ppermute | solution.py:12
  725.1 188.2 %reduce-scatter.3.cloned.1.call-start = ((), (), s32[]{:S(2)}) async-start(), calls=%async_computation.2 | async-start | bytes 278528 | tf_op jit(solution)/shard_map/reduce_scatter | solution.py:129
  (114 other events, 1571.1 us)
Sparse Core Ops, SparseCore 0:
  725.3 94.1 reduce-scatter.4
  824.7 88.5 reduce-scatter.2
where the time goes:
time: 927 us; the launch traced here: 921 us
  waiting for transfers between devices  564 us (61%)
  starting transfers between devices  254 us (27%)
  matrix products  43.5 us (5%)
  local copies, waits for them, and re-layouts  29.5 us (3%)
  between operations  14.2 us (2%)
  other arithmetic  10.3 us (1%)
    ppermute x128, waiting for transfers between devices, shifted(): return lax.ppermute(value, axis, pairs)  378 us
    ppermute x128, starting transfers between devices, shifted(): return lax.ppermute(value, axis, pairs)  254 us
    reduce_scatter x1, waiting for transfers between devices, local(): lax.psum_scatter(value_term, 'head', scatter_dimension=0, tiled=True)  92.9 us
    reduce_scatter x1, waiting for transfers between devices, local(): lax.psum_scatter(key_term, 'head', scatter_dimension=0, tiled=True)  92.6 us
    dynamic_slice x32, local copies, waits for them, and re-layouts, contribute(): seg_keys = lax.dynamic_slice_in_dim(segment_ids, key_start, count)  24.5 us
  transfers between devices with their start and end apart: 130, of which 98 were waited for; matrix products, arithmetic and copies ran while one was open for 7% of the time, Pallas kernels for 0%

commit v1 on v0

v1 whole, which is shorter than its diff:
```python
import functools
import math

import jax
import jax.numpy as jnp
from jax import lax
from jax.experimental import pallas as pl
from jax.experimental.pallas import tpu as pltpu
from jax.sharding import PartitionSpec as P

HD = 128
ROWS = 256
SCALE = HD ** (-0.5)
LOG2E = math.log2(math.e)
MSG = 4 * ROWS + 32
GROUP = 8
F32 = jnp.float32
BF16 = jnp.bfloat16
VMEM_LIMIT = 48 * 1024 * 1024

FIRST = ((1, 7), (2, 6))
SECOND = ((3, 5), (4, 8))


def place(index):
    blk, head = divmod(index, 16)
    x, z_lo = divmod(blk, 8)
    y, rest = divmod(head, 4)
    z_hi, core = divmod(rest, 2)
    return x, y, z_hi * 8 + z_lo, core


def device(x, y, z, core):
    z_hi, z_lo = divmod(z % 16, 8)
    return ((x % 4) * 8 + z_lo) * 16 + (y % 4) * 4 + z_hi * 2 + core


def pairs_from(source_of):
    return [(source_of(index), index) for index in range(512)]


def back_source(table, index):
    x, y, z, core = place(index)
    steps = table[y % 2][core]
    source_x = x if z % 8 >= steps else x - 1
    up = steps < 4 or (steps == 4 and z % 2 == 0)
    return device(source_x, y, z - steps if up else z + 8 - steps, core)


def other_core(index):
    x, y, z, core = place(index)
    return device(x, y, z, 1 - core)


def other_y(index):
    x, y, z, core = place(index)
    return device(x, y ^ 1, z, core)


def inverse(pairs):
    return [(target, source) for source, target in pairs]


def moved(value, pairs):
    return lax.ppermute(value, ("blk", "head"), pairs)


def steps_here(table):
    head = lax.axis_index("head")
    odd = lax.rem(lax.div(head, 4), 2) == 1
    core = lax.rem(head, 2) == 1
    return jnp.where(
        odd,
        jnp.where(core, table[1][1], table[1][0]),
        jnp.where(core, table[0][1], table[0][0]),
    )


def nt(a, b):
    return lax.dot_general(a, b, (((1,), (1,)), ((), ())), preferred_element_type=F32)


def nn(a, b):
    return lax.dot_general(a, b, (((1,), (0,)), ((), ())), preferred_element_type=F32)


def transposed(block):
    return block.astype(F32).T.astype(BF16)


def prep_kernel(
    q, k, v, o, do, lse, ent, seg, weight_index, weights, msg, kv, aux, rows
):
    blk = lax.axis_index("blk")
    head = lax.axis_index("head")
    column = pl.multiple_of(lax.div(head, 8) * HD, HD)
    kv[:, :HD] = k[:, pl.ds(column, HD)]
    kv[:, HD:] = v[:, pl.ds(column, HD)]
    docs = weight_index.shape[0]
    tokens = seg[...]
    first = seg[pl.ds(2 * blk, 1), :]
    second = seg[pl.ds(2 * blk + 1, 1), :]
    seg_rows = jnp.concatenate([first, second], axis=1)
    rate = jnp.zeros((1, ROWS), F32)
    for d in range(docs):
        rows[d : d + 1, :HD] = jnp.sum(
            jnp.where(tokens < d, 1.0, 0.0), axis=0, keepdims=True
        )
        rate = jnp.where(seg_rows == d, weights[weight_index[d]], rate)
    starts = jnp.sum(rows[:, :HD], axis=1, keepdims=True)
    doc = lax.broadcasted_iota(jnp.int32, (docs, ROWS), 0)
    start = jnp.sum(jnp.where(doc == seg_rows, starts, 0.0), axis=0, keepdims=True)
    aux[...] = jnp.zeros_like(aux)
    aux[0:1, :] = start
    aux[1:2, :] = rate
    rows[...] = jnp.zeros_like(rows)
    for h in range(2):
        columns = slice(h * HD, (h + 1) * HD)
        do_h = do[:, columns]
        msg[h * 512 : h * 512 + ROWS, :] = q[:, columns]
        msg[h * 512 + ROWS : h * 512 + 512, :] = do_h
        product = do_h.astype(F32) * o[:, columns].astype(F32)
        delta = jnp.sum(product.T, axis=0, keepdims=True)
        lse_h = lse[h : h + 1, :]
        const = delta + rate * (ent[h : h + 1, :] - lse_h)
        for at, value in ((3 * h, lse_h), (6 + 3 * h, const)):
            for part in range(3):
                piece = value.astype(BF16).astype(F32)
                rows[at + part : at + part + 1, :] = piece
                value = value - piece
    msg[1024:1040, :] = rows[:, :HD].astype(BF16)
    msg[1040:1056, :] = rows[:, HD:].astype(BF16)


def prep(q, k, v, o, do, lse, ent, seg, weight_index, weights):
    vmem = pl.BlockSpec(memory_space=pltpu.VMEM)
    smem = pl.BlockSpec(memory_space=pltpu.SMEM)
    return pl.pallas_call(
        prep_kernel,
        out_shape=(
            jax.ShapeDtypeStruct((MSG, HD), BF16),
            jax.ShapeDtypeStruct((ROWS, 2 * HD), BF16),
            jax.ShapeDtypeStruct((8, ROWS), F32),
        ),
        in_specs=[vmem] * 8 + [smem] * 2,
        out_specs=(vmem,) * 3,
        scratch_shapes=[pltpu.VMEM((16, ROWS), F32)],
        name="prep",
        compiler_params=pltpu.CompilerParams(vmem_limit_bytes=VMEM_LIMIT),
    )(q, k, v, o, do, lse, ent, seg, weight_index, weights)


def row_terms(stats_lo, stats_hi, h):
    def whole(at):
        both = [
            half[at : at + 1, :] + half[at + 1 : at + 2, :] + half[at + 2 : at + 3, :]
            for half in (stats_lo, stats_hi)
        ]
        return jnp.concatenate(both, axis=1)

    return whole(3 * h) * LOG2E, whole(6 + 3 * h)


def unit(key_block, key_turned, value_block, q, do, lse2, const, rate, visible):
    scores = nt(key_block, q)
    probs = jnp.where(visible, jnp.exp2(scores * (SCALE * LOG2E) - lse2), 0.0)
    dprobs = nt(value_block, do)
    dscores = probs * (dprobs - const - scores * rate)
    probs_low = probs.astype(BF16)
    dscores_low = dscores.astype(BF16)
    return nn(key_turned, dscores_low), nn(dscores_low, q), nn(probs_low, do)


def diag_kernel(msg, kv, aux, dq, dkv):
    blk = lax.axis_index("blk")
    threshold = aux[0:1, :] - (blk * ROWS).astype(F32)
    rate = aux[1:2, :] * SCALE
    key_at = lax.broadcasted_iota(jnp.int32, (ROWS, ROWS), 0)
    query_at = lax.broadcasted_iota(jnp.int32, (ROWS, ROWS), 1)
    visible = (key_at <= query_at) & (key_at.astype(F32) >= threshold)
    key_block, value_block = kv[:, :HD], kv[:, HD:]
    key_turned = transposed(key_block)
    stats_lo = msg[1024:1040, :].astype(F32)
    stats_hi = msg[1040:1056, :].astype(F32)
    key_sum = value_sum = None
    for h in range(2):
        lse2, const = row_terms(stats_lo, stats_hi, h)
        q = msg[h * 512 : h * 512 + ROWS, :]
        do = msg[h * 512 + ROWS : h * 512 + 512, :]
        query_add, key_add, value_add = unit(
            key_block, key_turned, value_block, q, do, lse2, const, rate, visible
        )
        dq[h] = query_add
        key_sum = key_add if h == 0 else key_sum + key_add
        value_sum = value_add if h == 0 else value_sum + value_add
    dkv[:, :HD] = key_sum
    dkv[:, HD:] = value_sum


def diag(msg, kv, aux):
    vmem = pl.BlockSpec(memory_space=pltpu.VMEM)
    return pl.pallas_call(
        diag_kernel,
        out_shape=(
            jax.ShapeDtypeStruct((2, HD, ROWS), F32),
            jax.ShapeDtypeStruct((ROWS, 2 * HD), F32),
        ),
        in_specs=[vmem] * 3,
        out_specs=(vmem,) * 2,
        name="diag",
        compiler_params=pltpu.CompilerParams(vmem_limit_bytes=VMEM_LIMIT),
        cost_estimate=pl.CostEstimate(
            flops=20 * ROWS * ROWS * HD, bytes_accessed=1 << 20, transcendentals=2 * ROWS * ROWS
        ),
    )(msg, kv, aux)


def main_kernel(
    own, other, kv_a, kv_b, aux, dq_diag, dkv_a, dkv_b, dq_send, dq_keep, dq, dkv
):
    blk = lax.axis_index("blk")
    start = aux[0:1, :]
    rate = aux[1:2, :] * SCALE
    first_start = jnp.min(start)
    key_at = lax.broadcasted_iota(jnp.int32, (ROWS, ROWS), 0).astype(F32)
    dq[...] = jnp.zeros_like(dq)
    dq[0, 0] = dq_diag[0]
    dq[0, 1] = dq_diag[1]
    for kv, table, out in ((kv_a, FIRST, dkv_a), (kv_b, SECOND, dkv_b)):
        key_start = ((blk - steps_here(table)) * ROWS).astype(F32)
        seen = key_start + (ROWS - 1) >= first_start

        @pl.when(jnp.logical_not(seen))
        def _():
            out[...] = jnp.zeros_like(out)

        @pl.when(seen)
        def _():
            key_block, value_block = kv[:, :HD], kv[:, HD:]
            key_turned = transposed(key_block)
            threshold = start - key_start
            dkv[...] = jnp.zeros_like(dkv)

            @pl.loop(0, 2)
            def _(src):
                base = src * MSG
                for part, ref in ((0, own), (1, other)):
                    at = pl.multiple_of(base + 1024, 16)
                    stats_lo = ref[pl.ds(at, 16), :].astype(F32)
                    stats_hi = ref[pl.ds(at + 16, 16), :].astype(F32)
                    for h in range(2):
                        lse2, const = row_terms(stats_lo, stats_hi, h)
                        at = pl.multiple_of(base + h * 512, 16)
                        q = ref[pl.ds(at, ROWS), :]
                        do = ref[pl.ds(at + ROWS, ROWS), :]
                        visible = key_at >= threshold
                        query_add, key_add, value_add = unit(
                            key_block,
                            key_turned,
                            value_block,
                            q,
                            do,
                            lse2,
                            const,
                            rate,
                            visible,
                        )
                        dq[part, 2 * src + h] += query_add
                        dkv[:, :HD] += key_add
                        dkv[:, HD:] += value_add

            out[...] = dkv[...].astype(BF16)

    for n in range(4):
        dq_keep[n * ROWS : (n + 1) * ROWS, :] = dq[0, n].T
        dq_send[n * ROWS : (n + 1) * ROWS, :] = dq[1, n].T.astype(BF16)


def main(own, other, kv_a, kv_b, aux, dq_diag):
    vmem = pl.BlockSpec(memory_space=pltpu.VMEM)
    return pl.pallas_call(
        main_kernel,
        out_shape=(
            jax.ShapeDtypeStruct((ROWS, 2 * HD), BF16),
            jax.ShapeDtypeStruct((ROWS, 2 * HD), BF16),
            jax.ShapeDtypeStruct((4 * ROWS, HD), BF16),
            jax.ShapeDtypeStruct((4 * ROWS, HD), F32),
        ),
        in_specs=[vmem] * 6,
        out_specs=(vmem,) * 4,
        scratch_shapes=[
            pltpu.VMEM((2, 4, HD, ROWS), F32),
            pltpu.VMEM((ROWS, 2 * HD), F32),
        ],
        name="main",
        compiler_params=pltpu.CompilerParams(vmem_limit_bytes=VMEM_LIMIT),
        cost_estimate=pl.CostEstimate(
            flops=160 * ROWS * ROWS * HD, bytes_accessed=3 << 20, transcendentals=16 * ROWS * ROWS
        ),
    )(own, other, kv_a, kv_b, aux, dq_diag)


def last_kernel(terms, dq_keep, dq_core, dq_y, grad_query, grad_key, grad_value):
    for h in range(2):
        at = slice(h * ROWS, (h + 1) * ROWS)
        total = dq_keep[at, :] + dq_core[at, :].astype(F32) + dq_y[at, :].astype(F32)
        grad_query[:, h * HD : (h + 1) * HD] = (total * SCALE).astype(BF16)
    half = terms.shape[0] // 2
    for g in range(2):
        total = jnp.sum(terms[g * half : (g + 1) * half], axis=0)
        grad_key[:, g * HD : (g + 1) * HD] = (total[:, :HD] * SCALE).astype(BF16)
        grad_value[:, g * HD : (g + 1) * HD] = total[:, HD:].astype(BF16)


def last(terms, dq_keep, dq_core, dq_y):
    vmem = pl.BlockSpec(memory_space=pltpu.VMEM)
    rows = terms.shape[1]
    return pl.pallas_call(
        last_kernel,
        out_shape=(
            jax.ShapeDtypeStruct((ROWS, 2 * HD), BF16),
            jax.ShapeDtypeStruct((rows, 2 * HD), BF16),
            jax.ShapeDtypeStruct((rows, 2 * HD), BF16),
        ),
        in_specs=[vmem] * 4,
        out_specs=(vmem,) * 3,
        name="last",
        compiler_params=pltpu.CompilerParams(vmem_limit_bytes=VMEM_LIMIT),
    )(terms, dq_keep, dq_core, dq_y)


def local(
    query,
    key,
    value,
    output,
    grad_output,
    log_norm,
    entropy,
    segment_ids,
    weight_index,
    penalty_weights,
):
    to_core = pairs_from(other_core)
    to_y = pairs_from(other_y)
    back_a = pairs_from(functools.partial(back_source, FIRST))
    back_b = pairs_from(functools.partial(back_source, SECOND))
    msg, kv, aux = prep(
        query,
        key,
        value,
        output,
        grad_output,
        log_norm,
        entropy,
        segment_ids.reshape(-1, HD),
        weight_index,
        penalty_weights,
    )
    msg_y = moved(msg, to_y)
    kv_a = moved(kv, back_a)
    kv_b = moved(kv, back_b)
    dq_diag, dkv_diag = diag(msg, kv, aux)
    msg_y, kv_a = lax.optimization_barrier((msg_y, kv_a))
    own = jnp.concatenate([msg, msg_y], axis=0)
    other = moved(own, to_core)
    dkv_a, dkv_b, dq_send, dq_keep = main(own, other, kv_a, kv_b, aux, dq_diag)
    got_a = moved(dkv_a, inverse(back_a))
    got_b = moved(dkv_b, inverse(back_b))
    dq_core = moved(dq_send, to_core)
    dq_pass = (dq_keep[512:] + dq_core[512:].astype(F32)).astype(BF16)
    dq_y = moved(dq_pass, to_y)
    terms = dkv_diag + got_a.astype(F32) + got_b.astype(F32)
    terms = lax.all_to_all(terms.reshape(16, 16, 2 * HD), "head", 0, 0)
    return last(terms, dq_keep, dq_core, dq_y)


def solution(mesh):
    in_specs = (
        P("blk", "head"),
        P("blk", None),
        P("blk", None),
        P("blk", "head"),
        P("blk", "head"),
        P("head", "blk"),
        P("head", "blk"),
        P(),
        P(),
        P(),
    )
    out_specs = (P("blk", "head"), P(("blk", "head"), None), P(("blk", "head"), None))
    return jax.shard_map(local, mesh=mesh, in_specs=in_specs, out_specs=out_specs, check_vma=False)
```

time: 927 us -> 99.1 us (0.11)
  the two profiles are of different devices: /device:TPU:1 before, /device:TPU:38 now
where the time goes in v1:
time: 99.1 us; the launch traced here: 98.5 us
  starting transfers between devices  52 us (52%)
  waiting for transfers between devices  32.1 us (32%)
  local copies, waits for them, and re-layouts  7.35 us (7%)
  Pallas kernels  5.53 us (6%)
    ppermute x8, starting transfers between devices, moved(): return lax.ppermute(value, ('blk', 'head'), pairs)  36.4 us
    ppermute x8, waiting for transfers between devices, moved(): return lax.ppermute(value, ('blk', 'head'), pairs)  18.1 us
    all_to_all x1, starting transfers between devices, local(): terms = lax.all_to_all(terms.reshape(16, 16, 2 * HD), 'head', 0, 0)  15.6 us
    all_to_all x1, waiting for transfers between devices, local(): terms = lax.all_to_all(terms.reshape(16, 16, 2 * HD), 'head', 0, 0)  14 us
    unnamed x21, local copies, waits for them, and re-layouts  7.31 us
    pallas_call x1, Pallas kernels, main(): pl.pallas_call(main_kernel, out_shape=(jax.ShapeDtypeStruct((ROWS, 2 * HD...  3.24 us
  transfers between devices with their start and end apart: 9, of which 6 were waited for; matrix products, arithmetic and copies ran while one was open for 0% of the time, Pallas kernels for 1%

profile of v1, /device:TPU:38, one launch (start us, length us, event | category | flops | bytes accessed | tf_op | source)
XLA Modules:
  0.0 98.5 jit_solution(7105805966241291150)
XLA Ops:
  1.3 0.9 copy-done
  2.2 0.9 copy-done.1
  3.1 0.9 copy-done.2
  4.0 0.9 copy-done.3
  4.9 0.9 copy-done.4
  5.8 0.8 copy-done.5
  8.0 0.8 prep.1
  8.8 3.5 %collective-permute-start = (bf16[1056,128]{1,0:T(8,128)(2,1)S(1)}, bf16[1056,128]{1,0:T(8,128)(2,1)S(1)}, u32[]{:S(2)}, u32[]{:S(2)}) collective-permute-start(bf16[1056,128]{1,0:T(8,128)(2,1)S(1)} %get-tuple-element.14.msg), channel_id=1, source_target_pairs={{4,0},{5,1},{6,2},{7,3},{0,4},{1,5},{2,6},{3,7},{12,8},{13,9},{14,... | collective-permute-start | bytes 811016 | tf_op jit(solution)/shard_map/ppermute | solution.py:65
  12.2 3.8 %collective-permute-start.1 = (bf16[256,256]{1,0:T(8,128)(2,1)S(1)}, bf16[256,256]{1,0:T(8,128)(2,1)S(1)}, u32[]{:S(2)}, u32[]{:S(2)}) collective-permute-start(bf16[256,256]{1,0:T(8,128)(2,1)S(1)} %get-tuple-element.15.kv), channel_id=1, source_target_pairs={{498,0},{401,1},{496,2},{403,3},{486,4},{421,5},{484,6},{423,7},{5... | collective-permute-start | bytes 393224 | tf_op jit(solution)/shard_map/ppermute | solution.py:65
  16.1 3.0 %collective-permute-done.1.kv_a = bf16[256,256]{1,0:T(8,128)(2,1)S(1)} collective-permute-done((bf16[256,256]{1,0:T(8,128)(2,1)S(1)}, bf16[256,256]{1,0:T(8,128)(2,1)S(1)}, u32[]{:S(2)}, u32[]{:S(2)}) %collective-permute-start.1) | collective-permute-done | bytes 131104 | tf_op jit(solution)/shard_map/ppermute | solution.py:65
  19.1 1.9 %collective-permute-start.2 = (bf16[2112,128]{1,0:T(8,128)(2,1)S(1)}, bf16[2112,128]{1,0:T(8,128)(2,1)S(1)}, u32[]{:S(2)}, u32[]{:S(2)}) collective-permute-start(bf16[2112,128]{1,0:T(8,128)(2,1)S(1)} %constant_dynamic-update-slice_fusion.own), channel_id=1, source_target_pairs={{1,0},{0,1},{3,2},{2,3},{5,4},{4,5},{7,6},{6,7},{9,8},{8,9},{11,10... | collective-permute-start | bytes 1622024 | tf_op jit(solution)/shard_map/ppermute | solution.py:65
  21.1 9.0 %collective-permute-start.3 = (bf16[256,256]{1,0:T(8,128)(2,1)S(1)}, bf16[256,256]{1,0:T(8,128)(2,1)S(1)}, u32[]{:S(2)}, u32[]{:S(2)}) collective-permute-start(bf16[256,256]{1,0:T(8,128)(2,1)S(1)} %get-tuple-element.15.kv), channel_id=1, source_target_pairs={{466,0},{433,1},{464,2},{435,3},{454,4},{389,5},{452,6},{391,7},{4... | collective-permute-start | bytes 393224 | tf_op jit(solution)/shard_map/ppermute | solution.py:65
  30.0 0.8 diag.1
  30.8 5.9 %collective-permute-done.3.kv_b = bf16[256,256]{1,0:T(8,128)(2,1)S(1)} collective-permute-done((bf16[256,256]{1,0:T(8,128)(2,1)S(1)}, bf16[256,256]{1,0:T(8,128)(2,1)S(1)}, u32[]{:S(2)}, u32[]{:S(2)}) %collective-permute-start.3) | collective-permute-done | bytes 131104 | tf_op jit(solution)/shard_map/ppermute | solution.py:65
  36.7 3.2 %main.1 = (bf16[256,256]{1,0:T(8,128)(2,1)S(1)}, bf16[256,256]{1,0:T(8,128)(2,1)S(1)}, bf16[1024,128]{1,0:T(8,128)(2,1)S(1)}, f32[1024,128]{1,0:T(8,128)S(1)}) custom-call(bf16[2112,128]{1,0:T(8,128)(2,1)S(1)} %constant_dynamic-update-slice_fusion.own, bf16[2112,128]{1,0:T(8,128)(2,1)S(1)} %collective-permute-done.2.other, ...), custom_call_target="tpu_custom_call" | custom-call | flops 1342177280 | bytes 3145728 | tf_op jit(solution)/shard_map/main/pallas_call | solution.py:281
  39.9 6.2 %collective-permute-start.4 = (bf16[256,256]{1,0:T(8,128)(2,1)S(1)}, bf16[256,256]{1,0:T(8,128)(2,1)S(1)}, u32[]{:S(2)}, u32[]{:S(2)}) collective-permute-start(bf16[256,256]{1,0:T(8,128)(2,1)S(1)} %get-tuple-element.21), channel_id=1, source_target_pairs={{0,498},{1,401},{2,496},{3,403},{4,486},{5,421},{6,484},{7,423},{8... | collective-permute-start | bytes 393224 | tf_op jit(solution)/shard_map/ppermute | solution.py:65
  46.2 5.9 %collective-permute-start.5 = (bf16[256,256]{1,0:T(8,128)(2,1)S(1)}, bf16[256,256]{1,0:T(8,128)(2,1)S(1)}, u32[]{:S(2)}, u32[]{:S(2)}) collective-permute-start(bf16[256,256]{1,0:T(8,128)(2,1)S(1)} %get-tuple-element.22), channel_id=1, source_target_pairs={{0,466},{1,433},{2,464},{3,435},{4,454},{5,389},{6,452},{7,391},{8... | collective-permute-start | bytes 393224 | tf_op jit(solution)/shard_map/ppermute | solution.py:65
  52.1 4.2 %collective-permute-done.5 = bf16[256,256]{1,0:T(8,128)(2,1)S(1)} collective-permute-done((bf16[256,256]{1,0:T(8,128)(2,1)S(1)}, bf16[256,256]{1,0:T(8,128)(2,1)S(1)}, u32[]{:S(2)}, u32[]{:S(2)}) %collective-permute-start.5) | collective-permute-done | bytes 131104 | tf_op jit(solution)/shard_map/ppermute | solution.py:65
  57.0 15.6 %all-to-all-start = ((f32[16,16,256]{2,1,0:T(8,128)}), f32[16,16,256]{2,1,0:T(8,128)S(1)}, u32[]{:S(2)}, u32[]{:S(2)}) async-start(f32[16,16,256]{2,1,0:T(8,128)} %bitcast.1), calls=%async_computation | async-start | bytes 524288 | tf_op jit(solution)/shard_map/all_to_all | solution.py:374
  72.6 2.3 %collective-permute-start.6 = (bf16[1024,128]{1,0:T(8,128)(2,1)S(1)}, bf16[1024,128]{1,0:T(8,128)(2,1)S(1)}, u32[]{:S(2)}, u32[]{:S(2)}) collective-permute-start(bf16[1024,128]{1,0:T(8,128)(2,1)S(1)} %get-tuple-element.24), channel_id=1, source_target_pairs={{1,0},{0,1},{3,2},{2,3},{5,4},{4,5},{7,6},{6,7},{9,8},{8,9},{11,10... | collective-permute-start | bytes 786440 | tf_op jit(solution)/shard_map/ppermute | solution.py:65
  74.9 1.1 %collective-permute-done.6.dq_core = bf16[1024,128]{1,0:T(8,128)(2,1)S(1)} collective-permute-done((bf16[1024,128]{1,0:T(8,128)(2,1)S(1)}, bf16[1024,128]{1,0:T(8,128)(2,1)S(1)}, u32[]{:S(2)}, u32[]{:S(2)}) %collective-permute-start.6) | collective-permute-done | bytes 262176 | tf_op jit(solution)/shard_map/ppermute | solution.py:65
  76.1 3.8 %collective-permute-start.7 = (bf16[512,128]{1,0:T(8,128)(2,1)S(1)}, bf16[512,128]{1,0:T(8,128)(2,1)S(1)}, u32[]{:S(2)}, u32[]{:S(2)}) collective-permute-start(bf16[512,128]{1,0:T(8,128)(2,1)S(1)} %add_convert_fusion), channel_id=1, source_target_pairs={{4,0},{5,1},{6,2},{7,3},{0,4},{1,5},{2,6},{3,7},{12,8},{13,9},{14,... | collective-permute-start | bytes 393224 | tf_op jit(solution)/shard_map/ppermute | solution.py:65
  79.9 3.9 %collective-permute-done.7.dq_y = bf16[512,128]{1,0:T(8,128)(2,1)S(1)} collective-permute-done((bf16[512,128]{1,0:T(8,128)(2,1)S(1)}, bf16[512,128]{1,0:T(8,128)(2,1)S(1)}, u32[]{:S(2)}, u32[]{:S(2)}) %collective-permute-start.7) | collective-permute-done | bytes 131104 | tf_op jit(solution)/shard_map/ppermute | solution.py:65
  83.8 14.0 %all-to-all-done.terms = f32[16,16,256]{2,1,0:T(8,128)S(1)} async-done(((f32[16,16,256]{2,1,0:T(8,128)}), f32[16,16,256]{2,1,0:T(8,128)S(1)}, u32[]{:S(2)}, u32[]{:S(2)}) %all-to-all-start) | async-done | bytes 262176 | tf_op jit(solution)/shard_map/all_to_all | solution.py:374
  (22 shorter events, 3.6 us)
Async XLA Ops:
  0.6 0.7 copy-start.9
  0.6 0.7 copy-start.8
  1.3 0.9 copy-start
  2.2 0.9 copy-start.1
  3.1 0.9 copy-start.2
  4.0 0.9 copy-start.3
  4.9 0.9 copy-start.4
  5.8 0.8 copy-start.5
  6.6 0.7 copy-start.6
  7.3 0.7 copy-start.7
  8.8 10.3 %collective-permute-start = (bf16[1056,128]{1,0:T(8,128)(2,1)S(1)}, bf16[1056,128]{1,0:T(8,128)(2,1)S(1)}, u32[]{:S(2)}, u32[]{:S(2)}) collective-permute-start(bf16[1056,128]{1,0:T(8,128)(2,1)S(1)} %get-tuple-element.14.msg), channel_id=1, source_target_pairs={{4,0},{5,1},{6,2},{7,3},{0,4},{1,5},{2,6},{3,7},{12,8},{13,9},{14,... | collective-permute-start | bytes 811016 | tf_op jit(solution)/shard_map/ppermute | solution.py:65
  12.2 6.9 %collective-permute-start.1 = (bf16[256,256]{1,0:T(8,128)(2,1)S(1)}, bf16[256,256]{1,0:T(8,128)(2,1)S(1)}, u32[]{:S(2)}, u32[]{:S(2)}) collective-permute-start(bf16[256,256]{1,0:T(8,128)(2,1)S(1)} %get-tuple-element.15.kv), channel_id=1, source_target_pairs={{498,0},{401,1},{496,2},{403,3},{486,4},{421,5},{484,6},{423,7},{5... | collective-permute-start | bytes 393224 | tf_op jit(solution)/shard_map/ppermute | solution.py:65
  19.1 17.5 %collective-permute-start.2 = (bf16[2112,128]{1,0:T(8,128)(2,1)S(1)}, bf16[2112,128]{1,0:T(8,128)(2,1)S(1)}, u32[]{:S(2)}, u32[]{:S(2)}) collective-permute-start(bf16[2112,128]{1,0:T(8,128)(2,1)S(1)} %constant_dynamic-update-slice_fusion.own), channel_id=1, source_target_pairs={{1,0},{0,1},{3,2},{2,3},{5,4},{4,5},{7,6},{6,7},{9,8},{8,9},{11,10... | collective-permute-start | bytes 1622024 | tf_op jit(solution)/shard_map/ppermute | solution.py:65
  21.1 15.6 %collective-permute-start.3 = (bf16[256,256]{1,0:T(8,128)(2,1)S(1)}, bf16[256,256]{1,0:T(8,128)(2,1)S(1)}, u32[]{:S(2)}, u32[]{:S(2)}) collective-permute-start(bf16[256,256]{1,0:T(8,128)(2,1)S(1)} %get-tuple-element.15.kv), channel_id=1, source_target_pairs={{466,0},{433,1},{464,2},{435,3},{454,4},{389,5},{452,6},{391,7},{4... | collective-permute-start | bytes 393224 | tf_op jit(solution)/shard_map/ppermute | solution.py:65
  39.9 12.2 %collective-permute-start.4 = (bf16[256,256]{1,0:T(8,128)(2,1)S(1)}, bf16[256,256]{1,0:T(8,128)(2,1)S(1)}, u32[]{:S(2)}, u32[]{:S(2)}) collective-permute-start(bf16[256,256]{1,0:T(8,128)(2,1)S(1)} %get-tuple-element.21), channel_id=1, source_target_pairs={{0,498},{1,401},{2,496},{3,403},{4,486},{5,421},{6,484},{7,423},{8... | collective-permute-start | bytes 393224 | tf_op jit(solution)/shard_map/ppermute | solution.py:65
  46.2 10.1 %collective-permute-start.5 = (bf16[256,256]{1,0:T(8,128)(2,1)S(1)}, bf16[256,256]{1,0:T(8,128)(2,1)S(1)}, u32[]{:S(2)}, u32[]{:S(2)}) collective-permute-start(bf16[256,256]{1,0:T(8,128)(2,1)S(1)} %get-tuple-element.22), channel_id=1, source_target_pairs={{0,466},{1,433},{2,464},{3,435},{4,454},{5,389},{6,452},{7,391},{8... | collective-permute-start | bytes 393224 | tf_op jit(solution)/shard_map/ppermute | solution.py:65
  57.0 40.8 %all-to-all-start = ((f32[16,16,256]{2,1,0:T(8,128)}), f32[16,16,256]{2,1,0:T(8,128)S(1)}, u32[]{:S(2)}, u32[]{:S(2)}) async-start(f32[16,16,256]{2,1,0:T(8,128)} %bitcast.1), calls=%async_computation | async-start | bytes 524288 | tf_op jit(solution)/shard_map/all_to_all | solution.py:374
  72.6 3.5 %collective-permute-start.6 = (bf16[1024,128]{1,0:T(8,128)(2,1)S(1)}, bf16[1024,128]{1,0:T(8,128)(2,1)S(1)}, u32[]{:S(2)}, u32[]{:S(2)}) collective-permute-start(bf16[1024,128]{1,0:T(8,128)(2,1)S(1)} %get-tuple-element.24), channel_id=1, source_target_pairs={{1,0},{0,1},{3,2},{2,3},{5,4},{4,5},{7,6},{6,7},{9,8},{8,9},{11,10... | collective-permute-start | bytes 786440 | tf_op jit(solution)/shard_map/ppermute | solution.py:65
  76.1 7.7 %collective-permute-start.7 = (bf16[512,128]{1,0:T(8,128)(2,1)S(1)}, bf16[512,128]{1,0:T(8,128)(2,1)S(1)}, u32[]{:S(2)}, u32[]{:S(2)}) collective-permute-start(bf16[512,128]{1,0:T(8,128)(2,1)S(1)} %add_convert_fusion), channel_id=1, source_target_pairs={{4,0},{5,1},{6,2},{7,3},{0,4},{1,5},{2,6},{3,7},{12,8},{13,9},{14,... | collective-permute-start | bytes 393224 | tf_op jit(solution)/shard_map/ppermute | solution.py:65

commit v2 on v1

--- a/solution.py
+++ b/solution.py
@@ -12,11 +12,12 @@
 ROWS = 256
 SCALE = HD ** (-0.5)
 LOG2E = math.log2(math.e)
-MSG = 4 * ROWS + 32
+MSG = 4 * ROWS + 64
 GROUP = 8
 F32 = jnp.float32
 BF16 = jnp.bfloat16
-VMEM_LIMIT = 48 * 1024 * 1024
+PREP_VMEM_LIMIT = 62 * 1024 * 1024
+VMEM_LIMIT = 24 * 1024 * 1024
 
 FIRST = ((1, 7), (2, 6))
 SECOND = ((3, 5), (4, 8))
@@ -89,8 +90,53 @@
 
 
 def prep_kernel(
-    q, k, v, o, do, lse, ent, seg, weight_index, weights, msg, kv, aux, rows
+    q_in,
+    k_in,
+    v_in,
+    o_in,
+    do_in,
+    lse_in,
+    ent_in,
+    seg_in,
+    weight_index_in,
+    weights_in,
+    msg,
+    kv,
+    aux,
+    q,
+    k,
+    v,
+    o,
+    do,
+    lse,
+    ent,
+    seg,
+    weight_index,
+    weights,
+    rows,
+    sems,
 ):
+    arriving = [
+        pltpu.make_async_copy(source, target, sems.at[n])
+        for n, (source, target) in enumerate(
+            (
+                (weight_index_in, weight_index),
+                (weights_in, weights),
+                (seg_in, seg),
+                (lse_in, lse),
+                (ent_in, ent),
+                (do_in, do),
+                (o_in, o),
+                (q_in, q),
+                (k_in, k),
+                (v_in, v),
+            )
+        )
+    ]
+    for copy in arriving:
+        copy.start()
+    for copy in arriving:
+        copy.wait()
     blk = lax.axis_index("blk")
     head = lax.axis_index("head")
     column = pl.multiple_of(lax.div(head, 8) * HD, HD)
@@ -107,7 +153,7 @@
             jnp.where(tokens < d, 1.0, 0.0), axis=0, keepdims=True
         )
         rate = jnp.where(seg_rows == d, weights[weight_index[d]], rate)
-    starts = jnp.sum(rows[:, :HD], axis=1, keepdims=True)
+    starts = jnp.sum(rows[:docs, :HD], axis=1, keepdims=True)
     doc = lax.broadcasted_iota(jnp.int32, (docs, ROWS), 0)
     start = jnp.sum(jnp.where(doc == seg_rows, starts, 0.0), axis=0, keepdims=True)
     aux[...] = jnp.zeros_like(aux)
@@ -123,18 +169,20 @@
         delta = jnp.sum(product.T, axis=0, keepdims=True)
         lse_h = lse[h : h + 1, :]
         const = delta + rate * (ent[h : h + 1, :] - lse_h)
-        for at, value in ((3 * h, lse_h), (6 + 3 * h, const)):
+        for at, value in ((0, lse_h), (3, const)):
             for part in range(3):
                 piece = value.astype(BF16).astype(F32)
                 rows[at + part : at + part + 1, :] = piece
                 value = value - piece
-    msg[1024:1040, :] = rows[:, :HD].astype(BF16)
-    msg[1040:1056, :] = rows[:, HD:].astype(BF16)
-
-
-def prep(q, k, v, o, do, lse, ent, seg, weight_index, weights):
+        at = 1024 + 32 * h
+        msg[at : at + 16, :] = rows[:, :HD].astype(BF16)
+        msg[at + 16 : at + 32, :] = rows[:, HD:].astype(BF16)
+
+
+def prep(*arrays):
     vmem = pl.BlockSpec(memory_space=pltpu.VMEM)
-    smem = pl.BlockSpec(memory_space=pltpu.SMEM)
+    held = [pltpu.VMEM(array.shape, array.dtype) for array in arrays[:8]]
+    held += [pltpu.SMEM(array.shape, array.dtype) for array in arrays[8:]]
     return pl.pallas_call(
         prep_kernel,
         out_shape=(
@@ -142,23 +190,29 @@
             jax.ShapeDtypeStruct((ROWS, 2 * HD), BF16),
             jax.ShapeDtypeStruct((8, ROWS), F32),
         ),
-        in_specs=[vmem] * 8 + [smem] * 2,
+        in_specs=[pl.BlockSpec(memory_space=pltpu.HBM)] * 10,
         out_specs=(vmem,) * 3,
-        scratch_shapes=[pltpu.VMEM((16, ROWS), F32)],
+        scratch_shapes=held
+        + [pltpu.VMEM((16, ROWS), F32), pltpu.SemaphoreType.DMA((10,))],
         name="prep",
-        compiler_params=pltpu.CompilerParams(vmem_limit_bytes=VMEM_LIMIT),
-    )(q, k, v, o, do, lse, ent, seg, weight_index, weights)
-
-
-def row_terms(stats_lo, stats_hi, h):
-    def whole(at):
+        compiler_params=pltpu.CompilerParams(vmem_limit_bytes=PREP_VMEM_LIMIT),
+    )(*arrays)
+
+
+def row_terms(ref, h):
+    at = 1024 + 32 * h
+    if not isinstance(h, int):
+        at = pl.multiple_of(at, 16)
+    halves = [ref[pl.ds(at, 16), :].astype(F32), ref[pl.ds(at + 16, 16), :].astype(F32)]
+
+    def whole(row):
         both = [
-            half[at : at + 1, :] + half[at + 1 : at + 2, :] + half[at + 2 : at + 3, :]
-            for half in (stats_lo, stats_hi)
+            half[row : row + 1, :] + half[row + 1 : row + 2, :] + half[row + 2 : row + 3, :]
+            for half in halves
         ]
         return jnp.concatenate(both, axis=1)
 
-    return whole(3 * h) * LOG2E, whole(6 + 3 * h)
+    return whole(0) * LOG2E, whole(3)
 
 
 def unit(key_block, key_turned, value_block, q, do, lse2, const, rate, visible):
@@ -180,11 +234,9 @@
     visible = (key_at <= query_at) & (key_at.astype(F32) >= threshold)
     key_block, value_block = kv[:, :HD], kv[:, HD:]
     key_turned = transposed(key_block)
-    stats_lo = msg[1024:1040, :].astype(F32)
-    stats_hi = msg[1040:1056, :].astype(F32)
     key_sum = value_sum = None
     for h in range(2):
-        lse2, const = row_terms(stats_lo, stats_hi, h)
+        lse2, const = row_terms(msg, h)
         q = msg[h * 512 : h * 512 + ROWS, :]
         do = msg[h * 512 + ROWS : h * 512 + 512, :]
         query_add, key_add, value_add = unit(
@@ -215,89 +267,84 @@
     )(msg, kv, aux)
 
 
-def main_kernel(
-    own, other, kv_a, kv_b, aux, dq_diag, dkv_a, dkv_b, dq_send, dq_keep, dq, dkv
-):
+def block_kernel(table, last_block, own, core, y, cross, kv, aux, dq_in, *rest):
+    if last_block:
+        out, dq_send, dq_keep, dq, dkv = rest
+    else:
+        out, dq, dkv = rest
     blk = lax.axis_index("blk")
     start = aux[0:1, :]
     rate = aux[1:2, :] * SCALE
-    first_start = jnp.min(start)
-    key_at = lax.broadcasted_iota(jnp.int32, (ROWS, ROWS), 0).astype(F32)
-    dq[...] = jnp.zeros_like(dq)
-    dq[0, 0] = dq_diag[0]
-    dq[0, 1] = dq_diag[1]
-    for kv, table, out in ((kv_a, FIRST, dkv_a), (kv_b, SECOND, dkv_b)):
-        key_start = ((blk - steps_here(table)) * ROWS).astype(F32)
-        seen = key_start + (ROWS - 1) >= first_start
-
-        @pl.when(jnp.logical_not(seen))
-        def _():
-            out[...] = jnp.zeros_like(out)
-
-        @pl.when(seen)
-        def _():
-            key_block, value_block = kv[:, :HD], kv[:, HD:]
-            key_turned = transposed(key_block)
-            threshold = start - key_start
-            dkv[...] = jnp.zeros_like(dkv)
-
-            @pl.loop(0, 2)
-            def _(src):
-                base = src * MSG
-                for part, ref in ((0, own), (1, other)):
-                    at = pl.multiple_of(base + 1024, 16)
-                    stats_lo = ref[pl.ds(at, 16), :].astype(F32)
-                    stats_hi = ref[pl.ds(at + 16, 16), :].astype(F32)
-                    for h in range(2):
-                        lse2, const = row_terms(stats_lo, stats_hi, h)
-                        at = pl.multiple_of(base + h * 512, 16)
-                        q = ref[pl.ds(at, ROWS), :]
-                        do = ref[pl.ds(at + ROWS, ROWS), :]
-                        visible = key_at >= threshold
-                        query_add, key_add, value_add = unit(
-                            key_block,
-                            key_turned,
-                            value_block,
-                            q,
-                            do,
-                            lse2,
-                            const,
-                            rate,
-                            visible,
-                        )
-                        dq[part, 2 * src + h] += query_add
-                        dkv[:, :HD] += key_add
-                        dkv[:, HD:] += value_add
-
-            out[...] = dkv[...].astype(BF16)
-
-    for n in range(4):
-        dq_keep[n * ROWS : (n + 1) * ROWS, :] = dq[0, n].T
-        dq_send[n * ROWS : (n + 1) * ROWS, :] = dq[1, n].T.astype(BF16)
-
-
-def main(own, other, kv_a, kv_b, aux, dq_diag):
+    key_start = ((blk - steps_here(table)) * ROWS).astype(F32)
+    seen = key_start + (ROWS - 1) >= jnp.min(start)
+    if last_block:
+        dq[...] = dq_in[...]
+    else:
+        dq[...] = jnp.zeros_like(dq)
+        dq[0] = dq_in[...]
+    dkv[...] = jnp.zeros_like(dkv)
+
+    @pl.when(seen)
+    def _():
+        key_block, value_block = kv[:, :HD], kv[:, HD:]
+        key_turned = transposed(key_block)
+        threshold = start - key_start
+        key_at = lax.broadcasted_iota(jnp.int32, (ROWS, ROWS), 0).astype(F32)
+
+        @pl.loop(0, 2)
+        def _(h):
+            for n, ref in enumerate((own, core, y, cross)):
+                lse2, const = row_terms(ref, h)
+                at = pl.multiple_of(h * 512, 512)
+                q = ref[pl.ds(at, ROWS), :]
+                do = ref[pl.ds(at + ROWS, ROWS), :]
+                query_add, key_add, value_add = unit(
+                    key_block,
+                    key_turned,
+                    value_block,
+                    q,
+                    do,
+                    lse2,
+                    const,
+                    rate,
+                    key_at >= threshold,
+                )
+                dq[n, h] += query_add
+                dkv[:, :HD] += key_add
+                dkv[:, HD:] += value_add
+
+    out[...] = dkv[...].astype(BF16)
+    if last_block:
+        for n, (kept, sent) in enumerate(((0, 1), (2, 3))):
+            for h in range(2):
+                at = slice((2 * n + h) * ROWS, (2 * n + h + 1) * ROWS)
+                dq_keep[at, :] = dq[kept, h].T
+                dq_send[at, :] = dq[sent, h].T.astype(BF16)
+
+
+def block(table, last_block, own, core, y, cross, kv, aux, dq_in):
     vmem = pl.BlockSpec(memory_space=pltpu.VMEM)
+    sums = (4, 2, HD, ROWS)
+    out_shape = [jax.ShapeDtypeStruct((ROWS, 2 * HD), BF16)]
+    scratch = [pltpu.VMEM((ROWS, 2 * HD), F32)]
+    if last_block:
+        out_shape.append(jax.ShapeDtypeStruct((4 * ROWS, HD), BF16))
+        out_shape.append(jax.ShapeDtypeStruct((4 * ROWS, HD), F32))
+        scratch.insert(0, pltpu.VMEM(sums, F32))
+    else:
+        out_shape.append(jax.ShapeDtypeStruct(sums, F32))
     return pl.pallas_call(
-        main_kernel,
-        out_shape=(
-            jax.ShapeDtypeStruct((ROWS, 2 * HD), BF16),
-            jax.ShapeDtypeStruct((ROWS, 2 * HD), BF16),
-            jax.ShapeDtypeStruct((4 * ROWS, HD), BF16),
-            jax.ShapeDtypeStruct((4 * ROWS, HD), F32),
-        ),
-        in_specs=[vmem] * 6,
-        out_specs=(vmem,) * 4,
-        scratch_shapes=[
-            pltpu.VMEM((2, 4, HD, ROWS), F32),
-            pltpu.VMEM((ROWS, 2 * HD), F32),
-        ],
-        name="main",
+        functools.partial(block_kernel, table, last_block),
+        out_shape=tuple(out_shape),
+        in_specs=[vmem] * 7,
+        out_specs=(vmem,) * len(out_shape),
+        scratch_shapes=scratch,
+        name="second" if last_block else "first",
         compiler_params=pltpu.CompilerParams(vmem_limit_bytes=VMEM_LIMIT),
         cost_estimate=pl.CostEstimate(
-            flops=160 * ROWS * ROWS * HD, bytes_accessed=3 << 20, transcendentals=16 * ROWS * ROWS
+            flops=80 * ROWS * ROWS * HD, bytes_accessed=3 << 20, transcendentals=8 * ROWS * ROWS
         ),
-    )(own, other, kv_a, kv_b, aux, dq_diag)
+    )(own, core, y, cross, kv, aux, dq_in)
 
 
 def last_kernel(terms, dq_keep, dq_core, dq_y, grad_query, grad_key, grad_value):
@@ -307,7 +354,7 @@
         grad_query[:, h * HD : (h + 1) * HD] = (total * SCALE).astype(BF16)
     half = terms.shape[0] // 2
     for g in range(2):
-        total = jnp.sum(terms[g * half : (g + 1) * half], axis=0)
+        total = jnp.sum(terms[g * half : (g + 1) * half].astype(F32), axis=0)
         grad_key[:, g * HD : (g + 1) * HD] = (total[:, :HD] * SCALE).astype(BF16)
         grad_value[:, g * HD : (g + 1) * HD] = total[:, HD:].astype(BF16)
 
@@ -343,6 +390,7 @@
 ):
     to_core = pairs_from(other_core)
     to_y = pairs_from(other_y)
+    to_cross = pairs_from(lambda index: other_y(other_core(index)))
     back_a = pairs_from(functools.partial(back_source, FIRST))
     back_b = pairs_from(functools.partial(back_source, SECOND))
     msg, kv, aux = prep(
@@ -358,19 +406,20 @@
         penalty_weights,
     )
     msg_y = moved(msg, to_y)
+    msg_cross = moved(msg, to_cross)
     kv_a = moved(kv, back_a)
     kv_b = moved(kv, back_b)
+    msg_core = moved(msg, to_core)
     dq_diag, dkv_diag = diag(msg, kv, aux)
-    msg_y, kv_a = lax.optimization_barrier((msg_y, kv_a))
-    own = jnp.concatenate([msg, msg_y], axis=0)
-    other = moved(own, to_core)
-    dkv_a, dkv_b, dq_send, dq_keep = main(own, other, kv_a, kv_b, aux, dq_diag)
+    messages = (msg, msg_core, msg_y, msg_cross)
+    dkv_a, dq = block(FIRST, False, *messages, kv_a, aux, dq_diag)
     got_a = moved(dkv_a, inverse(back_a))
+    dkv_b, dq_send, dq_keep = block(SECOND, True, *messages, kv_b, aux, dq)
     got_b = moved(dkv_b, inverse(back_b))
     dq_core = moved(dq_send, to_core)
     dq_pass = (dq_keep[512:] + dq_core[512:].astype(F32)).astype(BF16)
+    terms = (dkv_diag + got_a.astype(F32) + got_b.astype(F32)).astype(BF16)
     dq_y = moved(dq_pass, to_y)
-    terms = dkv_diag + got_a.astype(F32) + got_b.astype(F32)
     terms = lax.all_to_all(terms.reshape(16, 16, 2 * HD), "head", 0, 0)
     return last(terms, dq_keep, dq_core, dq_y)
 

time: 99.1 us -> 81.9 us (0.83)
  the two profiles are of different devices: /device:TPU:38 before, /device:TPU:33 now
where the time goes in v2:
time: 81.9 us; the launch traced here: 81.4 us
  starting transfers between devices  55.8 us (68%)
  waiting for transfers between devices  17.2 us (21%)
  Pallas kernels  4.29 us (5%)
  local copies, waits for them, and re-layouts  2.55 us (3%)
    ppermute x9, starting transfers between devices, moved(): return lax.ppermute(value, ('blk', 'head'), pairs)  40.8 us
    all_to_all x1, starting transfers between devices, local(): terms = lax.all_to_all(terms.reshape(16, 16, 2 * HD), 'head', 0, 0)  15 us
    all_to_all x1, waiting for transfers between devices, local(): terms = lax.all_to_all(terms.reshape(16, 16, 2 * HD), 'head', 0, 0)  12 us
    ppermute x9, waiting for transfers between devices, moved(): return lax.ppermute(value, ('blk', 'head'), pairs)  5.2 us
    unnamed x8, local copies, waits for them, and re-layouts  2.55 us
    pallas_call x1, Pallas kernels, prep(): pl.pallas_call(prep_kernel, out_shape=(jax.ShapeDtypeStruct((MSG, HD), BF...  2.27 us
  transfers between devices with their start and end apart: 10, of which 3 were waited for; matrix products, arithmetic and copies ran while one was open for 1% of the time, Pallas kernels for 1%

profile of v2, /device:TPU:33, one launch (start us, length us, event | category | flops | bytes accessed | tf_op | source)
XLA Modules:
  0.0 81.4 jit_solution(4580941657202306048)
XLA Ops:
  0.6 2.3 %prep.1 = (bf16[1088,128]{1,0:T(8,128)(2,1)}, bf16[256,256]{1,0:T(8,128)(2,1)}, f32[8,256]{1,0:T(8,128)}) custom-call(bf16[256,256]{1,0:T(8,128)(2,1)} %q_in.1, bf16[256,256]{1,0:T(8,128)(2,1)} %k_in.1, bf16[256,256]{1,0:T(8,128)(2,1)} %v_in.1, bf16[256,256]{1,0:T(8,128)(2,1)} %o_in.1, bf16[256,256]{1,0:T(8,128)(2,1)} %do_in.1, f32[2,256]{1,0:T(2,128)} %lse_in.1, ...), custom_call_target="tpu_custom_call" | custom-call | tf_op jit(solution)/shard_map/prep/pallas_call | solution.py:186
  2.9 3.8 %collective-permute-start.2 = (bf16[1088,128]{1,0:T(8,128)(2,1)}, bf16[1088,128]{1,0:T(8,128)(2,1)S(1)}, u32[]{:S(2)}, u32[]{:S(2)}) collective-permute-start(bf16[1088,128]{1,0:T(8,128)(2,1)} %get-tuple-element.13.msg.own), channel_id=1, source_target_pairs={{5,0},{4,1},{7,2},{6,3},{1,4},{0,5},{3,6},{2,7},{13,8},{12,9},{15,... | collective-permute-start | bytes 835592 | tf_op jit(solution)/shard_map/ppermute | solution.py:66
  6.7 2.1 %collective-permute-start.1 = (bf16[1088,128]{1,0:T(8,128)(2,1)}, bf16[1088,128]{1,0:T(8,128)(2,1)S(1)}, u32[]{:S(2)}, u32[]{:S(2)}) collective-permute-start(bf16[1088,128]{1,0:T(8,128)(2,1)} %get-tuple-element.13.msg.own), channel_id=1, source_target_pairs={{4,0},{5,1},{6,2},{7,3},{0,4},{1,5},{2,6},{3,7},{12,8},{13,9},{14,... | collective-permute-start | bytes 835592 | tf_op jit(solution)/shard_map/ppermute | solution.py:66
  8.8 2.1 %collective-permute-start = (bf16[1088,128]{1,0:T(8,128)(2,1)}, bf16[1088,128]{1,0:T(8,128)(2,1)S(1)}, u32[]{:S(2)}, u32[]{:S(2)}) collective-permute-start(bf16[1088,128]{1,0:T(8,128)(2,1)} %get-tuple-element.13.msg.own), channel_id=1, source_target_pairs={{1,0},{0,1},{3,2},{2,3},{5,4},{4,5},{7,6},{6,7},{9,8},{8,9},{11,10... | collective-permute-start | bytes 835592 | tf_op jit(solution)/shard_map/ppermute | solution.py:66
  10.9 2.7 %collective-permute-start.3 = (bf16[256,256]{1,0:T(8,128)(2,1)}, bf16[256,256]{1,0:T(8,128)(2,1)S(1)}, u32[]{:S(2)}, u32[]{:S(2)}) collective-permute-start(bf16[256,256]{1,0:T(8,128)(2,1)} %get-tuple-element.14.kv), channel_id=1, source_target_pairs={{498,0},{401,1},{496,2},{403,3},{486,4},{421,5},{484,6},{423,7},{5... | collective-permute-start | bytes 393224 | tf_op jit(solution)/shard_map/ppermute | solution.py:66
  13.6 12.0 %collective-permute-start.5 = (bf16[256,256]{1,0:T(8,128)(2,1)}, bf16[256,256]{1,0:T(8,128)(2,1)S(1)}, u32[]{:S(2)}, u32[]{:S(2)}) collective-permute-start(bf16[256,256]{1,0:T(8,128)(2,1)} %get-tuple-element.14.kv), channel_id=1, source_target_pairs={{466,0},{433,1},{464,2},{435,3},{454,4},{389,5},{452,6},{391,7},{4... | collective-permute-start | bytes 393224 | tf_op jit(solution)/shard_map/ppermute | solution.py:66
  25.6 0.9 %copy-done = bf16[1088,128]{1,0:T(8,128)(2,1)S(1)} copy-done((bf16[1088,128]{1,0:T(8,128)(2,1)S(1)}, bf16[1088,128]{1,0:T(8,128)(2,1)}, u32[]{:S(2)}) %copy-start) | copy-done | bytes 278552
  26.6 0.9 %copy-done.1 = bf16[256,256]{1,0:T(8,128)(2,1)S(1)} copy-done((bf16[256,256]{1,0:T(8,128)(2,1)S(1)}, bf16[256,256]{1,0:T(8,128)(2,1)}, u32[]{:S(2)}) %copy-start.1) | copy-done | bytes 131096
  27.5 0.7 copy-done.2
  28.2 0.8 diag.1
  29.0 0.0 collective-permute-done.2.cross
  29.0 0.0 collective-permute-done.1.y
  29.0 0.1 first.1
  29.1 1.5 %collective-permute-done.5.kv = bf16[256,256]{1,0:T(8,128)(2,1)S(1)} collective-permute-done((bf16[256,256]{1,0:T(8,128)(2,1)}, bf16[256,256]{1,0:T(8,128)(2,1)S(1)}, u32[]{:S(2)}, u32[]{:S(2)}) %collective-permute-start.5) | collective-permute-done | bytes 131104 | tf_op jit(solution)/shard_map/ppermute | solution.py:66
  30.7 0.4 second.1
  31.1 1.9 %collective-permute-start.6 = (bf16[256,256]{1,0:T(8,128)(2,1)S(1)}, bf16[256,256]{1,0:T(8,128)(2,1)S(1)}, u32[]{:S(2)}, u32[]{:S(2)}) collective-permute-start(bf16[256,256]{1,0:T(8,128)(2,1)S(1)} %get-tuple-element.20), channel_id=1, source_target_pairs={{0,466},{1,433},{2,464},{3,435},{4,454},{5,389},{6,452},{7,391},{8... | collective-permute-start | bytes 393224 | tf_op jit(solution)/shard_map/ppermute | solution.py:66
  33.0 6.8 %collective-permute-start.4 = (bf16[256,256]{1,0:T(8,128)(2,1)S(1)}, bf16[256,256]{1,0:T(8,128)(2,1)S(1)}, u32[]{:S(2)}, u32[]{:S(2)}) collective-permute-start(bf16[256,256]{1,0:T(8,128)(2,1)S(1)} %get-tuple-element.18), channel_id=1, source_target_pairs={{0,498},{1,401},{2,496},{3,403},{4,486},{5,421},{6,484},{7,423},{8... | collective-permute-start | bytes 393224 | tf_op jit(solution)/shard_map/ppermute | solution.py:66
  39.8 6.1 %collective-permute-start.7 = (bf16[1024,128]{1,0:T(8,128)(2,1)S(1)}, bf16[1024,128]{1,0:T(8,128)(2,1)S(1)}, u32[]{:S(2)}, u32[]{:S(2)}) collective-permute-start(bf16[1024,128]{1,0:T(8,128)(2,1)S(1)} %get-tuple-element.22), channel_id=1, source_target_pairs={{1,0},{0,1},{3,2},{2,3},{5,4},{4,5},{7,6},{6,7},{9,8},{8,9},{11,10... | collective-permute-start | bytes 786440 | tf_op jit(solution)/shard_map/ppermute | solution.py:66
  45.9 0.7 add_convert_fusion.1
  46.6 15.0 %all-to-all-start = ((bf16[16,16,256]{2,1,0:T(8,128)(2,1)}), bf16[16,16,256]{2,1,0:T(8,128)(2,1)S(1)}, u32[]{:S(2)}, u32[]{:S(2)}) async-start(bf16[16,16,256]{2,1,0:T(8,128)(2,1)} %bitcast.1), calls=%async_computation | async-start | bytes 262144 | tf_op jit(solution)/shard_map/all_to_all | solution.py:423
  61.7 3.3 %collective-permute-start.8 = (bf16[512,128]{1,0:T(8,128)(2,1)S(1)}, bf16[512,128]{1,0:T(8,128)(2,1)S(1)}, u32[]{:S(2)}, u32[]{:S(2)}) collective-permute-start(bf16[512,128]{1,0:T(8,128)(2,1)S(1)} %add_convert_fusion), channel_id=1, source_target_pairs={{4,0},{5,1},{6,2},{7,3},{0,4},{1,5},{2,6},{3,7},{12,8},{13,9},{14,... | collective-permute-start | bytes 393224 | tf_op jit(solution)/shard_map/ppermute | solution.py:66
  65.0 3.7 %collective-permute-done.8.dq_y = bf16[512,128]{1,0:T(8,128)(2,1)S(1)} collective-permute-done((bf16[512,128]{1,0:T(8,128)(2,1)S(1)}, bf16[512,128]{1,0:T(8,128)(2,1)S(1)}, u32[]{:S(2)}, u32[]{:S(2)}) %collective-permute-start.8) | collective-permute-done | bytes 131104 | tf_op jit(solution)/shard_map/ppermute | solution.py:66
  68.6 12.0 %all-to-all-done.terms = bf16[16,16,256]{2,1,0:T(8,128)(2,1)S(1)} async-done(((bf16[16,16,256]{2,1,0:T(8,128)(2,1)}), bf16[16,16,256]{2,1,0:T(8,128)(2,1)S(1)}, u32[]{:S(2)}, u32[]{:S(2)}) %all-to-all-start) | async-done | bytes 131104 | tf_op jit(solution)/shard_map/all_to_all | solution.py:423
  80.6 0.7 last.1
  (11 shorter events, 0.1 us)
Async XLA Ops:
  2.9 26.1 %collective-permute-start.2 = (bf16[1088,128]{1,0:T(8,128)(2,1)}, bf16[1088,128]{1,0:T(8,128)(2,1)S(1)}, u32[]{:S(2)}, u32[]{:S(2)}) collective-permute-start(bf16[1088,128]{1,0:T(8,128)(2,1)} %get-tuple-element.13.msg.own), channel_id=1, source_target_pairs={{5,0},{4,1},{7,2},{6,3},{1,4},{0,5},{3,6},{2,7},{13,8},{12,9},{15,... | collective-permute-start | bytes 835592 | tf_op jit(solution)/shard_map/ppermute | solution.py:66
  6.7 22.3 %collective-permute-start.1 = (bf16[1088,128]{1,0:T(8,128)(2,1)}, bf16[1088,128]{1,0:T(8,128)(2,1)S(1)}, u32[]{:S(2)}, u32[]{:S(2)}) collective-permute-start(bf16[1088,128]{1,0:T(8,128)(2,1)} %get-tuple-element.13.msg.own), channel_id=1, source_target_pairs={{4,0},{5,1},{6,2},{7,3},{0,4},{1,5},{2,6},{3,7},{12,8},{13,9},{14,... | collective-permute-start | bytes 835592 | tf_op jit(solution)/shard_map/ppermute | solution.py:66
  8.8 20.2 %collective-permute-start = (bf16[1088,128]{1,0:T(8,128)(2,1)}, bf16[1088,128]{1,0:T(8,128)(2,1)S(1)}, u32[]{:S(2)}, u32[]{:S(2)}) collective-permute-start(bf16[1088,128]{1,0:T(8,128)(2,1)} %get-tuple-element.13.msg.own), channel_id=1, source_target_pairs={{1,0},{0,1},{3,2},{2,3},{5,4},{4,5},{7,6},{6,7},{9,8},{8,9},{11,10... | collective-permute-start | bytes 835592 | tf_op jit(solution)/shard_map/ppermute | solution.py:66
  10.9 18.0 %collective-permute-start.3 = (bf16[256,256]{1,0:T(8,128)(2,1)}, bf16[256,256]{1,0:T(8,128)(2,1)S(1)}, u32[]{:S(2)}, u32[]{:S(2)}) collective-permute-start(bf16[256,256]{1,0:T(8,128)(2,1)} %get-tuple-element.14.kv), channel_id=1, source_target_pairs={{498,0},{401,1},{496,2},{403,3},{486,4},{421,5},{484,6},{423,7},{5... | collective-permute-start | bytes 393224 | tf_op jit(solution)/shard_map/ppermute | solution.py:66
  13.6 17.1 %collective-permute-start.5 = (bf16[256,256]{1,0:T(8,128)(2,1)}, bf16[256,256]{1,0:T(8,128)(2,1)S(1)}, u32[]{:S(2)}, u32[]{:S(2)}) collective-permute-start(bf16[256,256]{1,0:T(8,128)(2,1)} %get-tuple-element.14.kv), channel_id=1, source_target_pairs={{466,0},{433,1},{464,2},{435,3},{454,4},{389,5},{452,6},{391,7},{4... | collective-permute-start | bytes 393224 | tf_op jit(solution)/shard_map/ppermute | solution.py:66
  25.6 1.0 %copy-start = (bf16[1088,128]{1,0:T(8,128)(2,1)S(1)}, bf16[1088,128]{1,0:T(8,128)(2,1)}, u32[]{:S(2)}) copy-start(bf16[1088,128]{1,0:T(8,128)(2,1)} %get-tuple-element.13.msg.own) | copy-start | bytes 835588
  26.6 0.9 %copy-start.1 = (bf16[256,256]{1,0:T(8,128)(2,1)S(1)}, bf16[256,256]{1,0:T(8,128)(2,1)}, u32[]{:S(2)}) copy-start(bf16[256,256]{1,0:T(8,128)(2,1)} %get-tuple-element.14.kv) | copy-start | bytes 393220
  27.5 0.7 copy-start.2
  28.2 0.8 %copy-start.3 = (f32[8,256]{1,0:T(8,128)S(1)}, f32[8,256]{1,0:T(8,128)}, u32[]{:S(2)}) copy-start(f32[8,256]{1,0:T(8,128)} %get-tuple-element.15.aux) | copy-start | bytes 24580
  31.1 14.8 %collective-permute-start.6 = (bf16[256,256]{1,0:T(8,128)(2,1)S(1)}, bf16[256,256]{1,0:T(8,128)(2,1)S(1)}, u32[]{:S(2)}, u32[]{:S(2)}) collective-permute-start(bf16[256,256]{1,0:T(8,128)(2,1)S(1)} %get-tuple-element.20), channel_id=1, source_target_pairs={{0,466},{1,433},{2,464},{3,435},{4,454},{5,389},{6,452},{7,391},{8... | collective-permute-start | bytes 393224 | tf_op jit(solution)/shard_map/ppermute | solution.py:66
  33.0 12.9 %collective-permute-start.4 = (bf16[256,256]{1,0:T(8,128)(2,1)S(1)}, bf16[256,256]{1,0:T(8,128)(2,1)S(1)}, u32[]{:S(2)}, u32[]{:S(2)}) collective-permute-start(bf16[256,256]{1,0:T(8,128)(2,1)S(1)} %get-tuple-element.18), channel_id=1, source_target_pairs={{0,498},{1,401},{2,496},{3,403},{4,486},{5,421},{6,484},{7,423},{8... | collective-permute-start | bytes 393224 | tf_op jit(solution)/shard_map/ppermute | solution.py:66
  39.8 21.8 %collective-permute-start.7 = (bf16[1024,128]{1,0:T(8,128)(2,1)S(1)}, bf16[1024,128]{1,0:T(8,128)(2,1)S(1)}, u32[]{:S(2)}, u32[]{:S(2)}) collective-permute-start(bf16[1024,128]{1,0:T(8,128)(2,1)S(1)} %get-tuple-element.22), channel_id=1, source_target_pairs={{1,0},{0,1},{3,2},{2,3},{5,4},{4,5},{7,6},{6,7},{9,8},{8,9},{11,10... | collective-permute-start | bytes 786440 | tf_op jit(solution)/shard_map/ppermute | solution.py:66
  46.6 34.0 %all-to-all-start = ((bf16[16,16,256]{2,1,0:T(8,128)(2,1)}), bf16[16,16,256]{2,1,0:T(8,128)(2,1)S(1)}, u32[]{:S(2)}, u32[]{:S(2)}) async-start(bf16[16,16,256]{2,1,0:T(8,128)(2,1)} %bitcast.1), calls=%async_computation | async-start | bytes 262144 | tf_op jit(solution)/shard_map/all_to_all | solution.py:423
  61.7 7.0 %collective-permute-start.8 = (bf16[512,128]{1,0:T(8,128)(2,1)S(1)}, bf16[512,128]{1,0:T(8,128)(2,1)S(1)}, u32[]{:S(2)}, u32[]{:S(2)}) collective-permute-start(bf16[512,128]{1,0:T(8,128)(2,1)S(1)} %add_convert_fusion), channel_id=1, source_target_pairs={{4,0},{5,1},{6,2},{7,3},{0,4},{1,5},{2,6},{3,7},{12,8},{13,9},{14,... | collective-permute-start | bytes 393224 | tf_op jit(solution)/shard_map/ppermute | solution.py:66

commit v3 on v2

v3 whole, which is shorter than its diff:
```python
import functools
import math

import jax
import jax.numpy as jnp
from jax import lax
from jax.experimental import pallas as pl
from jax.experimental.pallas import tpu as pltpu
from jax.sharding import PartitionSpec as P

HD = 128
ROWS = 256
SCALE = HD ** (-0.5)
LOG2E = math.log2(math.e)
MSG = 4 * ROWS + 64
GROUP = 8
F32 = jnp.float32
OWN_FLOPS = 1 << 28
EARLY_FLOPS = 1 << 34
LATE_FLOPS = 1 << 30
TURN_FLOPS = 1 << 27
QUERY_FLOPS = 1 << 34
BF16 = jnp.bfloat16
PREP_VMEM_LIMIT = 62 * 1024 * 1024
VMEM_LIMIT = 24 * 1024 * 1024

NEAR = ((1, 7), (2, 6))
FAR = ((3, 5), (4, 8))

HEAD_ORDER = [y * 4 + z_hi * 2 + core for z_hi in (1, 0) for y in range(4) for core in range(2)]


def place(index):
    blk, head = divmod(index, 16)
    x, z_lo = divmod(blk, 8)
    y, rest = divmod(head, 4)
    z_hi, core = divmod(rest, 2)
    return x, y, z_hi * 8 + z_lo, core


def device(x, y, z, core):
    z_hi, z_lo = divmod(z % 16, 8)
    return ((x % 4) * 8 + z_lo) * 16 + (y % 4) * 4 + z_hi * 2 + core


def pairs_from(source_of):
    return [(source_of(index), index) for index in range(512)]


def back_source(table, index):
    x, y, z, core = place(index)
    steps = table[y % 2][core]
    source_x = x if z % 8 >= steps else x - 1
    up = steps < 4 or (steps == 4 and z % 2 == 0)
    return device(source_x, y, z - steps if up else z + 8 - steps, core)


def other_core(index):
    x, y, z, core = place(index)
    return device(x, y, z, 1 - core)


def other_y(index):
    x, y, z, core = place(index)
    return device(x, y ^ 1, z, core)


def inverse(pairs):
    return [(target, source) for source, target in pairs]


def moved(value, pairs):
    return lax.ppermute(value, ("blk", "head"), pairs)


def steps_here(table):
    head = lax.axis_index("head")
    odd = lax.rem(lax.div(head, 4), 2) == 1
    core = lax.rem(head, 2) == 1
    return jnp.where(
        odd,
        jnp.where(core, table[1][1], table[1][0]),
        jnp.where(core, table[0][1], table[0][0]),
    )


def nt(a, b):
    return lax.dot_general(a, b, (((1,), (1,)), ((), ())), preferred_element_type=F32)


def nn(a, b):
    return lax.dot_general(a, b, (((1,), (0,)), ((), ())), preferred_element_type=F32)


def transposed(block):
    return block.astype(F32).T.astype(BF16)


def prep_kernel(
    q_in,
    k_in,
    v_in,
    o_in,
    do_in,
    lse_in,
    ent_in,
    seg_in,
    weight_index_in,
    weights_in,
    msg,
    kv,
    aux,
    q,
    k,
    v,
    o,
    do,
    lse,
    ent,
    seg,
    weight_index,
    weights,
    rows,
    sems,
):
    arriving = [
        pltpu.make_async_copy(source, target, sems.at[n])
        for n, (source, target) in enumerate(
            (
                (weight_index_in, weight_index),
                (weights_in, weights),
                (seg_in, seg),
                (lse_in, lse),
                (ent_in, ent),
                (do_in, do),
                (o_in, o),
                (q_in, q),
                (k_in, k),
                (v_in, v),
            )
        )
    ]
    for copy in arriving:
        copy.start()
    for copy in arriving:
        copy.wait()
    blk = lax.axis_index("blk")
    head = lax.axis_index("head")
    column = pl.multiple_of(lax.div(head, 8) * HD, HD)
    kv[:, :HD] = k[:, pl.ds(column, HD)]
    kv[:, HD:] = v[:, pl.ds(column, HD)]
    docs = weight_index.shape[0]
    tokens = seg[...]
    first = seg[pl.ds(2 * blk, 1), :]
    second = seg[pl.ds(2 * blk + 1, 1), :]
    seg_rows = jnp.concatenate([first, second], axis=1)
    rate = jnp.zeros((1, ROWS), F32)
    for d in range(docs):
        rows[d : d + 1, :HD] = jnp.sum(
            jnp.where(tokens < d, 1.0, 0.0), axis=0, keepdims=True
        )
        rate = jnp.where(seg_rows == d, weights[weight_index[d]], rate)
    starts = jnp.sum(rows[:docs, :HD], axis=1, keepdims=True)
    doc = lax.broadcasted_iota(jnp.int32, (docs, ROWS), 0)
    start = jnp.sum(jnp.where(doc == seg_rows, starts, 0.0), axis=0, keepdims=True)
    aux[...] = jnp.zeros_like(aux)
    aux[0:1, :] = start
    aux[1:2, :] = rate
    rows[...] = jnp.zeros_like(rows)
    for h in range(2):
        columns = slice(h * HD, (h + 1) * HD)
        do_h = do[:, columns]
        msg[h * ROWS : (h + 1) * ROWS, :] = q[:, columns]
        msg[(2 + h) * ROWS : (3 + h) * ROWS, :] = do_h
        product = do_h.astype(F32) * o[:, columns].astype(F32)
        delta = jnp.sum(product.T, axis=0, keepdims=True)
        lse_h = lse[h : h + 1, :]
        const = delta + rate * (ent[h : h + 1, :] - lse_h)
        for at, value in ((0, lse_h), (3, const)):
            for part in range(3):
                piece = value.astype(BF16).astype(F32)
                rows[at + part : at + part + 1, :] = piece
                value = value - piece
        at = 1024 + 32 * h
        msg[at : at + 16, :] = rows[:, :HD].astype(BF16)
        msg[at + 16 : at + 32, :] = rows[:, HD:].astype(BF16)


def prep(*arrays):
    vmem = pl.BlockSpec(memory_space=pltpu.VMEM)
    held = [pltpu.VMEM(array.shape, array.dtype) for array in arrays[:8]]
    held += [pltpu.SMEM(array.shape, array.dtype) for array in arrays[8:]]
    return pl.pallas_call(
        prep_kernel,
        out_shape=(
            jax.ShapeDtypeStruct((MSG, HD), BF16),
            jax.ShapeDtypeStruct((ROWS, 2 * HD), BF16),
            jax.ShapeDtypeStruct((8, ROWS), F32),
        ),
        in_specs=[pl.BlockSpec(memory_space=pltpu.HBM)] * 10,
        out_specs=(vmem,) * 3,
        scratch_shapes=held
        + [pltpu.VMEM((16, ROWS), F32), pltpu.SemaphoreType.DMA((10,))],
        name="prep",
        compiler_params=pltpu.CompilerParams(vmem_limit_bytes=PREP_VMEM_LIMIT),
    )(*arrays)


def both(row):
    return jnp.concatenate([row, row], axis=1)


def row_terms(msg):
    halves = [msg[at : at + 16, :].astype(F32) for at in range(4 * ROWS, MSG, 16)]

    def whole(row):
        return jnp.concatenate(
            [
                half[row : row + 1, :] + half[row + 1 : row + 2, :] + half[row + 2 : row + 3, :]
                for half in halves
            ],
            axis=1,
        )

    return whole(0) * LOG2E, whole(3)


def probs_and_dscores(key_block, value_block, msg, rate, visible):
    lse2, const = row_terms(msg)
    scores = nt(key_block, msg[: 2 * ROWS, :])
    probs = jnp.where(visible, jnp.exp2(scores * (SCALE * LOG2E) - lse2), 0.0)
    dprobs = nt(value_block, msg[2 * ROWS : 4 * ROWS, :])
    dscores = probs * (dprobs - const - scores * rate)
    return probs.astype(BF16), dscores.astype(BF16)


def sums_of(messages, key_block, value_block, rate, visible, put_query_sum):
    key_turned = transposed(key_block)
    key_sum = value_sum = before = None
    for n, msg in enumerate((*messages, None)):
        here = None
        if msg is not None:
            here = probs_and_dscores(key_block, value_block, msg, rate, visible)
        if before is not None:
            probs, dscores = before
            past = messages[n - 1]
            put_query_sum(n - 1, nn(key_turned, dscores))
            key_add = nn(dscores, past[: 2 * ROWS, :])
            value_add = nn(probs, past[2 * ROWS : 4 * ROWS, :])
            key_sum = key_add if key_sum is None else key_sum + key_add
            value_sum = value_add if value_sum is None else value_sum + value_add
        before = here
    return key_sum, value_sum


def block_place(table, start):
    key_start = ((lax.axis_index("blk") - steps_here(table)) * ROWS).astype(F32)
    return start - key_start, key_start + (ROWS - 1) >= jnp.min(start)


def earlier_sums(table, messages, kv, aux, put):
    reach, _ = block_place(table, aux[0:1, :])
    key_at = lax.broadcasted_iota(jnp.int32, (ROWS, 2 * ROWS), 0).astype(F32)
    return sums_of(
        messages,
        kv[:, :HD],
        kv[:, HD:],
        both(aux[1:2, :] * SCALE),
        key_at >= both(reach),
        put,
    )


def early_kernel(own, y, cross, kv_far, aux, dq_own, far, dq):
    _, seen = block_place(FAR, aux[0:1, :])

    @pl.when(jnp.logical_not(seen))
    def _():
        dq[0] = dq_own[0]
        dq[1:] = jnp.zeros_like(dq[1:])
        far[...] = jnp.zeros_like(far)

    @pl.when(seen)
    def _():
        def put(n, query_sum):
            dq[n] = dq_own[0] + query_sum if n == 0 else query_sum

        key_sum, value_sum = earlier_sums(FAR, (own, y, cross), kv_far, aux, put)
        far[:, :HD] = key_sum
        far[:, HD:] = value_sum


def late_kernel(
    own, core, y, cross, kv_far, kv_near, aux, far_in, dq_in, far, near, dq
):
    _, far_seen = block_place(FAR, aux[0:1, :])
    _, near_seen = block_place(NEAR, aux[0:1, :])

    @pl.when(jnp.logical_not(near_seen))
    def _():
        dq[:3] = dq_in[...]
        dq[3] = jnp.zeros_like(dq[3])
        near[...] = jnp.zeros_like(near)

    @pl.when(near_seen)
    def _():
        def put(n, query_sum):
            dq[n] = dq_in[n] + query_sum if n < 3 else query_sum

        key_sum, value_sum = earlier_sums(NEAR, (own, y, cross, core), kv_near, aux, put)
        near[:, :HD] = key_sum.astype(BF16)
        near[:, HD:] = value_sum.astype(BF16)

    @pl.when(jnp.logical_not(far_seen))
    def _():
        far[...] = far_in[...].astype(BF16)

    @pl.when(far_seen)
    def _():
        def put(n, query_sum):
            dq[3] += query_sum

        key_sum, value_sum = earlier_sums(FAR, (core,), kv_far, aux, put)
        far[:, :HD] = (far_in[:, :HD] + key_sum).astype(BF16)
        far[:, HD:] = (far_in[:, HD:] + value_sum).astype(BF16)


def kernel_call(kernel, name, out_shape, flops, *arrays):
    vmem = pl.BlockSpec(memory_space=pltpu.VMEM)
    return pl.pallas_call(
        kernel,
        out_shape=out_shape,
        in_specs=[vmem] * len(arrays),
        out_specs=(vmem,) * len(out_shape),
        name=name,
        compiler_params=pltpu.CompilerParams(vmem_limit_bytes=VMEM_LIMIT),
        cost_estimate=pl.CostEstimate(flops=flops, bytes_accessed=1 << 20, transcendentals=0),
    )(*arrays)


def own_kernel(msg, kv, aux, dq, dkv):
    blk = lax.axis_index("blk")
    threshold = aux[0:1, :] - (blk * ROWS).astype(F32)
    key_at = lax.broadcasted_iota(jnp.int32, (ROWS, ROWS), 0)
    query_at = lax.broadcasted_iota(jnp.int32, (ROWS, ROWS), 1)
    causal = both(jnp.where(key_at <= query_at, key_at, -1).astype(F32))

    def put(n, query_sum):
        dq[n] = query_sum

    key_sum, value_sum = sums_of(
        (msg,),
        kv[:, :HD],
        kv[:, HD:],
        both(aux[1:2, :] * SCALE),
        causal >= both(jnp.maximum(threshold, 0.0)),
        put,
    )
    dkv[:, :HD] = key_sum
    dkv[:, HD:] = value_sum


def turn_kernel(dq, send, keep):
    for n, (kept, sent) in enumerate(((0, 3), (1, 2))):
        at = slice(2 * n * ROWS, 2 * (n + 1) * ROWS)
        keep[at, :] = dq[kept].T
        send[at, :] = dq[sent].T.astype(BF16)


def query_kernel(dq_keep, dq_core, dq_y, grad_query):
    for h in range(2):
        at = slice(h * ROWS, (h + 1) * ROWS)
        total = dq_keep[at, :] + dq_core[at, :].astype(F32) + dq_y[at, :].astype(F32)
        grad_query[:, h * HD : (h + 1) * HD] = (total * SCALE).astype(BF16)


def terms_kernel(own, far, near, terms):
    share = terms.shape[1]
    for n, head in enumerate(HEAD_ORDER):
        at = slice(head * share, (head + 1) * share)
        total = own[at, :] + far[at, :].astype(F32) + near[at, :].astype(F32)
        terms[n] = total.astype(BF16)


def key_value_kernel(terms, grad_key, grad_value):
    for g in range(2):
        total = 0.0
        for n, head in enumerate(HEAD_ORDER):
            if head // 8 == g:
                total = total + terms[n].astype(F32)
        grad_key[:, g * HD : (g + 1) * HD] = (total[:, :HD] * SCALE).astype(BF16)
        grad_value[:, g * HD : (g + 1) * HD] = total[:, HD:].astype(BF16)


def local(
    query,
    key,
    value,
    output,
    grad_output,
    log_norm,
    entropy,
    segment_ids,
    weight_index,
    penalty_weights,
):
    to_core = pairs_from(other_core)
    to_y = pairs_from(other_y)
    to_cross = pairs_from(lambda index: other_y(other_core(index)))
    back_near = pairs_from(functools.partial(back_source, NEAR))
    back_far = pairs_from(functools.partial(back_source, FAR))
    msg, kv, aux = prep(
        query,
        key,
        value,
        output,
        grad_output,
        log_norm,
        entropy,
        segment_ids.reshape(-1, HD),
        weight_index,
        penalty_weights,
    )
    msg_core = moved(msg, to_core)
    kv_near = moved(kv, back_near)
    msg_y = moved(msg, to_y)
    kv_far = moved(kv, back_far)
    msg_cross = moved(msg, to_cross)
    sums = functools.partial(jax.ShapeDtypeStruct, dtype=F32)
    pair = jax.ShapeDtypeStruct((ROWS, 2 * HD), BF16)
    dq_own, dkv_own = kernel_call(
        own_kernel,
        "own",
        (sums((1, HD, 2 * ROWS)), sums((ROWS, 2 * HD))),
        OWN_FLOPS,
        msg,
        kv,
        aux,
    )
    dkv_far, dq = kernel_call(
        early_kernel,
        "early",
        (sums((ROWS, 2 * HD)), sums((3, HD, 2 * ROWS))),
        EARLY_FLOPS,
        msg,
        msg_y,
        msg_cross,
        kv_far,
        aux,
        dq_own,
    )
    dkv_far, dkv_near, dq = kernel_call(
        late_kernel,
        "late",
        (pair, pair, sums((4, HD, 2 * ROWS))),
        LATE_FLOPS,
        msg,
        msg_core,
        msg_y,
        msg_cross,
        kv_far,
        kv_near,
        aux,
        dkv_far,
        dq,
    )
    got_near = moved(dkv_near, inverse(back_near))
    got_far = moved(dkv_far, inverse(back_far))
    dq_send, dq_keep = kernel_call(
        turn_kernel,
        "turn",
        (jax.ShapeDtypeStruct((4 * ROWS, HD), BF16), sums((4 * ROWS, HD))),
        TURN_FLOPS,
        dq,
    )
    dq_core = moved(dq_send, to_core)
    dq_pass = (dq_keep[512:] + dq_core[512:].astype(F32)).astype(BF16)
    share = jax.ShapeDtypeStruct((16, ROWS // 16, 2 * HD), BF16)
    (terms,) = kernel_call(terms_kernel, "terms", (share,), 0, dkv_own, got_far, got_near)
    dq_y = moved(dq_pass, to_y)
    terms = lax.all_to_all(terms, "head", 0, 0, axis_index_groups=[HEAD_ORDER])
    (grad_query,) = kernel_call(query_kernel, "query", (pair,), QUERY_FLOPS, dq_keep, dq_core, dq_y)
    result = jax.ShapeDtypeStruct((terms.shape[1], 2 * HD), BF16)
    return (grad_query, *kernel_call(key_value_kernel, "key_value", (result, result), 0, terms))


def solution(mesh):
    in_specs = (
        P("blk", "head"),
        P("blk", None),
        P("blk", None),
        P("blk", "head"),
        P("blk", "head"),
        P("head", "blk"),
        P("head", "blk"),
        P(),
        P(),
        P(),
    )
    out_specs = (P("blk", "head"), P(("blk", "head"), None), P(("blk", "head"), None))
    return jax.shard_map(local, mesh=mesh, in_specs=in_specs, out_specs=out_specs, check_vma=False)
```

time: 81.9 us -> 74.9 us (0.915)
  the two profiles are of different devices: /device:TPU:33 before, /device:TPU:453 now
where the time goes in v3:
time: 74.9 us; the launch traced here: 74.3 us
  starting transfers between devices  44.9 us (60%)
  waiting for transfers between devices  20.4 us (27%)
  Pallas kernels  5.63 us (8%)
  local copies, waits for them, and re-layouts  2.56 us (3%)
  between operations  0.82 us (1%)
    ppermute x9, starting transfers between devices, moved(): return lax.ppermute(value, ('blk', 'head'), pairs)  29.5 us
    all_to_all x1, waiting for transfers between devices, local(): terms = lax.all_to_all(terms, 'head', 0, 0, axis_index_groups=[HEAD_ORDER])  17.3 us
    all_to_all x1, starting transfers between devices, local(): terms = lax.all_to_all(terms, 'head', 0, 0, axis_index_groups=[HEAD_ORDER])  15.4 us
    pallas_call x7, Pallas kernels, kernel_call(): pl.pallas_call(kernel, out_shape=out_shape, in_specs=[vmem] * len(arrays)...  3.37 us
    ppermute x9, waiting for transfers between devices, moved(): return lax.ppermute(value, ('blk', 'head'), pairs)  3.12 us
    unnamed x8, local copies, waits for them, and re-layouts  2.56 us
    pallas_call x1, Pallas kernels, prep(): pl.pallas_call(prep_kernel, out_shape=(jax.ShapeDtypeStruct((MSG, HD), BF...  2.26 us
  transfers between devices with their start and end apart: 10, of which 3 were waited for; matrix products, arithmetic and copies ran while one was open for 0% of the time, Pallas kernels for 3%

profile of v3, /device:TPU:453, one launch (start us, length us, event | category | flops | bytes accessed | tf_op | source)
XLA Modules:
  0.0 74.3 jit_solution(10195726366476479252)
XLA Ops:
  0.6 2.3 %prep.1 = (bf16[1088,128]{1,0:T(8,128)(2,1)}, bf16[256,256]{1,0:T(8,128)(2,1)}, f32[8,256]{1,0:T(8,128)}) custom-call(bf16[256,256]{1,0:T(8,128)(2,1)} %q_in.1, bf16[256,256]{1,0:T(8,128)(2,1)} %k_in.1, bf16[256,256]{1,0:T(8,128)(2,1)} %v_in.1, bf16[256,256]{1,0:T(8,128)(2,1)} %o_in.1, bf16[256,256]{1,0:T(8,128)(2,1)} %do_in.1, f32[2,256]{1,0:T(2,128)} %lse_in.1, ...), custom_call_target="tpu_custom_call" | custom-call | tf_op jit(solution)/shard_map/prep/pallas_call | solution.py:193
  2.9 3.8 %collective-permute-start.2 = (bf16[1088,128]{1,0:T(8,128)(2,1)}, bf16[1088,128]{1,0:T(8,128)(2,1)S(1)}, u32[]{:S(2)}, u32[]{:S(2)}) collective-permute-start(bf16[1088,128]{1,0:T(8,128)(2,1)} %get-tuple-element.17.msg.own), channel_id=1, source_target_pairs={{5,0},{4,1},{7,2},{6,3},{1,4},{0,5},{3,6},{2,7},{13,8},{12,9},{15,... | collective-permute-start | bytes 835592 | tf_op jit(solution)/shard_map/ppermute | solution.py:73
  6.7 2.1 %collective-permute-start.1 = (bf16[1088,128]{1,0:T(8,128)(2,1)}, bf16[1088,128]{1,0:T(8,128)(2,1)S(1)}, u32[]{:S(2)}, u32[]{:S(2)}) collective-permute-start(bf16[1088,128]{1,0:T(8,128)(2,1)} %get-tuple-element.17.msg.own), channel_id=1, source_target_pairs={{4,0},{5,1},{6,2},{7,3},{0,4},{1,5},{2,6},{3,7},{12,8},{13,9},{14,... | collective-permute-start | bytes 835592 | tf_op jit(solution)/shard_map/ppermute | solution.py:73
  8.8 5.4 %collective-permute-start.3 = (bf16[256,256]{1,0:T(8,128)(2,1)}, bf16[256,256]{1,0:T(8,128)(2,1)S(1)}, u32[]{:S(2)}, u32[]{:S(2)}) collective-permute-start(bf16[256,256]{1,0:T(8,128)(2,1)} %get-tuple-element.18.kv), channel_id=1, source_target_pairs={{466,0},{433,1},{464,2},{435,3},{454,4},{389,5},{452,6},{391,7},{4... | collective-permute-start | bytes 393224 | tf_op jit(solution)/shard_map/ppermute | solution.py:73
  14.1 2.5 %collective-permute-start.4 = (bf16[256,256]{1,0:T(8,128)(2,1)}, bf16[256,256]{1,0:T(8,128)(2,1)S(1)}, u32[]{:S(2)}, u32[]{:S(2)}) collective-permute-start(bf16[256,256]{1,0:T(8,128)(2,1)} %get-tuple-element.18.kv), channel_id=1, source_target_pairs={{498,0},{401,1},{496,2},{403,3},{486,4},{421,5},{484,6},{423,7},{5... | collective-permute-start | bytes 393224 | tf_op jit(solution)/shard_map/ppermute | solution.py:73
  16.7 1.9 %collective-permute-start = (bf16[1088,128]{1,0:T(8,128)(2,1)}, bf16[1088,128]{1,0:T(8,128)(2,1)S(1)}, u32[]{:S(2)}, u32[]{:S(2)}) collective-permute-start(bf16[1088,128]{1,0:T(8,128)(2,1)} %get-tuple-element.17.msg.own), channel_id=1, source_target_pairs={{1,0},{0,1},{3,2},{2,3},{5,4},{4,5},{7,6},{6,7},{9,8},{8,9},{11,10... | collective-permute-start | bytes 835592 | tf_op jit(solution)/shard_map/ppermute | solution.py:73
  18.6 0.9 %copy-done = bf16[1088,128]{1,0:T(8,128)(2,1)S(1)} copy-done((bf16[1088,128]{1,0:T(8,128)(2,1)S(1)}, bf16[1088,128]{1,0:T(8,128)(2,1)}, u32[]{:S(2)}) %copy-start) | copy-done | bytes 278552
  19.6 0.9 %copy-done.1 = bf16[256,256]{1,0:T(8,128)(2,1)S(1)} copy-done((bf16[256,256]{1,0:T(8,128)(2,1)S(1)}, bf16[256,256]{1,0:T(8,128)(2,1)}, u32[]{:S(2)}) %copy-start.1) | copy-done | bytes 131096
  20.5 0.7 copy-done.2
  21.2 0.7 own.1
  21.9 0.2 early.1
  22.1 0.2 late.1
  22.3 0.3 turn.1
  22.6 4.0 %collective-permute-start.5 = (bf16[1024,128]{1,0:T(8,128)(2,1)S(1)}, bf16[1024,128]{1,0:T(8,128)(2,1)S(1)}, u32[]{:S(2)}, u32[]{:S(2)}) collective-permute-start(bf16[1024,128]{1,0:T(8,128)(2,1)S(1)} %get-tuple-element.25), channel_id=1, source_target_pairs={{1,0},{0,1},{3,2},{2,3},{5,4},{4,5},{7,6},{6,7},{9,8},{8,9},{11,10... | collective-permute-start | bytes 786440 | tf_op jit(solution)/shard_map/ppermute | solution.py:73
  26.6 5.5 %collective-permute-start.7 = (bf16[256,256]{1,0:T(8,128)(2,1)S(1)}, bf16[256,256]{1,0:T(8,128)(2,1)S(1)}, u32[]{:S(2)}, u32[]{:S(2)}) collective-permute-start(bf16[256,256]{1,0:T(8,128)(2,1)S(1)} %get-tuple-element.27), channel_id=1, source_target_pairs={{0,466},{1,433},{2,464},{3,435},{4,454},{5,389},{6,452},{7,391},{8... | collective-permute-start | bytes 393224 | tf_op jit(solution)/shard_map/ppermute | solution.py:73
  32.2 1.9 %collective-permute-start.8 = (bf16[256,256]{1,0:T(8,128)(2,1)S(1)}, bf16[256,256]{1,0:T(8,128)(2,1)S(1)}, u32[]{:S(2)}, u32[]{:S(2)}) collective-permute-start(bf16[256,256]{1,0:T(8,128)(2,1)S(1)} %get-tuple-element.28), channel_id=1, source_target_pairs={{0,498},{1,401},{2,496},{3,403},{4,486},{5,421},{6,484},{7,423},{8... | collective-permute-start | bytes 393224 | tf_op jit(solution)/shard_map/ppermute | solution.py:73
  34.1 2.4 %collective-permute-start.6 = (bf16[512,128]{1,0:T(8,128)(2,1)S(1)}, bf16[512,128]{1,0:T(8,128)(2,1)S(1)}, u32[]{:S(2)}, u32[]{:S(2)}) collective-permute-start(bf16[512,128]{1,0:T(8,128)(2,1)S(1)} %add_convert_fusion), channel_id=1, source_target_pairs={{4,0},{5,1},{6,2},{7,3},{0,4},{1,5},{2,6},{3,7},{12,8},{13,9},{14,... | collective-permute-start | bytes 393224 | tf_op jit(solution)/shard_map/ppermute | solution.py:73
  36.5 0.6 collective-permute-done.7.far
  37.2 2.5 %collective-permute-done.8.near = bf16[256,256]{1,0:T(8,128)(2,1)S(1)} collective-permute-done((bf16[256,256]{1,0:T(8,128)(2,1)S(1)}, bf16[256,256]{1,0:T(8,128)(2,1)S(1)}, u32[]{:S(2)}, u32[]{:S(2)}) %collective-permute-start.8) | collective-permute-done | bytes 131104 | tf_op jit(solution)/shard_map/ppermute | solution.py:73
  39.6 0.7 terms.1
  40.4 15.4 %all-to-all-start = ((bf16[16,16,256]{2,1,0:T(8,128)(2,1)}), bf16[16,16,256]{2,1,0:T(8,128)(2,1)S(1)}, u32[]{:S(2)}, u32[]{:S(2)}) async-start(bf16[16,16,256]{2,1,0:T(8,128)(2,1)} %terms.1), calls=%async_computation | async-start | bytes 262144 | tf_op jit(solution)/shard_map/all_to_all | solution.py:481
  55.7 0.7 query.1
  56.4 17.3 %all-to-all-done.terms = bf16[16,16,256]{2,1,0:T(8,128)(2,1)S(1)} async-done(((bf16[16,16,256]{2,1,0:T(8,128)(2,1)}), bf16[16,16,256]{2,1,0:T(8,128)(2,1)S(1)}, u32[]{:S(2)}, u32[]{:S(2)}) %all-to-all-start) | async-done | bytes 131104 | tf_op jit(solution)/shard_map/all_to_all | solution.py:481
  73.7 0.6 key_value.1
  (13 shorter events, 0.1 us)
Async XLA Ops:
  2.9 19.0 %collective-permute-start.2 = (bf16[1088,128]{1,0:T(8,128)(2,1)}, bf16[1088,128]{1,0:T(8,128)(2,1)S(1)}, u32[]{:S(2)}, u32[]{:S(2)}) collective-permute-start(bf16[1088,128]{1,0:T(8,128)(2,1)} %get-tuple-element.17.msg.own), channel_id=1, source_target_pairs={{5,0},{4,1},{7,2},{6,3},{1,4},{0,5},{3,6},{2,7},{13,8},{12,9},{15,... | collective-permute-start | bytes 835592 | tf_op jit(solution)/shard_map/ppermute | solution.py:73
  6.7 15.2 %collective-permute-start.1 = (bf16[1088,128]{1,0:T(8,128)(2,1)}, bf16[1088,128]{1,0:T(8,128)(2,1)S(1)}, u32[]{:S(2)}, u32[]{:S(2)}) collective-permute-start(bf16[1088,128]{1,0:T(8,128)(2,1)} %get-tuple-element.17.msg.own), channel_id=1, source_target_pairs={{4,0},{5,1},{6,2},{7,3},{0,4},{1,5},{2,6},{3,7},{12,8},{13,9},{14,... | collective-permute-start | bytes 835592 | tf_op jit(solution)/shard_map/ppermute | solution.py:73
  8.8 13.1 %collective-permute-start.3 = (bf16[256,256]{1,0:T(8,128)(2,1)}, bf16[256,256]{1,0:T(8,128)(2,1)S(1)}, u32[]{:S(2)}, u32[]{:S(2)}) collective-permute-start(bf16[256,256]{1,0:T(8,128)(2,1)} %get-tuple-element.18.kv), channel_id=1, source_target_pairs={{466,0},{433,1},{464,2},{435,3},{454,4},{389,5},{452,6},{391,7},{4... | collective-permute-start | bytes 393224 | tf_op jit(solution)/shard_map/ppermute | solution.py:73
  14.1 8.0 %collective-permute-start.4 = (bf16[256,256]{1,0:T(8,128)(2,1)}, bf16[256,256]{1,0:T(8,128)(2,1)S(1)}, u32[]{:S(2)}, u32[]{:S(2)}) collective-permute-start(bf16[256,256]{1,0:T(8,128)(2,1)} %get-tuple-element.18.kv), channel_id=1, source_target_pairs={{498,0},{401,1},{496,2},{403,3},{486,4},{421,5},{484,6},{423,7},{5... | collective-permute-start | bytes 393224 | tf_op jit(solution)/shard_map/ppermute | solution.py:73
  16.7 5.4 %collective-permute-start = (bf16[1088,128]{1,0:T(8,128)(2,1)}, bf16[1088,128]{1,0:T(8,128)(2,1)S(1)}, u32[]{:S(2)}, u32[]{:S(2)}) collective-permute-start(bf16[1088,128]{1,0:T(8,128)(2,1)} %get-tuple-element.17.msg.own), channel_id=1, source_target_pairs={{1,0},{0,1},{3,2},{2,3},{5,4},{4,5},{7,6},{6,7},{9,8},{8,9},{11,10... | collective-permute-start | bytes 835592 | tf_op jit(solution)/shard_map/ppermute | solution.py:73
  18.6 1.0 %copy-start = (bf16[1088,128]{1,0:T(8,128)(2,1)S(1)}, bf16[1088,128]{1,0:T(8,128)(2,1)}, u32[]{:S(2)}) copy-start(bf16[1088,128]{1,0:T(8,128)(2,1)} %get-tuple-element.17.msg.own) | copy-start | bytes 835588
  19.6 0.9 %copy-start.1 = (bf16[256,256]{1,0:T(8,128)(2,1)S(1)}, bf16[256,256]{1,0:T(8,128)(2,1)}, u32[]{:S(2)}) copy-start(bf16[256,256]{1,0:T(8,128)(2,1)} %get-tuple-element.18.kv) | copy-start | bytes 393220
  20.5 0.7 copy-start.2
  21.2 0.7 copy-start.3
  22.6 11.5 %collective-permute-start.5 = (bf16[1024,128]{1,0:T(8,128)(2,1)S(1)}, bf16[1024,128]{1,0:T(8,128)(2,1)S(1)}, u32[]{:S(2)}, u32[]{:S(2)}) collective-permute-start(bf16[1024,128]{1,0:T(8,128)(2,1)S(1)} %get-tuple-element.25), channel_id=1, source_target_pairs={{1,0},{0,1},{3,2},{2,3},{5,4},{4,5},{7,6},{6,7},{9,8},{8,9},{11,10... | collective-permute-start | bytes 786440 | tf_op jit(solution)/shard_map/ppermute | solution.py:73
  26.6 10.5 %collective-permute-start.7 = (bf16[256,256]{1,0:T(8,128)(2,1)S(1)}, bf16[256,256]{1,0:T(8,128)(2,1)S(1)}, u32[]{:S(2)}, u32[]{:S(2)}) collective-permute-start(bf16[256,256]{1,0:T(8,128)(2,1)S(1)} %get-tuple-element.27), channel_id=1, source_target_pairs={{0,466},{1,433},{2,464},{3,435},{4,454},{5,389},{6,452},{7,391},{8... | collective-permute-start | bytes 393224 | tf_op jit(solution)/shard_map/ppermute | solution.py:73
  32.2 7.5 %collective-permute-start.8 = (bf16[256,256]{1,0:T(8,128)(2,1)S(1)}, bf16[256,256]{1,0:T(8,128)(2,1)S(1)}, u32[]{:S(2)}, u32[]{:S(2)}) collective-permute-start(bf16[256,256]{1,0:T(8,128)(2,1)S(1)} %get-tuple-element.28), channel_id=1, source_target_pairs={{0,498},{1,401},{2,496},{3,403},{4,486},{5,421},{6,484},{7,423},{8... | collective-permute-start | bytes 393224 | tf_op jit(solution)/shard_map/ppermute | solution.py:73
  34.1 21.6 %collective-permute-start.6 = (bf16[512,128]{1,0:T(8,128)(2,1)S(1)}, bf16[512,128]{1,0:T(8,128)(2,1)S(1)}, u32[]{:S(2)}, u32[]{:S(2)}) collective-permute-start(bf16[512,128]{1,0:T(8,128)(2,1)S(1)} %add_convert_fusion), channel_id=1, source_target_pairs={{4,0},{5,1},{6,2},{7,3},{0,4},{1,5},{2,6},{3,7},{12,8},{13,9},{14,... | collective-permute-start | bytes 393224 | tf_op jit(solution)/shard_map/ppermute | solution.py:73
  40.4 33.4 %all-to-all-start = ((bf16[16,16,256]{2,1,0:T(8,128)(2,1)}), bf16[16,16,256]{2,1,0:T(8,128)(2,1)S(1)}, u32[]{:S(2)}, u32[]{:S(2)}) async-start(bf16[16,16,256]{2,1,0:T(8,128)(2,1)} %terms.1), calls=%async_computation | async-start | bytes 262144 | tf_op jit(solution)/shard_map/all_to_all | solution.py:481

commit v4 on v3

--- a/solution.py
+++ b/solution.py
@@ -21,7 +21,6 @@
 TURN_FLOPS = 1 << 27
 QUERY_FLOPS = 1 << 34
 BF16 = jnp.bfloat16
-PREP_VMEM_LIMIT = 62 * 1024 * 1024
 VMEM_LIMIT = 24 * 1024 * 1024
 
 NEAR = ((1, 7), (2, 6))
@@ -202,8 +201,8 @@
         scratch_shapes=held
         + [pltpu.VMEM((16, ROWS), F32), pltpu.SemaphoreType.DMA((10,))],
         name="prep",
-        compiler_params=pltpu.CompilerParams(vmem_limit_bytes=PREP_VMEM_LIMIT),
-    )(*arrays)
+        compiler_params=pltpu.CompilerParams(vmem_limit_bytes=VMEM_LIMIT),
+    )(*[pltpu.with_memory_space_constraint(array, pltpu.HBM) for array in arrays])
 
 
 def both(row):

time: 74.9 us -> 72.6 us (0.969)
  the two profiles are of different devices: /device:TPU:453 before, /device:TPU:1 now
where the time goes in v4:
time: 72.6 us; the launch traced here: 72.1 us
  starting transfers between devices  58.5 us (81%)
  waiting for transfers between devices  7.83 us (11%)
  Pallas kernels  4.97 us (7%)
  between operations  0.8 us (1%)
    ppermute x9, starting transfers between devices, moved(): return lax.ppermute(value, ('blk', 'head'), pairs)  38.4 us
    all_to_all x1, starting transfers between devices, local(): terms = lax.all_to_all(terms, 'head', 0, 0, axis_index_groups=[HEAD_ORDER])  20.1 us
    all_to_all x1, waiting for transfers between devices, local(): terms = lax.all_to_all(terms, 'head', 0, 0, axis_index_groups=[HEAD_ORDER])  4.52 us
    pallas_call x7, Pallas kernels, kernel_call(): pl.pallas_call(kernel, out_shape=out_shape, in_specs=[vmem] * len(arrays)...  3.38 us
    ppermute x9, waiting for transfers between devices, moved(): return lax.ppermute(value, ('blk', 'head'), pairs)  3.31 us
    pallas_call x1, Pallas kernels, prep(): pl.pallas_call(prep_kernel, out_shape=(jax.ShapeDtypeStruct((MSG, HD), BF...  1.59 us
  transfers between devices with their start and end apart: 10, of which 2 were waited for; matrix products, arithmetic and copies ran while one was open for 0% of the time, Pallas kernels for 3%

profile of v4, /device:TPU:1, one launch (start us, length us, event | category | flops | bytes accessed | tf_op | source)
XLA Modules:
  0.0 72.1 jit_solution(11103405882227969032)
XLA Ops:
  0.6 1.6 %prep.1 = (bf16[1088,128]{1,0:T(8,128)(2,1)S(1)}, bf16[256,256]{1,0:T(8,128)(2,1)S(1)}, f32[8,256]{1,0:T(8,128)S(1)}) custom-call(bf16[256,256]{1,0:T(8,128)(2,1)} %q_in.1, bf16[256,256]{1,0:T(8,128)(2,1)} %k_in.1, bf16[256,256]{1,0:T(8,128)(2,1)} %v_in.1, bf16[256,256]{1,0:T(8,128)(2,1)} %o_in.1, bf16[256,256]{1,0:T(8,128)(2,1)} %do_in.1, f32[2,256]{1,0:T(2,128)} %lse_in.1, ...), custom_call_target="tpu_custom_call" | custom-call | tf_op jit(solution)/shard_map/prep/pallas_call | solution.py:192
  2.2 4.6 %collective-permute-start.2 = (bf16[1088,128]{1,0:T(8,128)(2,1)S(1)}, bf16[1088,128]{1,0:T(8,128)(2,1)S(1)}, u32[]{:S(2)}, u32[]{:S(2)}) collective-permute-start(bf16[1088,128]{1,0:T(8,128)(2,1)S(1)} %get-tuple-element.17.msg.own), channel_id=1, source_target_pairs={{5,0},{4,1},{7,2},{6,3},{1,4},{0,5},{3,6},{2,7},{13,8},{12,9},{15,... | collective-permute-start | bytes 835592 | tf_op jit(solution)/shard_map/ppermute | solution.py:72
  6.8 7.5 %collective-permute-start.1 = (bf16[1088,128]{1,0:T(8,128)(2,1)S(1)}, bf16[1088,128]{1,0:T(8,128)(2,1)S(1)}, u32[]{:S(2)}, u32[]{:S(2)}) collective-permute-start(bf16[1088,128]{1,0:T(8,128)(2,1)S(1)} %get-tuple-element.17.msg.own), channel_id=1, source_target_pairs={{4,0},{5,1},{6,2},{7,3},{0,4},{1,5},{2,6},{3,7},{12,8},{13,9},{14,... | collective-permute-start | bytes 835592 | tf_op jit(solution)/shard_map/ppermute | solution.py:72
  14.3 6.6 %collective-permute-start.3 = (bf16[256,256]{1,0:T(8,128)(2,1)S(1)}, bf16[256,256]{1,0:T(8,128)(2,1)S(1)}, u32[]{:S(2)}, u32[]{:S(2)}) collective-permute-start(bf16[256,256]{1,0:T(8,128)(2,1)S(1)} %get-tuple-element.18.kv), channel_id=1, source_target_pairs={{466,0},{433,1},{464,2},{435,3},{454,4},{389,5},{452,6},{391,7},{4... | collective-permute-start | bytes 393224 | tf_op jit(solution)/shard_map/ppermute | solution.py:72
  20.9 3.6 %collective-permute-start.4 = (bf16[256,256]{1,0:T(8,128)(2,1)S(1)}, bf16[256,256]{1,0:T(8,128)(2,1)S(1)}, u32[]{:S(2)}, u32[]{:S(2)}) collective-permute-start(bf16[256,256]{1,0:T(8,128)(2,1)S(1)} %get-tuple-element.18.kv), channel_id=1, source_target_pairs={{498,0},{401,1},{496,2},{403,3},{486,4},{421,5},{484,6},{423,7},{5... | collective-permute-start | bytes 393224 | tf_op jit(solution)/shard_map/ppermute | solution.py:72
  24.5 1.9 %collective-permute-start = (bf16[1088,128]{1,0:T(8,128)(2,1)S(1)}, bf16[1088,128]{1,0:T(8,128)(2,1)S(1)}, u32[]{:S(2)}, u32[]{:S(2)}) collective-permute-start(bf16[1088,128]{1,0:T(8,128)(2,1)S(1)} %get-tuple-element.17.msg.own), channel_id=1, source_target_pairs={{1,0},{0,1},{3,2},{2,3},{5,4},{4,5},{7,6},{6,7},{9,8},{8,9},{11,10... | collective-permute-start | bytes 835592 | tf_op jit(solution)/shard_map/ppermute | solution.py:72
  26.4 0.7 own.1
  27.1 0.0 collective-permute-done.3.kv_far
  27.1 0.0 collective-permute-done.1.y
  27.1 0.2 early.1
  27.3 3.3 %collective-permute-done.4.kv_near = bf16[256,256]{1,0:T(8,128)(2,1)S(1)} collective-permute-done((bf16[256,256]{1,0:T(8,128)(2,1)S(1)}, bf16[256,256]{1,0:T(8,128)(2,1)S(1)}, u32[]{:S(2)}, u32[]{:S(2)}) %collective-permute-start.4) | collective-permute-done | bytes 131104 | tf_op jit(solution)/shard_map/ppermute | solution.py:72
  30.6 0.2 late.1
  30.8 0.3 turn.1
  31.1 2.3 %collective-permute-start.5 = (bf16[1024,128]{1,0:T(8,128)(2,1)S(1)}, bf16[1024,128]{1,0:T(8,128)(2,1)S(1)}, u32[]{:S(2)}, u32[]{:S(2)}) collective-permute-start(bf16[1024,128]{1,0:T(8,128)(2,1)S(1)} %get-tuple-element.25), channel_id=1, source_target_pairs={{1,0},{0,1},{3,2},{2,3},{5,4},{4,5},{7,6},{6,7},{9,8},{8,9},{11,10... | collective-permute-start | bytes 786440 | tf_op jit(solution)/shard_map/ppermute | solution.py:72
  33.5 5.0 %collective-permute-start.7 = (bf16[256,256]{1,0:T(8,128)(2,1)S(1)}, bf16[256,256]{1,0:T(8,128)(2,1)S(1)}, u32[]{:S(2)}, u32[]{:S(2)}) collective-permute-start(bf16[256,256]{1,0:T(8,128)(2,1)S(1)} %get-tuple-element.27), channel_id=1, source_target_pairs={{0,466},{1,433},{2,464},{3,435},{4,454},{5,389},{6,452},{7,391},{8... | collective-permute-start | bytes 393224 | tf_op jit(solution)/shard_map/ppermute | solution.py:72
  38.5 3.8 %collective-permute-start.8 = (bf16[256,256]{1,0:T(8,128)(2,1)S(1)}, bf16[256,256]{1,0:T(8,128)(2,1)S(1)}, u32[]{:S(2)}, u32[]{:S(2)}) collective-permute-start(bf16[256,256]{1,0:T(8,128)(2,1)S(1)} %get-tuple-element.28), channel_id=1, source_target_pairs={{0,498},{1,401},{2,496},{3,403},{4,486},{5,421},{6,484},{7,423},{8... | collective-permute-start | bytes 393224 | tf_op jit(solution)/shard_map/ppermute | solution.py:72
  42.3 0.0 collective-permute-done.5.dq_core
  42.4 3.1 %collective-permute-start.6 = (bf16[512,128]{1,0:T(8,128)(2,1)S(1)}, bf16[512,128]{1,0:T(8,128)(2,1)S(1)}, u32[]{:S(2)}, u32[]{:S(2)}) collective-permute-start(bf16[512,128]{1,0:T(8,128)(2,1)S(1)} %add_convert_fusion), channel_id=1, source_target_pairs={{4,0},{5,1},{6,2},{7,3},{0,4},{1,5},{2,6},{3,7},{12,8},{13,9},{14,... | collective-permute-start | bytes 393224 | tf_op jit(solution)/shard_map/ppermute | solution.py:72
  45.5 0.0 collective-permute-done.7.far
  45.5 0.7 terms.1
  46.2 20.1 %all-to-all-start = ((bf16[16,16,256]{2,1,0:T(8,128)(2,1)}), bf16[16,16,256]{2,1,0:T(8,128)(2,1)S(1)}, u32[]{:S(2)}, u32[]{:S(2)}) async-start(bf16[16,16,256]{2,1,0:T(8,128)(2,1)} %terms.1), calls=%async_computation | async-start | bytes 262144 | tf_op jit(solution)/shard_map/all_to_all | solution.py:480
  66.3 0.7 query.1
  67.0 4.5 %all-to-all-done.terms = bf16[16,16,256]{2,1,0:T(8,128)(2,1)S(1)} async-done(((bf16[16,16,256]{2,1,0:T(8,128)(2,1)}), bf16[16,16,256]{2,1,0:T(8,128)(2,1)S(1)}, u32[]{:S(2)}, u32[]{:S(2)}) %all-to-all-start) | async-done | bytes 131104 | tf_op jit(solution)/shard_map/all_to_all | solution.py:480
  71.5 0.6 key_value.1
  (5 shorter events, 0.0 us)
Async XLA Ops:
  2.2 24.9 %collective-permute-start.2 = (bf16[1088,128]{1,0:T(8,128)(2,1)S(1)}, bf16[1088,128]{1,0:T(8,128)(2,1)S(1)}, u32[]{:S(2)}, u32[]{:S(2)}) collective-permute-start(bf16[1088,128]{1,0:T(8,128)(2,1)S(1)} %get-tuple-element.17.msg.own), channel_id=1, source_target_pairs={{5,0},{4,1},{7,2},{6,3},{1,4},{0,5},{3,6},{2,7},{13,8},{12,9},{15,... | collective-permute-start | bytes 835592 | tf_op jit(solution)/shard_map/ppermute | solution.py:72
  6.8 20.3 %collective-permute-start.1 = (bf16[1088,128]{1,0:T(8,128)(2,1)S(1)}, bf16[1088,128]{1,0:T(8,128)(2,1)S(1)}, u32[]{:S(2)}, u32[]{:S(2)}) collective-permute-start(bf16[1088,128]{1,0:T(8,128)(2,1)S(1)} %get-tuple-element.17.msg.own), channel_id=1, source_target_pairs={{4,0},{5,1},{6,2},{7,3},{0,4},{1,5},{2,6},{3,7},{12,8},{13,9},{14,... | collective-permute-start | bytes 835592 | tf_op jit(solution)/shard_map/ppermute | solution.py:72
  14.3 12.8 %collective-permute-start.3 = (bf16[256,256]{1,0:T(8,128)(2,1)S(1)}, bf16[256,256]{1,0:T(8,128)(2,1)S(1)}, u32[]{:S(2)}, u32[]{:S(2)}) collective-permute-start(bf16[256,256]{1,0:T(8,128)(2,1)S(1)} %get-tuple-element.18.kv), channel_id=1, source_target_pairs={{466,0},{433,1},{464,2},{435,3},{454,4},{389,5},{452,6},{391,7},{4... | collective-permute-start | bytes 393224 | tf_op jit(solution)/shard_map/ppermute | solution.py:72
  20.9 9.7 %collective-permute-start.4 = (bf16[256,256]{1,0:T(8,128)(2,1)S(1)}, bf16[256,256]{1,0:T(8,128)(2,1)S(1)}, u32[]{:S(2)}, u32[]{:S(2)}) collective-permute-start(bf16[256,256]{1,0:T(8,128)(2,1)S(1)} %get-tuple-element.18.kv), channel_id=1, source_target_pairs={{498,0},{401,1},{496,2},{403,3},{486,4},{421,5},{484,6},{423,7},{5... | collective-permute-start | bytes 393224 | tf_op jit(solution)/shard_map/ppermute | solution.py:72
  24.5 6.1 %collective-permute-start = (bf16[1088,128]{1,0:T(8,128)(2,1)S(1)}, bf16[1088,128]{1,0:T(8,128)(2,1)S(1)}, u32[]{:S(2)}, u32[]{:S(2)}) collective-permute-start(bf16[1088,128]{1,0:T(8,128)(2,1)S(1)} %get-tuple-element.17.msg.own), channel_id=1, source_target_pairs={{1,0},{0,1},{3,2},{2,3},{5,4},{4,5},{7,6},{6,7},{9,8},{8,9},{11,10... | collective-permute-start | bytes 835592 | tf_op jit(solution)/shard_map/ppermute | solution.py:72
  31.1 11.2 %collective-permute-start.5 = (bf16[1024,128]{1,0:T(8,128)(2,1)S(1)}, bf16[1024,128]{1,0:T(8,128)(2,1)S(1)}, u32[]{:S(2)}, u32[]{:S(2)}) collective-permute-start(bf16[1024,128]{1,0:T(8,128)(2,1)S(1)} %get-tuple-element.25), channel_id=1, source_target_pairs={{1,0},{0,1},{3,2},{2,3},{5,4},{4,5},{7,6},{6,7},{9,8},{8,9},{11,10... | collective-permute-start | bytes 786440 | tf_op jit(solution)/shard_map/ppermute | solution.py:72
  33.5 12.0 %collective-permute-start.7 = (bf16[256,256]{1,0:T(8,128)(2,1)S(1)}, bf16[256,256]{1,0:T(8,128)(2,1)S(1)}, u32[]{:S(2)}, u32[]{:S(2)}) collective-permute-start(bf16[256,256]{1,0:T(8,128)(2,1)S(1)} %get-tuple-element.27), channel_id=1, source_target_pairs={{0,466},{1,433},{2,464},{3,435},{4,454},{5,389},{6,452},{7,391},{8... | collective-permute-start | bytes 393224 | tf_op jit(solution)/shard_map/ppermute | solution.py:72
  38.5 7.0 %collective-permute-start.8 = (bf16[256,256]{1,0:T(8,128)(2,1)S(1)}, bf16[256,256]{1,0:T(8,128)(2,1)S(1)}, u32[]{:S(2)}, u32[]{:S(2)}) collective-permute-start(bf16[256,256]{1,0:T(8,128)(2,1)S(1)} %get-tuple-element.28), channel_id=1, source_target_pairs={{0,498},{1,401},{2,496},{3,403},{4,486},{5,421},{6,484},{7,423},{8... | collective-permute-start | bytes 393224 | tf_op jit(solution)/shard_map/ppermute | solution.py:72
  42.4 23.9 %collective-permute-start.6 = (bf16[512,128]{1,0:T(8,128)(2,1)S(1)}, bf16[512,128]{1,0:T(8,128)(2,1)S(1)}, u32[]{:S(2)}, u32[]{:S(2)}) collective-permute-start(bf16[512,128]{1,0:T(8,128)(2,1)S(1)} %add_convert_fusion), channel_id=1, source_target_pairs={{4,0},{5,1},{6,2},{7,3},{0,4},{1,5},{2,6},{3,7},{12,8},{13,9},{14,... | collective-permute-start | bytes 393224 | tf_op jit(solution)/shard_map/ppermute | solution.py:72
  46.2 25.3 %all-to-all-start = ((bf16[16,16,256]{2,1,0:T(8,128)(2,1)}), bf16[16,16,256]{2,1,0:T(8,128)(2,1)S(1)}, u32[]{:S(2)}, u32[]{:S(2)}) async-start(bf16[16,16,256]{2,1,0:T(8,128)(2,1)} %terms.1), calls=%async_computation | async-start | bytes 262144 | tf_op jit(solution)/shard_map/all_to_all | solution.py:480

commit v5 on v4

--- a/solution.py
+++ b/solution.py
@@ -270,7 +270,7 @@
     )
 
 
-def early_kernel(own, y, cross, kv_far, aux, dq_own, far, dq):
+def early_kernel(own, y, kv_far, aux, dq_own, far, dq):
     _, seen = block_place(FAR, aux[0:1, :])
 
     @pl.when(jnp.logical_not(seen))
@@ -284,29 +284,28 @@
         def put(n, query_sum):
             dq[n] = dq_own[0] + query_sum if n == 0 else query_sum
 
-        key_sum, value_sum = earlier_sums(FAR, (own, y, cross), kv_far, aux, put)
+        key_sum, value_sum = earlier_sums(FAR, (own, y), kv_far, aux, put)
         far[:, :HD] = key_sum
         far[:, HD:] = value_sum
 
 
-def late_kernel(
-    own, core, y, cross, kv_far, kv_near, aux, far_in, dq_in, far, near, dq
-):
+def late_kernel(own, y, kv_near, kv_far, other, aux, far_in, dq_in, far, near, dq):
+    core, cross = other.at[:MSG, :], other.at[MSG:, :]
     _, far_seen = block_place(FAR, aux[0:1, :])
     _, near_seen = block_place(NEAR, aux[0:1, :])
 
     @pl.when(jnp.logical_not(near_seen))
     def _():
-        dq[:3] = dq_in[...]
-        dq[3] = jnp.zeros_like(dq[3])
+        dq[:2] = dq_in[...]
+        dq[2:] = jnp.zeros_like(dq[2:])
         near[...] = jnp.zeros_like(near)
 
     @pl.when(near_seen)
     def _():
         def put(n, query_sum):
-            dq[n] = dq_in[n] + query_sum if n < 3 else query_sum
-
-        key_sum, value_sum = earlier_sums(NEAR, (own, y, cross, core), kv_near, aux, put)
+            dq[n] = dq_in[n] + query_sum if n < 2 else query_sum
+
+        key_sum, value_sum = earlier_sums(NEAR, (own, y, core, cross), kv_near, aux, put)
         near[:, :HD] = key_sum.astype(BF16)
         near[:, HD:] = value_sum.astype(BF16)
 
@@ -317,9 +316,9 @@
     @pl.when(far_seen)
     def _():
         def put(n, query_sum):
-            dq[3] += query_sum
-
-        key_sum, value_sum = earlier_sums(FAR, (core,), kv_far, aux, put)
+            dq[2 + n] += query_sum
+
+        key_sum, value_sum = earlier_sums(FAR, (core, cross), kv_far, aux, put)
         far[:, :HD] = (far_in[:, :HD] + key_sum).astype(BF16)
         far[:, HD:] = (far_in[:, HD:] + value_sum).astype(BF16)
 
@@ -360,7 +359,7 @@
 
 
 def turn_kernel(dq, send, keep):
-    for n, (kept, sent) in enumerate(((0, 3), (1, 2))):
+    for n, (kept, sent) in enumerate(((0, 2), (1, 3))):
         at = slice(2 * n * ROWS, 2 * (n + 1) * ROWS)
         keep[at, :] = dq[kept].T
         send[at, :] = dq[sent].T.astype(BF16)
@@ -405,7 +404,6 @@
 ):
     to_core = pairs_from(other_core)
     to_y = pairs_from(other_y)
-    to_cross = pairs_from(lambda index: other_y(other_core(index)))
     back_near = pairs_from(functools.partial(back_source, NEAR))
     back_far = pairs_from(functools.partial(back_source, FAR))
     msg, kv, aux = prep(
@@ -420,11 +418,10 @@
         weight_index,
         penalty_weights,
     )
-    msg_core = moved(msg, to_core)
     kv_near = moved(kv, back_near)
     msg_y = moved(msg, to_y)
     kv_far = moved(kv, back_far)
-    msg_cross = moved(msg, to_cross)
+    msg_other = moved(jnp.concatenate([msg, msg_y], axis=0), to_core)
     sums = functools.partial(jax.ShapeDtypeStruct, dtype=F32)
     pair = jax.ShapeDtypeStruct((ROWS, 2 * HD), BF16)
     dq_own, dkv_own = kernel_call(
@@ -439,11 +436,10 @@
     dkv_far, dq = kernel_call(
         early_kernel,
         "early",
-        (sums((ROWS, 2 * HD)), sums((3, HD, 2 * ROWS))),
+        (sums((ROWS, 2 * HD)), sums((2, HD, 2 * ROWS))),
         EARLY_FLOPS,
         msg,
         msg_y,
-        msg_cross,
         kv_far,
         aux,
         dq_own,
@@ -454,11 +450,10 @@
         (pair, pair, sums((4, HD, 2 * ROWS))),
         LATE_FLOPS,
         msg,
-        msg_core,
         msg_y,
-        msg_cross,
+        kv_near,
         kv_far,
-        kv_near,
+        msg_other,
         aux,
         dkv_far,
         dq,

time: 72.6 us -> 70.8 us (0.975)
  the two profiles are of different devices: /device:TPU:1 before, /device:TPU:35 now
where the time goes in v5:
time: 70.8 us; the launch traced here: 70.4 us
  starting transfers between devices  55.7 us (79%)
  waiting for transfers between devices  8.87 us (13%)
  Pallas kernels  4.95 us (7%)
  between operations  0.8 us (1%)
    ppermute x8, starting transfers between devices, moved(): return lax.ppermute(value, ('blk', 'head'), pairs)  36.3 us
    all_to_all x1, starting transfers between devices, local(): terms = lax.all_to_all(terms, 'head', 0, 0, axis_index_groups=[HEAD_ORDER])  19.5 us
    all_to_all x1, waiting for transfers between devices, local(): terms = lax.all_to_all(terms, 'head', 0, 0, axis_index_groups=[HEAD_ORDER])  7.13 us
    pallas_call x7, Pallas kernels, kernel_call(): pl.pallas_call(kernel, out_shape=out_shape, in_specs=[vmem] * len(arrays)...  3.37 us
    ppermute x8, waiting for transfers between devices, moved(): return lax.ppermute(value, ('blk', 'head'), pairs)  1.74 us
    pallas_call x1, Pallas kernels, prep(): pl.pallas_call(prep_kernel, out_shape=(jax.ShapeDtypeStruct((MSG, HD), BF...  1.59 us
  transfers between devices with their start and end apart: 9, of which 3 were waited for; matrix products, arithmetic and copies ran while one was open for 0% of the time, Pallas kernels for 3%

profile of v5, /device:TPU:35, one launch (start us, length us, event | category | flops | bytes accessed | tf_op | source)
XLA Modules:
  0.0 70.4 jit_solution(12648141744510221352)
XLA Ops:
  0.6 1.6 %prep.1 = (bf16[1088,128]{1,0:T(8,128)(2,1)S(1)}, bf16[256,256]{1,0:T(8,128)(2,1)S(1)}, f32[8,256]{1,0:T(8,128)S(1)}) custom-call(bf16[256,256]{1,0:T(8,128)(2,1)} %q_in.1, bf16[256,256]{1,0:T(8,128)(2,1)} %k_in.1, bf16[256,256]{1,0:T(8,128)(2,1)} %v_in.1, bf16[256,256]{1,0:T(8,128)(2,1)} %o_in.1, bf16[256,256]{1,0:T(8,128)(2,1)} %do_in.1, f32[2,256]{1,0:T(2,128)} %lse_in.1, ...), custom_call_target="tpu_custom_call" | custom-call | tf_op jit(solution)/shard_map/prep/pallas_call | solution.py:192
  2.2 3.2 %collective-permute-start = (bf16[1088,128]{1,0:T(8,128)(2,1)S(1)}, bf16[1088,128]{1,0:T(8,128)(2,1)S(1)}, u32[]{:S(2)}, u32[]{:S(2)}) collective-permute-start(bf16[1088,128]{1,0:T(8,128)(2,1)S(1)} %get-tuple-element.17.msg.own), channel_id=1, source_target_pairs={{4,0},{5,1},{6,2},{7,3},{0,4},{1,5},{2,6},{3,7},{12,8},{13,9},{14,... | collective-permute-start | bytes 835592 | tf_op jit(solution)/shard_map/ppermute | solution.py:72
  5.4 11.1 %collective-permute-start.2 = (bf16[256,256]{1,0:T(8,128)(2,1)S(1)}, bf16[256,256]{1,0:T(8,128)(2,1)S(1)}, u32[]{:S(2)}, u32[]{:S(2)}) collective-permute-start(bf16[256,256]{1,0:T(8,128)(2,1)S(1)} %get-tuple-element.18.kv), channel_id=1, source_target_pairs={{466,0},{433,1},{464,2},{435,3},{454,4},{389,5},{452,6},{391,7},{4... | collective-permute-start | bytes 393224 | tf_op jit(solution)/shard_map/ppermute | solution.py:72
  16.6 3.6 %collective-permute-start.1 = (bf16[256,256]{1,0:T(8,128)(2,1)S(1)}, bf16[256,256]{1,0:T(8,128)(2,1)S(1)}, u32[]{:S(2)}, u32[]{:S(2)}) collective-permute-start(bf16[256,256]{1,0:T(8,128)(2,1)S(1)} %get-tuple-element.18.kv), channel_id=1, source_target_pairs={{498,0},{401,1},{496,2},{403,3},{486,4},{421,5},{484,6},{423,7},{5... | collective-permute-start | bytes 393224 | tf_op jit(solution)/shard_map/ppermute | solution.py:72
  20.1 0.7 own.1
  20.8 0.0 collective-permute-done.y
  20.9 1.9 %collective-permute-start.3 = (bf16[2176,128]{1,0:T(8,128)(2,1)S(1)}, bf16[2176,128]{1,0:T(8,128)(2,1)S(1)}, u32[]{:S(2)}, u32[]{:S(2)}) collective-permute-start(bf16[2176,128]{1,0:T(8,128)(2,1)S(1)} %pad_maximum_fusion), channel_id=1, source_target_pairs={{1,0},{0,1},{3,2},{2,3},{5,4},{4,5},{7,6},{6,7},{9,8},{8,9},{11,10... | collective-permute-start | bytes 1671176 | tf_op jit(solution)/shard_map/ppermute | solution.py:72
  22.8 0.0 collective-permute-done.2.kv_far
  22.8 0.2 early.1
  23.0 0.2 collective-permute-done.1.kv_near
  23.2 1.5 %collective-permute-done.3.other = bf16[2176,128]{1,0:T(8,128)(2,1)S(1)} collective-permute-done((bf16[2176,128]{1,0:T(8,128)(2,1)S(1)}, bf16[2176,128]{1,0:T(8,128)(2,1)S(1)}, u32[]{:S(2)}, u32[]{:S(2)}) %collective-permute-start.3) | collective-permute-done | bytes 557088 | tf_op jit(solution)/shard_map/ppermute | solution.py:72
  24.7 0.2 late.1
  24.9 0.3 turn.1
  25.2 4.6 %collective-permute-start.4 = (bf16[1024,128]{1,0:T(8,128)(2,1)S(1)}, bf16[1024,128]{1,0:T(8,128)(2,1)S(1)}, u32[]{:S(2)}, u32[]{:S(2)}) collective-permute-start(bf16[1024,128]{1,0:T(8,128)(2,1)S(1)} %get-tuple-element.25), channel_id=1, source_target_pairs={{1,0},{0,1},{3,2},{2,3},{5,4},{4,5},{7,6},{6,7},{9,8},{8,9},{11,10... | collective-permute-start | bytes 786440 | tf_op jit(solution)/shard_map/ppermute | solution.py:72
  29.8 5.1 %collective-permute-start.6 = (bf16[256,256]{1,0:T(8,128)(2,1)S(1)}, bf16[256,256]{1,0:T(8,128)(2,1)S(1)}, u32[]{:S(2)}, u32[]{:S(2)}) collective-permute-start(bf16[256,256]{1,0:T(8,128)(2,1)S(1)} %get-tuple-element.27), channel_id=1, source_target_pairs={{0,466},{1,433},{2,464},{3,435},{4,454},{5,389},{6,452},{7,391},{8... | collective-permute-start | bytes 393224 | tf_op jit(solution)/shard_map/ppermute | solution.py:72
  34.9 4.8 %collective-permute-start.7 = (bf16[256,256]{1,0:T(8,128)(2,1)S(1)}, bf16[256,256]{1,0:T(8,128)(2,1)S(1)}, u32[]{:S(2)}, u32[]{:S(2)}) collective-permute-start(bf16[256,256]{1,0:T(8,128)(2,1)S(1)} %get-tuple-element.28), channel_id=1, source_target_pairs={{0,498},{1,401},{2,496},{3,403},{4,486},{5,421},{6,484},{7,423},{8... | collective-permute-start | bytes 393224 | tf_op jit(solution)/shard_map/ppermute | solution.py:72
  39.8 0.0 collective-permute-done.4.dq_core
  39.8 1.9 %collective-permute-start.5 = (bf16[512,128]{1,0:T(8,128)(2,1)S(1)}, bf16[512,128]{1,0:T(8,128)(2,1)S(1)}, u32[]{:S(2)}, u32[]{:S(2)}) collective-permute-start(bf16[512,128]{1,0:T(8,128)(2,1)S(1)} %add_convert_fusion), channel_id=1, source_target_pairs={{4,0},{5,1},{6,2},{7,3},{0,4},{1,5},{2,6},{3,7},{12,8},{13,9},{14,... | collective-permute-start | bytes 393224 | tf_op jit(solution)/shard_map/ppermute | solution.py:72
  41.7 0.0 collective-permute-done.6.far
  41.8 0.7 %terms.1 = bf16[16,16,256]{2,1,0:T(8,128)(2,1)} custom-call(f32[256,256]{1,0:T(8,128)S(1)} %get-tuple-element.26.own, bf16[256,256]{1,0:T(8,128)(2,1)S(1)} %collective-permute-done.6.far, bf16[256,256]{1,0:T(8,128)(2,1)S(1)} %collective-permute-done.7.near), custom_call_target="tpu_custom_call" | custom-call | bytes 1048576 | tf_op jit(solution)/shard_map/terms/pallas_call | solution.py:328
  42.5 19.5 %all-to-all-start = ((bf16[16,16,256]{2,1,0:T(8,128)(2,1)}), bf16[16,16,256]{2,1,0:T(8,128)(2,1)S(1)}, u32[]{:S(2)}, u32[]{:S(2)}) async-start(bf16[16,16,256]{2,1,0:T(8,128)(2,1)} %terms.1), calls=%async_computation | async-start | bytes 262144 | tf_op jit(solution)/shard_map/all_to_all | solution.py:475
  61.9 0.7 %query.1 = bf16[256,256]{1,0:T(8,128)(2,1)} custom-call(f32[1024,128]{1,0:T(8,128)S(1)} %get-tuple-element.24.dq_keep, bf16[1024,128]{1,0:T(8,128)(2,1)S(1)} %collective-permute-done.4.dq_core, bf16[512,128]{1,0:T(8,128)(2,1)S(1)} %collective-permute-done.5.dq_y), custom_call_target="tpu_custom_call" | custom-call | flops 17179869184 | bytes 1048576 | tf_op jit(solution)/shard_map/query/pallas_call | solution.py:328
  62.7 7.1 %all-to-all-done.terms = bf16[16,16,256]{2,1,0:T(8,128)(2,1)S(1)} async-done(((bf16[16,16,256]{2,1,0:T(8,128)(2,1)}), bf16[16,16,256]{2,1,0:T(8,128)(2,1)S(1)}, u32[]{:S(2)}, u32[]{:S(2)}) %all-to-all-start) | async-done | bytes 131104 | tf_op jit(solution)/shard_map/all_to_all | solution.py:475
  69.8 0.6 key_value.1
  (4 shorter events, 0.1 us)
Async XLA Ops:
  2.2 18.6 %collective-permute-start = (bf16[1088,128]{1,0:T(8,128)(2,1)S(1)}, bf16[1088,128]{1,0:T(8,128)(2,1)S(1)}, u32[]{:S(2)}, u32[]{:S(2)}) collective-permute-start(bf16[1088,128]{1,0:T(8,128)(2,1)S(1)} %get-tuple-element.17.msg.own), channel_id=1, source_target_pairs={{4,0},{5,1},{6,2},{7,3},{0,4},{1,5},{2,6},{3,7},{12,8},{13,9},{14,... | collective-permute-start | bytes 835592 | tf_op jit(solution)/shard_map/ppermute | solution.py:72
  5.4 17.3 %collective-permute-start.2 = (bf16[256,256]{1,0:T(8,128)(2,1)S(1)}, bf16[256,256]{1,0:T(8,128)(2,1)S(1)}, u32[]{:S(2)}, u32[]{:S(2)}) collective-permute-start(bf16[256,256]{1,0:T(8,128)(2,1)S(1)} %get-tuple-element.18.kv), channel_id=1, source_target_pairs={{466,0},{433,1},{464,2},{435,3},{454,4},{389,5},{452,6},{391,7},{4... | collective-permute-start | bytes 393224 | tf_op jit(solution)/shard_map/ppermute | solution.py:72
  16.6 6.6 %collective-permute-start.1 = (bf16[256,256]{1,0:T(8,128)(2,1)S(1)}, bf16[256,256]{1,0:T(8,128)(2,1)S(1)}, u32[]{:S(2)}, u32[]{:S(2)}) collective-permute-start(bf16[256,256]{1,0:T(8,128)(2,1)S(1)} %get-tuple-element.18.kv), channel_id=1, source_target_pairs={{498,0},{401,1},{496,2},{403,3},{486,4},{421,5},{484,6},{423,7},{5... | collective-permute-start | bytes 393224 | tf_op jit(solution)/shard_map/ppermute | solution.py:72
  20.9 3.9 %collective-permute-start.3 = (bf16[2176,128]{1,0:T(8,128)(2,1)S(1)}, bf16[2176,128]{1,0:T(8,128)(2,1)S(1)}, u32[]{:S(2)}, u32[]{:S(2)}) collective-permute-start(bf16[2176,128]{1,0:T(8,128)(2,1)S(1)} %pad_maximum_fusion), channel_id=1, source_target_pairs={{1,0},{0,1},{3,2},{2,3},{5,4},{4,5},{7,6},{6,7},{9,8},{8,9},{11,10... | collective-permute-start | bytes 1671176 | tf_op jit(solution)/shard_map/ppermute | solution.py:72
  25.2 14.6 %collective-permute-start.4 = (bf16[1024,128]{1,0:T(8,128)(2,1)S(1)}, bf16[1024,128]{1,0:T(8,128)(2,1)S(1)}, u32[]{:S(2)}, u32[]{:S(2)}) collective-permute-start(bf16[1024,128]{1,0:T(8,128)(2,1)S(1)} %get-tuple-element.25), channel_id=1, source_target_pairs={{1,0},{0,1},{3,2},{2,3},{5,4},{4,5},{7,6},{6,7},{9,8},{8,9},{11,10... | collective-permute-start | bytes 786440 | tf_op jit(solution)/shard_map/ppermute | solution.py:72
  29.8 11.9 %collective-permute-start.6 = (bf16[256,256]{1,0:T(8,128)(2,1)S(1)}, bf16[256,256]{1,0:T(8,128)(2,1)S(1)}, u32[]{:S(2)}, u32[]{:S(2)}) collective-permute-start(bf16[256,256]{1,0:T(8,128)(2,1)S(1)} %get-tuple-element.27), channel_id=1, source_target_pairs={{0,466},{1,433},{2,464},{3,435},{4,454},{5,389},{6,452},{7,391},{8... | collective-permute-start | bytes 393224 | tf_op jit(solution)/shard_map/ppermute | solution.py:72
  34.9 6.8 %collective-permute-start.7 = (bf16[256,256]{1,0:T(8,128)(2,1)S(1)}, bf16[256,256]{1,0:T(8,128)(2,1)S(1)}, u32[]{:S(2)}, u32[]{:S(2)}) collective-permute-start(bf16[256,256]{1,0:T(8,128)(2,1)S(1)} %get-tuple-element.28), channel_id=1, source_target_pairs={{0,498},{1,401},{2,496},{3,403},{4,486},{5,421},{6,484},{7,423},{8... | collective-permute-start | bytes 393224 | tf_op jit(solution)/shard_map/ppermute | solution.py:72
  39.8 22.1 %collective-permute-start.5 = (bf16[512,128]{1,0:T(8,128)(2,1)S(1)}, bf16[512,128]{1,0:T(8,128)(2,1)S(1)}, u32[]{:S(2)}, u32[]{:S(2)}) collective-permute-start(bf16[512,128]{1,0:T(8,128)(2,1)S(1)} %add_convert_fusion), channel_id=1, source_target_pairs={{4,0},{5,1},{6,2},{7,3},{0,4},{1,5},{2,6},{3,7},{12,8},{13,9},{14,... | collective-permute-start | bytes 393224 | tf_op jit(solution)/shard_map/ppermute | solution.py:72
  42.5 27.3 %all-to-all-start = ((bf16[16,16,256]{2,1,0:T(8,128)(2,1)}), bf16[16,16,256]{2,1,0:T(8,128)(2,1)S(1)}, u32[]{:S(2)}, u32[]{:S(2)}) async-start(bf16[16,16,256]{2,1,0:T(8,128)(2,1)} %terms.1), calls=%async_computation | async-start | bytes 262144 | tf_op jit(solution)/shard_map/all_to_all | solution.py:475

commit v6 on v5

--- a/solution.py
+++ b/solution.py
@@ -18,8 +18,9 @@
 OWN_FLOPS = 1 << 28
 EARLY_FLOPS = 1 << 34
 LATE_FLOPS = 1 << 30
-TURN_FLOPS = 1 << 27
-QUERY_FLOPS = 1 << 34
+QUERY_FLOPS = 1 << 27
+PART_FLOPS = 1 << 34
+TERMS_FLOPS = 1 << 34
 BF16 = jnp.bfloat16
 VMEM_LIMIT = 24 * 1024 * 1024
 
@@ -270,19 +271,18 @@
     )
 
 
-def early_kernel(own, y, kv_far, aux, dq_own, far, dq):
+def early_kernel(own, y, kv_far, aux, far, dq):
     _, seen = block_place(FAR, aux[0:1, :])
 
     @pl.when(jnp.logical_not(seen))
     def _():
-        dq[0] = dq_own[0]
-        dq[1:] = jnp.zeros_like(dq[1:])
+        dq[...] = jnp.zeros_like(dq)
         far[...] = jnp.zeros_like(far)
 
     @pl.when(seen)
     def _():
         def put(n, query_sum):
-            dq[n] = dq_own[0] + query_sum if n == 0 else query_sum
+            dq[n] = query_sum
 
         key_sum, value_sum = earlier_sums(FAR, (own, y), kv_far, aux, put)
         far[:, :HD] = key_sum
@@ -336,7 +336,7 @@
     )(*arrays)
 
 
-def own_kernel(msg, kv, aux, dq, dkv):
+def own_kernel(msg, kv, aux, dq, dkv, keep, core, send):
     blk = lax.axis_index("blk")
     threshold = aux[0:1, :] - (blk * ROWS).astype(F32)
     key_at = lax.broadcasted_iota(jnp.int32, (ROWS, ROWS), 0)
@@ -344,7 +344,7 @@
     causal = both(jnp.where(key_at <= query_at, key_at, -1).astype(F32))
 
     def put(n, query_sum):
-        dq[n] = query_sum
+        keep[...] = (dq[0] + query_sum).T
 
     key_sum, value_sum = sums_of(
         (msg,),
@@ -356,19 +356,20 @@
     )
     dkv[:, :HD] = key_sum
     dkv[:, HD:] = value_sum
-
-
-def turn_kernel(dq, send, keep):
-    for n, (kept, sent) in enumerate(((0, 2), (1, 3))):
-        at = slice(2 * n * ROWS, 2 * (n + 1) * ROWS)
-        keep[at, :] = dq[kept].T
-        send[at, :] = dq[sent].T.astype(BF16)
-
-
-def query_kernel(dq_keep, dq_core, dq_y, grad_query):
+    core[...] = dq[2].T
+    send[: 2 * ROWS, :] = dq[1].T.astype(BF16)
+    send[2 * ROWS :, :] = dq[3].T.astype(BF16)
+
+
+def part_kernel(keep, core, dq_y, part, onward):
+    part[...] = keep[...] + dq_y[: 2 * ROWS, :].astype(F32)
+    onward[...] = (core[...] + dq_y[2 * ROWS :, :].astype(F32)).astype(BF16)
+
+
+def query_kernel(part, dq_core, grad_query):
     for h in range(2):
         at = slice(h * ROWS, (h + 1) * ROWS)
-        total = dq_keep[at, :] + dq_core[at, :].astype(F32) + dq_y[at, :].astype(F32)
+        total = part[at, :] + dq_core[at, :].astype(F32)
         grad_query[:, h * HD : (h + 1) * HD] = (total * SCALE).astype(BF16)
 
 
@@ -424,15 +425,6 @@
     msg_other = moved(jnp.concatenate([msg, msg_y], axis=0), to_core)
     sums = functools.partial(jax.ShapeDtypeStruct, dtype=F32)
     pair = jax.ShapeDtypeStruct((ROWS, 2 * HD), BF16)
-    dq_own, dkv_own = kernel_call(
-        own_kernel,
-        "own",
-        (sums((1, HD, 2 * ROWS)), sums((ROWS, 2 * HD))),
-        OWN_FLOPS,
-        msg,
-        kv,
-        aux,
-    )
     dkv_far, dq = kernel_call(
         early_kernel,
         "early",
@@ -442,7 +434,6 @@
         msg_y,
         kv_far,
         aux,
-        dq_own,
     )
     dkv_far, dkv_near, dq = kernel_call(
         late_kernel,
@@ -460,20 +451,32 @@
     )
     got_near = moved(dkv_near, inverse(back_near))
     got_far = moved(dkv_far, inverse(back_far))
-    dq_send, dq_keep = kernel_call(
-        turn_kernel,
-        "turn",
-        (jax.ShapeDtypeStruct((4 * ROWS, HD), BF16), sums((4 * ROWS, HD))),
-        TURN_FLOPS,
+    held = sums((2 * ROWS, HD))
+    dkv_own, dq_keep, dq_core, dq_y = kernel_call(
+        own_kernel,
+        "own",
+        (sums((ROWS, 2 * HD)), held, held, jax.ShapeDtypeStruct((4 * ROWS, HD), BF16)),
+        OWN_FLOPS,
+        msg,
+        kv,
+        aux,
         dq,
     )
-    dq_core = moved(dq_send, to_core)
-    dq_pass = (dq_keep[512:] + dq_core[512:].astype(F32)).astype(BF16)
+    dq_y = moved(dq_y, to_y)
+    dq_part, dq_core = kernel_call(
+        part_kernel,
+        "part",
+        (held, jax.ShapeDtypeStruct((2 * ROWS, HD), BF16)),
+        PART_FLOPS,
+        dq_keep,
+        dq_core,
+        dq_y,
+    )
+    dq_core = moved(dq_core, to_core)
     share = jax.ShapeDtypeStruct((16, ROWS // 16, 2 * HD), BF16)
-    (terms,) = kernel_call(terms_kernel, "terms", (share,), 0, dkv_own, got_far, got_near)
-    dq_y = moved(dq_pass, to_y)
+    (terms,) = kernel_call(terms_kernel, "terms", (share,), TERMS_FLOPS, dkv_own, got_far, got_near)
     terms = lax.all_to_all(terms, "head", 0, 0, axis_index_groups=[HEAD_ORDER])
-    (grad_query,) = kernel_call(query_kernel, "query", (pair,), QUERY_FLOPS, dq_keep, dq_core, dq_y)
+    (grad_query,) = kernel_call(query_kernel, "query", (pair,), QUERY_FLOPS, dq_part, dq_core)
     result = jax.ShapeDtypeStruct((terms.shape[1], 2 * HD), BF16)
     return (grad_query, *kernel_call(key_value_kernel, "key_value", (result, result), 0, terms))
 

time: 70.8 us -> 66.5 us (0.939)
  the two profiles are of different devices: /device:TPU:35 before, /device:TPU:1 now
where the time goes in v6:
time: 66.5 us; the launch traced here: 65.5 us
  starting transfers between devices  54.9 us (83%)
  waiting for transfers between devices  5.06 us (8%)
  Pallas kernels  4.74 us (7%)
  between operations  0.78 us (1%)
    ppermute x8, starting transfers between devices, moved(): return lax.ppermute(value, ('blk', 'head'), pairs)  35.4 us
    all_to_all x1, starting transfers between devices, local(): terms = lax.all_to_all(terms, 'head', 0, 0, axis_index_groups=[HEAD_ORDER])  19.5 us
    ppermute x8, waiting for transfers between devices, moved(): return lax.ppermute(value, ('blk', 'head'), pairs)  3.87 us
    pallas_call x7, Pallas kernels, kernel_call(): pl.pallas_call(kernel, out_shape=out_shape, in_specs=[vmem] * len(arrays)...  3.15 us
    pallas_call x1, Pallas kernels, prep(): pl.pallas_call(prep_kernel, out_shape=(jax.ShapeDtypeStruct((MSG, HD), BF...  1.59 us
  transfers between devices with their start and end apart: 9, of which 3 were waited for; matrix products, arithmetic and copies ran while one was open for 0% of the time, Pallas kernels for 4%

profile of v6, /device:TPU:1, one launch (start us, length us, event | category | flops | bytes accessed | tf_op | source)
XLA Modules:
  0.0 65.5 jit_solution(3507887023618683513)
XLA Ops:
  0.6 1.6 %prep.1 = (bf16[1088,128]{1,0:T(8,128)(2,1)S(1)}, bf16[256,256]{1,0:T(8,128)(2,1)S(1)}, f32[8,256]{1,0:T(8,128)S(1)}) custom-call(bf16[256,256]{1,0:T(8,128)(2,1)} %q_in.1, bf16[256,256]{1,0:T(8,128)(2,1)} %k_in.1, bf16[256,256]{1,0:T(8,128)(2,1)} %v_in.1, bf16[256,256]{1,0:T(8,128)(2,1)} %o_in.1, bf16[256,256]{1,0:T(8,128)(2,1)} %do_in.1, f32[2,256]{1,0:T(2,128)} %lse_in.1, ...), custom_call_target="tpu_custom_call" | custom-call | tf_op jit(solution)/shard_map/prep/pallas_call | solution.py:193
  2.2 4.0 %collective-permute-start = (bf16[1088,128]{1,0:T(8,128)(2,1)S(1)}, bf16[1088,128]{1,0:T(8,128)(2,1)S(1)}, u32[]{:S(2)}, u32[]{:S(2)}) collective-permute-start(bf16[1088,128]{1,0:T(8,128)(2,1)S(1)} %get-tuple-element.19.own.msg), channel_id=1, source_target_pairs={{4,0},{5,1},{6,2},{7,3},{0,4},{1,5},{2,6},{3,7},{12,8},{13,9},{14,... | collective-permute-start | bytes 835592 | tf_op jit(solution)/shard_map/ppermute | solution.py:73
  6.3 12.0 %collective-permute-start.2 = (bf16[256,256]{1,0:T(8,128)(2,1)S(1)}, bf16[256,256]{1,0:T(8,128)(2,1)S(1)}, u32[]{:S(2)}, u32[]{:S(2)}) collective-permute-start(bf16[256,256]{1,0:T(8,128)(2,1)S(1)} %get-tuple-element.20.kv), channel_id=1, source_target_pairs={{466,0},{433,1},{464,2},{435,3},{454,4},{389,5},{452,6},{391,7},{4... | collective-permute-start | bytes 393224 | tf_op jit(solution)/shard_map/ppermute | solution.py:73
  18.3 3.6 %collective-permute-start.1 = (bf16[256,256]{1,0:T(8,128)(2,1)S(1)}, bf16[256,256]{1,0:T(8,128)(2,1)S(1)}, u32[]{:S(2)}, u32[]{:S(2)}) collective-permute-start(bf16[256,256]{1,0:T(8,128)(2,1)S(1)} %get-tuple-element.20.kv), channel_id=1, source_target_pairs={{498,0},{401,1},{496,2},{403,3},{486,4},{421,5},{484,6},{423,7},{5... | collective-permute-start | bytes 393224 | tf_op jit(solution)/shard_map/ppermute | solution.py:73
  21.9 0.0 collective-permute-done.y
  21.9 1.9 %collective-permute-start.3 = (bf16[2176,128]{1,0:T(8,128)(2,1)S(1)}, bf16[2176,128]{1,0:T(8,128)(2,1)S(1)}, u32[]{:S(2)}, u32[]{:S(2)}) collective-permute-start(bf16[2176,128]{1,0:T(8,128)(2,1)S(1)} %pad_maximum_fusion), channel_id=1, source_target_pairs={{1,0},{0,1},{3,2},{2,3},{5,4},{4,5},{7,6},{6,7},{9,8},{8,9},{11,10... | collective-permute-start | bytes 1671176 | tf_op jit(solution)/shard_map/ppermute | solution.py:73
  23.8 0.0 collective-permute-done.2.kv_far
  23.9 0.2 early.1
  24.0 2.9 %collective-permute-done.1.kv_near = bf16[256,256]{1,0:T(8,128)(2,1)S(1)} collective-permute-done((bf16[256,256]{1,0:T(8,128)(2,1)S(1)}, bf16[256,256]{1,0:T(8,128)(2,1)S(1)}, u32[]{:S(2)}, u32[]{:S(2)}) %collective-permute-start.1) | collective-permute-done | bytes 131104 | tf_op jit(solution)/shard_map/ppermute | solution.py:73
  26.9 0.0 collective-permute-done.3.other
  26.9 0.2 late.1
  27.2 3.9 %collective-permute-start.6 = (bf16[256,256]{1,0:T(8,128)(2,1)S(1)}, bf16[256,256]{1,0:T(8,128)(2,1)S(1)}, u32[]{:S(2)}, u32[]{:S(2)}) collective-permute-start(bf16[256,256]{1,0:T(8,128)(2,1)S(1)} %get-tuple-element.31), channel_id=1, source_target_pairs={{0,466},{1,433},{2,464},{3,435},{4,454},{5,389},{6,452},{7,391},{8... | collective-permute-start | bytes 393224 | tf_op jit(solution)/shard_map/ppermute | solution.py:73
  31.0 5.7 %collective-permute-start.7 = (bf16[256,256]{1,0:T(8,128)(2,1)S(1)}, bf16[256,256]{1,0:T(8,128)(2,1)S(1)}, u32[]{:S(2)}, u32[]{:S(2)}) collective-permute-start(bf16[256,256]{1,0:T(8,128)(2,1)S(1)} %get-tuple-element.32), channel_id=1, source_target_pairs={{0,498},{1,401},{2,496},{3,403},{4,486},{5,421},{6,484},{7,423},{8... | collective-permute-start | bytes 393224 | tf_op jit(solution)/shard_map/ppermute | solution.py:73
  36.7 0.7 %own.1 = (f32[256,256]{1,0:T(8,128)S(1)}, f32[512,128]{1,0:T(8,128)S(1)}, f32[512,128]{1,0:T(8,128)S(1)}, bf16[1024,128]{1,0:T(8,128)(2,1)S(1)}) custom-call(bf16[1088,128]{1,0:T(8,128)(2,1)S(1)} %get-tuple-element.19.own.msg, bf16[256,256]{1,0:T(8,128)(2,1)S(1)} %get-tuple-element.20.kv, f32[8,256]{1,0:T(8,128)S(1)} %get-tuple-element.21.aux, ...), custom_call_target="tpu_custom_call" | custom-call | flops 268435456 | bytes 1048576 | tf_op jit(solution)/shard_map/own/pallas_call | solution.py:328
  37.4 2.1 %collective-permute-start.4 = (bf16[1024,128]{1,0:T(8,128)(2,1)S(1)}, bf16[1024,128]{1,0:T(8,128)(2,1)S(1)}, u32[]{:S(2)}, u32[]{:S(2)}) collective-permute-start(bf16[1024,128]{1,0:T(8,128)(2,1)S(1)} %get-tuple-element.27), channel_id=1, source_target_pairs={{4,0},{5,1},{6,2},{7,3},{0,4},{1,5},{2,6},{3,7},{12,8},{13,9},{14,... | collective-permute-start | bytes 786440 | tf_op jit(solution)/shard_map/ppermute | solution.py:73
  39.5 0.0 collective-permute-done.6.far
  39.5 0.0 collective-permute-done.7.near
  39.5 0.7 %terms.1 = bf16[16,16,256]{2,1,0:T(8,128)(2,1)} custom-call(f32[256,256]{1,0:T(8,128)S(1)} %get-tuple-element.30.own, bf16[256,256]{1,0:T(8,128)(2,1)S(1)} %collective-permute-done.6.far, bf16[256,256]{1,0:T(8,128)(2,1)S(1)} %collective-permute-done.7.near), custom_call_target="tpu_custom_call" | custom-call | flops 17179869184 | bytes 1048576 | tf_op jit(solution)/shard_map/terms/pallas_call | solution.py:328
  40.2 19.5 %all-to-all-start = ((bf16[16,16,256]{2,1,0:T(8,128)(2,1)}), bf16[16,16,256]{2,1,0:T(8,128)(2,1)S(1)}, u32[]{:S(2)}, u32[]{:S(2)}) async-start(bf16[16,16,256]{2,1,0:T(8,128)(2,1)} %terms.1), calls=%async_computation | async-start | bytes 262144 | tf_op jit(solution)/shard_map/all_to_all | solution.py:478
  59.8 2.3 %collective-permute-start.5 = (bf16[512,128]{1,0:T(8,128)(2,1)S(1)}, bf16[512,128]{1,0:T(8,128)(2,1)S(1)}, u32[]{:S(2)}, u32[]{:S(2)}) collective-permute-start(bf16[512,128]{1,0:T(8,128)(2,1)S(1)} %get-tuple-element.29), channel_id=1, source_target_pairs={{1,0},{0,1},{3,2},{2,3},{5,4},{4,5},{7,6},{6,7},{9,8},{8,9},{11,10... | collective-permute-start | bytes 393224 | tf_op jit(solution)/shard_map/ppermute | solution.py:73
  62.0 1.0 %collective-permute-done.5.dq_core = bf16[512,128]{1,0:T(8,128)(2,1)S(1)} collective-permute-done((bf16[512,128]{1,0:T(8,128)(2,1)S(1)}, bf16[512,128]{1,0:T(8,128)(2,1)S(1)}, u32[]{:S(2)}, u32[]{:S(2)}) %collective-permute-start.5) | collective-permute-done | bytes 131104 | tf_op jit(solution)/shard_map/ppermute | solution.py:73
  63.0 0.7 %query.1 = bf16[256,256]{1,0:T(8,128)(2,1)} custom-call(f32[512,128]{1,0:T(8,128)S(1)} %get-tuple-element.28.part, bf16[512,128]{1,0:T(8,128)(2,1)S(1)} %collective-permute-done.5.dq_core), custom_call_target="tpu_custom_call" | custom-call | flops 134217728 | bytes 1048576 | tf_op jit(solution)/shard_map/query/pallas_call | solution.py:328
  63.7 1.2 %all-to-all-done.terms = bf16[16,16,256]{2,1,0:T(8,128)(2,1)S(1)} async-done(((bf16[16,16,256]{2,1,0:T(8,128)(2,1)}), bf16[16,16,256]{2,1,0:T(8,128)(2,1)S(1)}, u32[]{:S(2)}, u32[]{:S(2)}) %all-to-all-start) | async-done | bytes 131104 | tf_op jit(solution)/shard_map/all_to_all | solution.py:478
  64.9 0.6 key_value.1
  (3 shorter events, 0.1 us)
Async XLA Ops:
  2.2 19.6 %collective-permute-start = (bf16[1088,128]{1,0:T(8,128)(2,1)S(1)}, bf16[1088,128]{1,0:T(8,128)(2,1)S(1)}, u32[]{:S(2)}, u32[]{:S(2)}) collective-permute-start(bf16[1088,128]{1,0:T(8,128)(2,1)S(1)} %get-tuple-element.19.own.msg), channel_id=1, source_target_pairs={{4,0},{5,1},{6,2},{7,3},{0,4},{1,5},{2,6},{3,7},{12,8},{13,9},{14,... | collective-permute-start | bytes 835592 | tf_op jit(solution)/shard_map/ppermute | solution.py:73
  6.3 17.6 %collective-permute-start.2 = (bf16[256,256]{1,0:T(8,128)(2,1)S(1)}, bf16[256,256]{1,0:T(8,128)(2,1)S(1)}, u32[]{:S(2)}, u32[]{:S(2)}) collective-permute-start(bf16[256,256]{1,0:T(8,128)(2,1)S(1)} %get-tuple-element.20.kv), channel_id=1, source_target_pairs={{466,0},{433,1},{464,2},{435,3},{454,4},{389,5},{452,6},{391,7},{4... | collective-permute-start | bytes 393224 | tf_op jit(solution)/shard_map/ppermute | solution.py:73
  18.3 8.6 %collective-permute-start.1 = (bf16[256,256]{1,0:T(8,128)(2,1)S(1)}, bf16[256,256]{1,0:T(8,128)(2,1)S(1)}, u32[]{:S(2)}, u32[]{:S(2)}) collective-permute-start(bf16[256,256]{1,0:T(8,128)(2,1)S(1)} %get-tuple-element.20.kv), channel_id=1, source_target_pairs={{498,0},{401,1},{496,2},{403,3},{486,4},{421,5},{484,6},{423,7},{5... | collective-permute-start | bytes 393224 | tf_op jit(solution)/shard_map/ppermute | solution.py:73
  21.9 5.0 %collective-permute-start.3 = (bf16[2176,128]{1,0:T(8,128)(2,1)S(1)}, bf16[2176,128]{1,0:T(8,128)(2,1)S(1)}, u32[]{:S(2)}, u32[]{:S(2)}) collective-permute-start(bf16[2176,128]{1,0:T(8,128)(2,1)S(1)} %pad_maximum_fusion), channel_id=1, source_target_pairs={{1,0},{0,1},{3,2},{2,3},{5,4},{4,5},{7,6},{6,7},{9,8},{8,9},{11,10... | collective-permute-start | bytes 1671176 | tf_op jit(solution)/shard_map/ppermute | solution.py:73
  27.2 12.3 %collective-permute-start.6 = (bf16[256,256]{1,0:T(8,128)(2,1)S(1)}, bf16[256,256]{1,0:T(8,128)(2,1)S(1)}, u32[]{:S(2)}, u32[]{:S(2)}) collective-permute-start(bf16[256,256]{1,0:T(8,128)(2,1)S(1)} %get-tuple-element.31), channel_id=1, source_target_pairs={{0,466},{1,433},{2,464},{3,435},{4,454},{5,389},{6,452},{7,391},{8... | collective-permute-start | bytes 393224 | tf_op jit(solution)/shard_map/ppermute | solution.py:73
  31.0 8.5 %collective-permute-start.7 = (bf16[256,256]{1,0:T(8,128)(2,1)S(1)}, bf16[256,256]{1,0:T(8,128)(2,1)S(1)}, u32[]{:S(2)}, u32[]{:S(2)}) collective-permute-start(bf16[256,256]{1,0:T(8,128)(2,1)S(1)} %get-tuple-element.32), channel_id=1, source_target_pairs={{0,498},{1,401},{2,496},{3,403},{4,486},{5,421},{6,484},{7,423},{8... | collective-permute-start | bytes 393224 | tf_op jit(solution)/shard_map/ppermute | solution.py:73
  37.4 22.3 %collective-permute-start.4 = (bf16[1024,128]{1,0:T(8,128)(2,1)S(1)}, bf16[1024,128]{1,0:T(8,128)(2,1)S(1)}, u32[]{:S(2)}, u32[]{:S(2)}) collective-permute-start(bf16[1024,128]{1,0:T(8,128)(2,1)S(1)} %get-tuple-element.27), channel_id=1, source_target_pairs={{4,0},{5,1},{6,2},{7,3},{0,4},{1,5},{2,6},{3,7},{12,8},{13,9},{14,... | collective-permute-start | bytes 786440 | tf_op jit(solution)/shard_map/ppermute | solution.py:73
  40.2 24.7 %all-to-all-start = ((bf16[16,16,256]{2,1,0:T(8,128)(2,1)}), bf16[16,16,256]{2,1,0:T(8,128)(2,1)S(1)}, u32[]{:S(2)}, u32[]{:S(2)}) async-start(bf16[16,16,256]{2,1,0:T(8,128)(2,1)} %terms.1), calls=%async_computation | async-start | bytes 262144 | tf_op jit(solution)/shard_map/all_to_all | solution.py:478
  59.8 3.2 %collective-permute-start.5 = (bf16[512,128]{1,0:T(8,128)(2,1)S(1)}, bf16[512,128]{1,0:T(8,128)(2,1)S(1)}, u32[]{:S(2)}, u32[]{:S(2)}) collective-permute-start(bf16[512,128]{1,0:T(8,128)(2,1)S(1)} %get-tuple-element.29), channel_id=1, source_target_pairs={{1,0},{0,1},{3,2},{2,3},{5,4},{4,5},{7,6},{6,7},{9,8},{8,9},{11,10... | collective-permute-start | bytes 393224 | tf_op jit(solution)/shard_map/ppermute | solution.py:73

commit v7 on v6

--- a/solution.py
+++ b/solution.py
@@ -24,8 +24,8 @@
 BF16 = jnp.bfloat16
 VMEM_LIMIT = 24 * 1024 * 1024
 
-NEAR = ((1, 7), (2, 6))
-FAR = ((3, 5), (4, 8))
+NEAR = ((1, 7), (8, 2))
+FAR = ((5, 3), (4, 6))
 
 HEAD_ORDER = [y * 4 + z_hi * 2 + core for z_hi in (1, 0) for y in range(4) for core in range(2)]
 
@@ -51,7 +51,7 @@
     x, y, z, core = place(index)
     steps = table[y % 2][core]
     source_x = x if z % 8 >= steps else x - 1
-    up = steps < 4 or (steps == 4 and z % 2 == 0)
+    up = steps < 4 or (steps == 4 and z % 4 != 3)
     return device(source_x, y, z - steps if up else z + 8 - steps, core)
 
 
@@ -110,11 +110,7 @@
     msg,
     kv,
     aux,
-    q,
-    k,
-    v,
     o,
-    do,
     lse,
     ent,
     seg,
@@ -123,32 +119,24 @@
     rows,
     sems,
 ):
-    arriving = [
+    blk = lax.axis_index("blk")
+    column = pl.multiple_of(lax.div(lax.axis_index("head"), 8) * HD, HD)
+    moves = [(weight_index_in, weight_index), (weights_in, weights), (seg_in, seg)]
+    moves += [(lse_in, lse), (ent_in, ent), (o_in, o)]
+    for first, source in ((2, do_in), (0, q_in)):
+        for h in range(2):
+            target = msg.at[(first + h) * ROWS : (first + h + 1) * ROWS, :]
+            moves.append((source.at[:, h * HD : (h + 1) * HD], target))
+    moves.append((k_in.at[:, pl.ds(column, HD)], kv.at[:, :HD]))
+    moves.append((v_in.at[:, pl.ds(column, HD)], kv.at[:, HD:]))
+    copies = [
         pltpu.make_async_copy(source, target, sems.at[n])
-        for n, (source, target) in enumerate(
-            (
-                (weight_index_in, weight_index),
-                (weights_in, weights),
-                (seg_in, seg),
-                (lse_in, lse),
-                (ent_in, ent),
-                (do_in, do),
-                (o_in, o),
-                (q_in, q),
-                (k_in, k),
-                (v_in, v),
-            )
-        )
+        for n, (source, target) in enumerate(moves)
     ]
-    for copy in arriving:
+    for copy in copies:
         copy.start()
-    for copy in arriving:
+    for copy in copies[:3]:
         copy.wait()
-    blk = lax.axis_index("blk")
-    head = lax.axis_index("head")
-    column = pl.multiple_of(lax.div(head, 8) * HD, HD)
-    kv[:, :HD] = k[:, pl.ds(column, HD)]
-    kv[:, HD:] = v[:, pl.ds(column, HD)]
     docs = weight_index.shape[0]
     tokens = seg[...]
     first = seg[pl.ds(2 * blk, 1), :]
@@ -167,12 +155,11 @@
     aux[0:1, :] = start
     aux[1:2, :] = rate
     rows[...] = jnp.zeros_like(rows)
+    for copy in copies[3:8]:
+        copy.wait()
     for h in range(2):
-        columns = slice(h * HD, (h + 1) * HD)
-        do_h = do[:, columns]
-        msg[h * ROWS : (h + 1) * ROWS, :] = q[:, columns]
-        msg[(2 + h) * ROWS : (3 + h) * ROWS, :] = do_h
-        product = do_h.astype(F32) * o[:, columns].astype(F32)
+        do = msg[(2 + h) * ROWS : (3 + h) * ROWS, :]
+        product = do.astype(F32) * o[:, h * HD : (h + 1) * HD].astype(F32)
         delta = jnp.sum(product.T, axis=0, keepdims=True)
         lse_h = lse[h : h + 1, :]
         const = delta + rate * (ent[h : h + 1, :] - lse_h)
@@ -184,11 +171,13 @@
         at = 1024 + 32 * h
         msg[at : at + 16, :] = rows[:, :HD].astype(BF16)
         msg[at + 16 : at + 32, :] = rows[:, HD:].astype(BF16)
+    for copy in copies[8:]:
+        copy.wait()
 
 
 def prep(*arrays):
     vmem = pl.BlockSpec(memory_space=pltpu.VMEM)
-    held = [pltpu.VMEM(array.shape, array.dtype) for array in arrays[:8]]
+    held = [pltpu.VMEM(arrays[n].shape, arrays[n].dtype) for n in (3, 5, 6, 7)]
     held += [pltpu.SMEM(array.shape, array.dtype) for array in arrays[8:]]
     return pl.pallas_call(
         prep_kernel,
@@ -200,7 +189,7 @@
         in_specs=[pl.BlockSpec(memory_space=pltpu.HBM)] * 10,
         out_specs=(vmem,) * 3,
         scratch_shapes=held
-        + [pltpu.VMEM((16, ROWS), F32), pltpu.SemaphoreType.DMA((10,))],
+        + [pltpu.VMEM((16, ROWS), F32), pltpu.SemaphoreType.DMA((12,))],
         name="prep",
         compiler_params=pltpu.CompilerParams(vmem_limit_bytes=VMEM_LIMIT),
     )(*[pltpu.with_memory_space_constraint(array, pltpu.HBM) for array in arrays])

time: 66.5 us -> 66.1 us (level)
  the two profiles are of different devices: /device:TPU:1 before, /device:TPU:32 now
where the time goes in v7:
time: 66.1 us; the launch traced here: 65.7 us
  starting transfers between devices  53.1 us (80%)
  Pallas kernels  6 us (9%)
  waiting for transfers between devices  5.81 us (9%)
  between operations  0.78 us (1%)
    ppermute x8, starting transfers between devices, moved(): return lax.ppermute(value, ('blk', 'head'), pairs)  38.4 us
    all_to_all x1, starting transfers between devices, local(): terms = lax.all_to_all(terms, 'head', 0, 0, axis_index_groups=[HEAD_ORDER])  14.7 us
    pallas_call x7, Pallas kernels, kernel_call(): pl.pallas_call(kernel, out_shape=out_shape, in_specs=[vmem] * len(arrays)...  4.73 us
    ppermute x8, waiting for transfers between devices, moved(): return lax.ppermute(value, ('blk', 'head'), pairs)  2.94 us
    all_to_all x1, waiting for transfers between devices, local(): terms = lax.all_to_all(terms, 'head', 0, 0, axis_index_groups=[HEAD_ORDER])  2.87 us
  transfers between devices with their start and end apart: 9, of which 3 were waited for; matrix products, arithmetic and copies ran while one was open for 0% of the time, Pallas kernels for 4%

profile of v7, /device:TPU:32, one launch (start us, length us, event | category | flops | bytes accessed | tf_op | source)
XLA Modules:
  0.0 65.7 jit_solution(4397436184308174437)
XLA Ops:
  0.6 1.3 %prep.1 = (bf16[1088,128]{1,0:T(8,128)(2,1)S(1)}, bf16[256,256]{1,0:T(8,128)(2,1)S(1)}, f32[8,256]{1,0:T(8,128)S(1)}) custom-call(bf16[256,256]{1,0:T(8,128)(2,1)} %q_in.1, bf16[256,256]{1,0:T(8,128)(2,1)} %k_in.1, bf16[256,256]{1,0:T(8,128)(2,1)} %v_in.1, bf16[256,256]{1,0:T(8,128)(2,1)} %o_in.1, bf16[256,256]{1,0:T(8,128)(2,1)} %do_in.1, f32[2,256]{1,0:T(2,128)} %lse_in.1, ...), custom_call_target="tpu_custom_call" | custom-call | tf_op jit(solution)/shard_map/prep/pallas_call | solution.py:182
  1.9 3.5 %collective-permute-start = (bf16[1088,128]{1,0:T(8,128)(2,1)S(1)}, bf16[1088,128]{1,0:T(8,128)(2,1)S(1)}, u32[]{:S(2)}, u32[]{:S(2)}) collective-permute-start(bf16[1088,128]{1,0:T(8,128)(2,1)S(1)} %get-tuple-element.19.own.msg), channel_id=1, source_target_pairs={{4,0},{5,1},{6,2},{7,3},{0,4},{1,5},{2,6},{3,7},{12,8},{13,9},{14,... | collective-permute-start | bytes 835592 | tf_op jit(solution)/shard_map/ppermute | solution.py:73
  5.4 11.4 %collective-permute-start.2 = (bf16[256,256]{1,0:T(8,128)(2,1)S(1)}, bf16[256,256]{1,0:T(8,128)(2,1)S(1)}, u32[]{:S(2)}, u32[]{:S(2)}) collective-permute-start(bf16[256,256]{1,0:T(8,128)(2,1)S(1)} %get-tuple-element.20.kv), channel_id=1, source_target_pairs={{432,0},{467,1},{434,2},{465,3},{454,4},{421,5},{452,6},{423,7},{4... | collective-permute-start | bytes 393224 | tf_op jit(solution)/shard_map/ppermute | solution.py:73
  16.8 2.9 %collective-permute-start.1 = (bf16[256,256]{1,0:T(8,128)(2,1)S(1)}, bf16[256,256]{1,0:T(8,128)(2,1)S(1)}, u32[]{:S(2)}, u32[]{:S(2)}) collective-permute-start(bf16[256,256]{1,0:T(8,128)(2,1)S(1)} %get-tuple-element.20.kv), channel_id=1, source_target_pairs={{498,0},{401,1},{496,2},{403,3},{388,4},{487,5},{390,6},{485,7},{5... | collective-permute-start | bytes 393224 | tf_op jit(solution)/shard_map/ppermute | solution.py:73
  19.7 0.0 collective-permute-done.y
  19.8 1.9 %collective-permute-start.3 = (bf16[2176,128]{1,0:T(8,128)(2,1)S(1)}, bf16[2176,128]{1,0:T(8,128)(2,1)S(1)}, u32[]{:S(2)}, u32[]{:S(2)}) collective-permute-start(bf16[2176,128]{1,0:T(8,128)(2,1)S(1)} %pad_maximum_fusion), channel_id=1, source_target_pairs={{1,0},{0,1},{3,2},{2,3},{5,4},{4,5},{7,6},{6,7},{9,8},{8,9},{11,10... | collective-permute-start | bytes 1671176 | tf_op jit(solution)/shard_map/ppermute | solution.py:73
  21.7 0.0 collective-permute-done.2.kv_far
  21.7 0.2 early.1
  21.9 1.7 %collective-permute-done.1.kv_near = bf16[256,256]{1,0:T(8,128)(2,1)S(1)} collective-permute-done((bf16[256,256]{1,0:T(8,128)(2,1)S(1)}, bf16[256,256]{1,0:T(8,128)(2,1)S(1)}, u32[]{:S(2)}, u32[]{:S(2)}) %collective-permute-start.1) | collective-permute-done | bytes 131104 | tf_op jit(solution)/shard_map/ppermute | solution.py:73
  23.7 0.0 collective-permute-done.3.other
  23.7 1.8 %late.1 = (bf16[256,256]{1,0:T(8,128)(2,1)S(1)}, bf16[256,256]{1,0:T(8,128)(2,1)S(1)}, f32[4,128,512]{2,1,0:T(8,128)S(1)}) custom-call(bf16[1088,128]{1,0:T(8,128)(2,1)S(1)} %get-tuple-element.19.own.msg, bf16[1088,128]{1,0:T(8,128)(2,1)S(1)} %collective-permute-done.y, bf16[256,256]{1,0:T(8,128)(2,1)S(1)} %collective-permute-done.1.kv_near, ...), custom_call_target="tpu_custom_call" | custom-call | flops 1073741824 | bytes 1048576 | tf_op jit(solution)/shard_map/late/pallas_call | solution.py:317
  25.5 4.3 %collective-permute-start.6 = (bf16[256,256]{1,0:T(8,128)(2,1)S(1)}, bf16[256,256]{1,0:T(8,128)(2,1)S(1)}, u32[]{:S(2)}, u32[]{:S(2)}) collective-permute-start(bf16[256,256]{1,0:T(8,128)(2,1)S(1)} %get-tuple-element.31), channel_id=1, source_target_pairs={{0,432},{1,467},{2,434},{3,465},{4,454},{5,421},{6,452},{7,423},{8... | collective-permute-start | bytes 393224 | tf_op jit(solution)/shard_map/ppermute | solution.py:73
  29.8 4.6 %collective-permute-start.7 = (bf16[256,256]{1,0:T(8,128)(2,1)S(1)}, bf16[256,256]{1,0:T(8,128)(2,1)S(1)}, u32[]{:S(2)}, u32[]{:S(2)}) collective-permute-start(bf16[256,256]{1,0:T(8,128)(2,1)S(1)} %get-tuple-element.32), channel_id=1, source_target_pairs={{0,498},{1,401},{2,496},{3,403},{4,388},{5,487},{6,390},{7,485},{8... | collective-permute-start | bytes 393224 | tf_op jit(solution)/shard_map/ppermute | solution.py:73
  34.4 0.7 %own.1 = (f32[256,256]{1,0:T(8,128)S(1)}, f32[512,128]{1,0:T(8,128)S(1)}, f32[512,128]{1,0:T(8,128)S(1)}, bf16[1024,128]{1,0:T(8,128)(2,1)S(1)}) custom-call(bf16[1088,128]{1,0:T(8,128)(2,1)S(1)} %get-tuple-element.19.own.msg, bf16[256,256]{1,0:T(8,128)(2,1)S(1)} %get-tuple-element.20.kv, f32[8,256]{1,0:T(8,128)S(1)} %get-tuple-element.21.aux, ...), custom_call_target="tpu_custom_call" | custom-call | flops 268435456 | bytes 1048576 | tf_op jit(solution)/shard_map/own/pallas_call | solution.py:317
  35.1 7.7 %collective-permute-start.4 = (bf16[1024,128]{1,0:T(8,128)(2,1)S(1)}, bf16[1024,128]{1,0:T(8,128)(2,1)S(1)}, u32[]{:S(2)}, u32[]{:S(2)}) collective-permute-start(bf16[1024,128]{1,0:T(8,128)(2,1)S(1)} %get-tuple-element.27), channel_id=1, source_target_pairs={{4,0},{5,1},{6,2},{7,3},{0,4},{1,5},{2,6},{3,7},{12,8},{13,9},{14,... | collective-permute-start | bytes 786440 | tf_op jit(solution)/shard_map/ppermute | solution.py:73
  42.8 0.0 collective-permute-done.6.far
  42.8 0.7 %terms.1 = bf16[16,16,256]{2,1,0:T(8,128)(2,1)} custom-call(f32[256,256]{1,0:T(8,128)S(1)} %get-tuple-element.30.own, bf16[256,256]{1,0:T(8,128)(2,1)S(1)} %collective-permute-done.6.far, bf16[256,256]{1,0:T(8,128)(2,1)S(1)} %collective-permute-done.7.near), custom_call_target="tpu_custom_call" | custom-call | flops 17179869184 | bytes 1048576 | tf_op jit(solution)/shard_map/terms/pallas_call | solution.py:317
  43.6 14.7 %all-to-all-start = ((bf16[16,16,256]{2,1,0:T(8,128)(2,1)}), bf16[16,16,256]{2,1,0:T(8,128)(2,1)S(1)}, u32[]{:S(2)}, u32[]{:S(2)}) async-start(bf16[16,16,256]{2,1,0:T(8,128)(2,1)} %terms.1), calls=%async_computation | async-start | bytes 262144 | tf_op jit(solution)/shard_map/all_to_all | solution.py:467
  58.2 0.0 collective-permute-done.4.dq_y
  58.3 2.1 %collective-permute-start.5 = (bf16[512,128]{1,0:T(8,128)(2,1)S(1)}, bf16[512,128]{1,0:T(8,128)(2,1)S(1)}, u32[]{:S(2)}, u32[]{:S(2)}) collective-permute-start(bf16[512,128]{1,0:T(8,128)(2,1)S(1)} %get-tuple-element.29), channel_id=1, source_target_pairs={{1,0},{0,1},{3,2},{2,3},{5,4},{4,5},{7,6},{6,7},{9,8},{8,9},{11,10... | collective-permute-start | bytes 393224 | tf_op jit(solution)/shard_map/ppermute | solution.py:73
  60.3 1.2 %collective-permute-done.5.dq_core = bf16[512,128]{1,0:T(8,128)(2,1)S(1)} collective-permute-done((bf16[512,128]{1,0:T(8,128)(2,1)S(1)}, bf16[512,128]{1,0:T(8,128)(2,1)S(1)}, u32[]{:S(2)}, u32[]{:S(2)}) %collective-permute-start.5) | collective-permute-done | bytes 131104 | tf_op jit(solution)/shard_map/ppermute | solution.py:73
  61.5 0.7 %query.1 = bf16[256,256]{1,0:T(8,128)(2,1)} custom-call(f32[512,128]{1,0:T(8,128)S(1)} %get-tuple-element.28.part, bf16[512,128]{1,0:T(8,128)(2,1)S(1)} %collective-permute-done.5.dq_core), custom_call_target="tpu_custom_call" | custom-call | flops 134217728 | bytes 1048576 | tf_op jit(solution)/shard_map/query/pallas_call | solution.py:317
  62.2 2.9 %all-to-all-done.terms = bf16[16,16,256]{2,1,0:T(8,128)(2,1)S(1)} async-done(((bf16[16,16,256]{2,1,0:T(8,128)(2,1)}), bf16[16,16,256]{2,1,0:T(8,128)(2,1)S(1)}, u32[]{:S(2)}, u32[]{:S(2)}) %all-to-all-start) | async-done | bytes 131104 | tf_op jit(solution)/shard_map/all_to_all | solution.py:467
  65.1 0.6 key_value.1
  (3 shorter events, 0.1 us)
Async XLA Ops:
  1.9 17.8 %collective-permute-start = (bf16[1088,128]{1,0:T(8,128)(2,1)S(1)}, bf16[1088,128]{1,0:T(8,128)(2,1)S(1)}, u32[]{:S(2)}, u32[]{:S(2)}) collective-permute-start(bf16[1088,128]{1,0:T(8,128)(2,1)S(1)} %get-tuple-element.19.own.msg), channel_id=1, source_target_pairs={{4,0},{5,1},{6,2},{7,3},{0,4},{1,5},{2,6},{3,7},{12,8},{13,9},{14,... | collective-permute-start | bytes 835592 | tf_op jit(solution)/shard_map/ppermute | solution.py:73
  5.4 16.3 %collective-permute-start.2 = (bf16[256,256]{1,0:T(8,128)(2,1)S(1)}, bf16[256,256]{1,0:T(8,128)(2,1)S(1)}, u32[]{:S(2)}, u32[]{:S(2)}) collective-permute-start(bf16[256,256]{1,0:T(8,128)(2,1)S(1)} %get-tuple-element.20.kv), channel_id=1, source_target_pairs={{432,0},{467,1},{434,2},{465,3},{454,4},{421,5},{452,6},{423,7},{4... | collective-permute-start | bytes 393224 | tf_op jit(solution)/shard_map/ppermute | solution.py:73
  16.8 6.9 %collective-permute-start.1 = (bf16[256,256]{1,0:T(8,128)(2,1)S(1)}, bf16[256,256]{1,0:T(8,128)(2,1)S(1)}, u32[]{:S(2)}, u32[]{:S(2)}) collective-permute-start(bf16[256,256]{1,0:T(8,128)(2,1)S(1)} %get-tuple-element.20.kv), channel_id=1, source_target_pairs={{498,0},{401,1},{496,2},{403,3},{388,4},{487,5},{390,6},{485,7},{5... | collective-permute-start | bytes 393224 | tf_op jit(solution)/shard_map/ppermute | solution.py:73
  19.8 3.9 %collective-permute-start.3 = (bf16[2176,128]{1,0:T(8,128)(2,1)S(1)}, bf16[2176,128]{1,0:T(8,128)(2,1)S(1)}, u32[]{:S(2)}, u32[]{:S(2)}) collective-permute-start(bf16[2176,128]{1,0:T(8,128)(2,1)S(1)} %pad_maximum_fusion), channel_id=1, source_target_pairs={{1,0},{0,1},{3,2},{2,3},{5,4},{4,5},{7,6},{6,7},{9,8},{8,9},{11,10... | collective-permute-start | bytes 1671176 | tf_op jit(solution)/shard_map/ppermute | solution.py:73
  25.5 17.4 %collective-permute-start.6 = (bf16[256,256]{1,0:T(8,128)(2,1)S(1)}, bf16[256,256]{1,0:T(8,128)(2,1)S(1)}, u32[]{:S(2)}, u32[]{:S(2)}) collective-permute-start(bf16[256,256]{1,0:T(8,128)(2,1)S(1)} %get-tuple-element.31), channel_id=1, source_target_pairs={{0,432},{1,467},{2,434},{3,465},{4,454},{5,421},{6,452},{7,423},{8... | collective-permute-start | bytes 393224 | tf_op jit(solution)/shard_map/ppermute | solution.py:73
  29.8 13.0 %collective-permute-start.7 = (bf16[256,256]{1,0:T(8,128)(2,1)S(1)}, bf16[256,256]{1,0:T(8,128)(2,1)S(1)}, u32[]{:S(2)}, u32[]{:S(2)}) collective-permute-start(bf16[256,256]{1,0:T(8,128)(2,1)S(1)} %get-tuple-element.32), channel_id=1, source_target_pairs={{0,498},{1,401},{2,496},{3,403},{4,388},{5,487},{6,390},{7,485},{8... | collective-permute-start | bytes 393224 | tf_op jit(solution)/shard_map/ppermute | solution.py:73
  35.1 23.1 %collective-permute-start.4 = (bf16[1024,128]{1,0:T(8,128)(2,1)S(1)}, bf16[1024,128]{1,0:T(8,128)(2,1)S(1)}, u32[]{:S(2)}, u32[]{:S(2)}) collective-permute-start(bf16[1024,128]{1,0:T(8,128)(2,1)S(1)} %get-tuple-element.27), channel_id=1, source_target_pairs={{4,0},{5,1},{6,2},{7,3},{0,4},{1,5},{2,6},{3,7},{12,8},{13,9},{14,... | collective-permute-start | bytes 786440 | tf_op jit(solution)/shard_map/ppermute | solution.py:73
  43.6 21.5 %all-to-all-start = ((bf16[16,16,256]{2,1,0:T(8,128)(2,1)}), bf16[16,16,256]{2,1,0:T(8,128)(2,1)S(1)}, u32[]{:S(2)}, u32[]{:S(2)}) async-start(bf16[16,16,256]{2,1,0:T(8,128)(2,1)} %terms.1), calls=%async_computation | async-start | bytes 262144 | tf_op jit(solution)/shard_map/all_to_all | solution.py:467
  58.3 3.2 %collective-permute-start.5 = (bf16[512,128]{1,0:T(8,128)(2,1)S(1)}, bf16[512,128]{1,0:T(8,128)(2,1)S(1)}, u32[]{:S(2)}, u32[]{:S(2)}) collective-permute-start(bf16[512,128]{1,0:T(8,128)(2,1)S(1)} %get-tuple-element.29), channel_id=1, source_target_pairs={{1,0},{0,1},{3,2},{2,3},{5,4},{4,5},{7,6},{6,7},{9,8},{8,9},{11,10... | collective-permute-start | bytes 393224 | tf_op jit(solution)/shard_map/ppermute | solution.py:73

commit v8 on v7

--- a/solution.py
+++ b/solution.py
@@ -51,7 +51,7 @@
     x, y, z, core = place(index)
     steps = table[y % 2][core]
     source_x = x if z % 8 >= steps else x - 1
-    up = steps < 4 or (steps == 4 and z % 4 != 3)
+    up = steps < 4 or (steps == 4 and z % 2 == 0)
     return device(source_x, y, z - steps if up else z + 8 - steps, core)
 
 

time: 66.1 us -> 65 us (0.983)
  the two profiles are of different devices: /device:TPU:32 before, /device:TPU:1 now
where the time goes in v8:
time: 65 us; the launch traced here: 64.3 us
  starting transfers between devices  53.3 us (82%)
  waiting for transfers between devices  5.74 us (9%)
  Pallas kernels  4.42 us (7%)
  between operations  0.78 us (1%)
    ppermute x8, starting transfers between devices, moved(): return lax.ppermute(value, ('blk', 'head'), pairs)  38.5 us
    all_to_all x1, starting transfers between devices, local(): terms = lax.all_to_all(terms, 'head', 0, 0, axis_index_groups=[HEAD_ORDER])  14.8 us
    ppermute x8, waiting for transfers between devices, moved(): return lax.ppermute(value, ('blk', 'head'), pairs)  4.5 us
    pallas_call x7, Pallas kernels, kernel_call(): pl.pallas_call(kernel, out_shape=out_shape, in_specs=[vmem] * len(arrays)...  3.15 us
  transfers between devices with their start and end apart: 9, of which 5 were waited for; matrix products, arithmetic and copies ran while one was open for 0% of the time, Pallas kernels for 4%

profile of v8, /device:TPU:1, one launch (start us, length us, event | category | flops | bytes accessed | tf_op | source)
XLA Modules:
  0.0 64.3 jit_solution(16943432518168939855)
XLA Ops:
  0.6 1.3 %prep.1 = (bf16[1088,128]{1,0:T(8,128)(2,1)S(1)}, bf16[256,256]{1,0:T(8,128)(2,1)S(1)}, f32[8,256]{1,0:T(8,128)S(1)}) custom-call(bf16[256,256]{1,0:T(8,128)(2,1)} %q_in.1, bf16[256,256]{1,0:T(8,128)(2,1)} %k_in.1, bf16[256,256]{1,0:T(8,128)(2,1)} %v_in.1, bf16[256,256]{1,0:T(8,128)(2,1)} %o_in.1, bf16[256,256]{1,0:T(8,128)(2,1)} %do_in.1, f32[2,256]{1,0:T(2,128)} %lse_in.1, ...), custom_call_target="tpu_custom_call" | custom-call | tf_op jit(solution)/shard_map/prep/pallas_call | solution.py:182
  1.9 4.0 %collective-permute-start = (bf16[1088,128]{1,0:T(8,128)(2,1)S(1)}, bf16[1088,128]{1,0:T(8,128)(2,1)S(1)}, u32[]{:S(2)}, u32[]{:S(2)}) collective-permute-start(bf16[1088,128]{1,0:T(8,128)(2,1)S(1)} %get-tuple-element.19.own.msg), channel_id=1, source_target_pairs={{4,0},{5,1},{6,2},{7,3},{0,4},{1,5},{2,6},{3,7},{12,8},{13,9},{14,... | collective-permute-start | bytes 835592 | tf_op jit(solution)/shard_map/ppermute | solution.py:73
  6.0 6.3 %collective-permute-start.2 = (bf16[256,256]{1,0:T(8,128)(2,1)S(1)}, bf16[256,256]{1,0:T(8,128)(2,1)S(1)}, u32[]{:S(2)}, u32[]{:S(2)}) collective-permute-start(bf16[256,256]{1,0:T(8,128)(2,1)S(1)} %get-tuple-element.20.kv), channel_id=1, source_target_pairs={{432,0},{467,1},{434,2},{465,3},{454,4},{421,5},{452,6},{423,7},{4... | collective-permute-start | bytes 393224 | tf_op jit(solution)/shard_map/ppermute | solution.py:73
  12.2 6.8 %collective-permute-start.1 = (bf16[256,256]{1,0:T(8,128)(2,1)S(1)}, bf16[256,256]{1,0:T(8,128)(2,1)S(1)}, u32[]{:S(2)}, u32[]{:S(2)}) collective-permute-start(bf16[256,256]{1,0:T(8,128)(2,1)S(1)} %get-tuple-element.20.kv), channel_id=1, source_target_pairs={{498,0},{401,1},{496,2},{403,3},{388,4},{487,5},{390,6},{485,7},{5... | collective-permute-start | bytes 393224 | tf_op jit(solution)/shard_map/ppermute | solution.py:73
  19.0 0.0 collective-permute-done.y
  19.1 5.0 %collective-permute-start.3 = (bf16[2176,128]{1,0:T(8,128)(2,1)S(1)}, bf16[2176,128]{1,0:T(8,128)(2,1)S(1)}, u32[]{:S(2)}, u32[]{:S(2)}) collective-permute-start(bf16[2176,128]{1,0:T(8,128)(2,1)S(1)} %pad_maximum_fusion), channel_id=1, source_target_pairs={{1,0},{0,1},{3,2},{2,3},{5,4},{4,5},{7,6},{6,7},{9,8},{8,9},{11,10... | collective-permute-start | bytes 1671176 | tf_op jit(solution)/shard_map/ppermute | solution.py:73
  24.1 0.0 collective-permute-done.2.kv_far
  24.1 0.2 early.1
  24.3 0.5 collective-permute-done.1.kv_near
  24.8 0.9 %collective-permute-done.3.other = bf16[2176,128]{1,0:T(8,128)(2,1)S(1)} collective-permute-done((bf16[2176,128]{1,0:T(8,128)(2,1)S(1)}, bf16[2176,128]{1,0:T(8,128)(2,1)S(1)}, u32[]{:S(2)}, u32[]{:S(2)}) %collective-permute-start.3) | collective-permute-done | bytes 557088 | tf_op jit(solution)/shard_map/ppermute | solution.py:73
  25.7 0.2 late.1
  25.9 10.1 %collective-permute-start.6 = (bf16[256,256]{1,0:T(8,128)(2,1)S(1)}, bf16[256,256]{1,0:T(8,128)(2,1)S(1)}, u32[]{:S(2)}, u32[]{:S(2)}) collective-permute-start(bf16[256,256]{1,0:T(8,128)(2,1)S(1)} %get-tuple-element.31), channel_id=1, source_target_pairs={{0,432},{1,467},{2,434},{3,465},{4,454},{5,421},{6,452},{7,423},{8... | collective-permute-start | bytes 393224 | tf_op jit(solution)/shard_map/ppermute | solution.py:73
  36.0 1.9 %collective-permute-start.7 = (bf16[256,256]{1,0:T(8,128)(2,1)S(1)}, bf16[256,256]{1,0:T(8,128)(2,1)S(1)}, u32[]{:S(2)}, u32[]{:S(2)}) collective-permute-start(bf16[256,256]{1,0:T(8,128)(2,1)S(1)} %get-tuple-element.32), channel_id=1, source_target_pairs={{0,498},{1,401},{2,496},{3,403},{4,388},{5,487},{6,390},{7,485},{8... | collective-permute-start | bytes 393224 | tf_op jit(solution)/shard_map/ppermute | solution.py:73
  37.9 0.7 %own.1 = (f32[256,256]{1,0:T(8,128)S(1)}, f32[512,128]{1,0:T(8,128)S(1)}, f32[512,128]{1,0:T(8,128)S(1)}, bf16[1024,128]{1,0:T(8,128)(2,1)S(1)}) custom-call(bf16[1088,128]{1,0:T(8,128)(2,1)S(1)} %get-tuple-element.19.own.msg, bf16[256,256]{1,0:T(8,128)(2,1)S(1)} %get-tuple-element.20.kv, f32[8,256]{1,0:T(8,128)S(1)} %get-tuple-element.21.aux, ...), custom_call_target="tpu_custom_call" | custom-call | flops 268435456 | bytes 1048576 | tf_op jit(solution)/shard_map/own/pallas_call | solution.py:317
  38.6 2.1 %collective-permute-start.4 = (bf16[1024,128]{1,0:T(8,128)(2,1)S(1)}, bf16[1024,128]{1,0:T(8,128)(2,1)S(1)}, u32[]{:S(2)}, u32[]{:S(2)}) collective-permute-start(bf16[1024,128]{1,0:T(8,128)(2,1)S(1)} %get-tuple-element.27), channel_id=1, source_target_pairs={{4,0},{5,1},{6,2},{7,3},{0,4},{1,5},{2,6},{3,7},{12,8},{13,9},{14,... | collective-permute-start | bytes 786440 | tf_op jit(solution)/shard_map/ppermute | solution.py:73
  40.7 0.0 collective-permute-done.6.far
  40.7 2.2 %collective-permute-done.7.near = bf16[256,256]{1,0:T(8,128)(2,1)S(1)} collective-permute-done((bf16[256,256]{1,0:T(8,128)(2,1)S(1)}, bf16[256,256]{1,0:T(8,128)(2,1)S(1)}, u32[]{:S(2)}, u32[]{:S(2)}) %collective-permute-start.7) | collective-permute-done | bytes 131104 | tf_op jit(solution)/shard_map/ppermute | solution.py:73
  42.9 0.7 %terms.1 = bf16[16,16,256]{2,1,0:T(8,128)(2,1)} custom-call(f32[256,256]{1,0:T(8,128)S(1)} %get-tuple-element.30.own, bf16[256,256]{1,0:T(8,128)(2,1)S(1)} %collective-permute-done.6.far, bf16[256,256]{1,0:T(8,128)(2,1)S(1)} %collective-permute-done.7.near), custom_call_target="tpu_custom_call" | custom-call | flops 17179869184 | bytes 1048576 | tf_op jit(solution)/shard_map/terms/pallas_call | solution.py:317
  43.6 14.8 %all-to-all-start = ((bf16[16,16,256]{2,1,0:T(8,128)(2,1)}), bf16[16,16,256]{2,1,0:T(8,128)(2,1)S(1)}, u32[]{:S(2)}, u32[]{:S(2)}) async-start(bf16[16,16,256]{2,1,0:T(8,128)(2,1)} %terms.1), calls=%async_computation | async-start | bytes 262144 | tf_op jit(solution)/shard_map/all_to_all | solution.py:467
  58.5 2.3 %collective-permute-start.5 = (bf16[512,128]{1,0:T(8,128)(2,1)S(1)}, bf16[512,128]{1,0:T(8,128)(2,1)S(1)}, u32[]{:S(2)}, u32[]{:S(2)}) collective-permute-start(bf16[512,128]{1,0:T(8,128)(2,1)S(1)} %get-tuple-element.29), channel_id=1, source_target_pairs={{1,0},{0,1},{3,2},{2,3},{5,4},{4,5},{7,6},{6,7},{9,8},{8,9},{11,10... | collective-permute-start | bytes 393224 | tf_op jit(solution)/shard_map/ppermute | solution.py:73
  60.8 1.0 %collective-permute-done.5.dq_core = bf16[512,128]{1,0:T(8,128)(2,1)S(1)} collective-permute-done((bf16[512,128]{1,0:T(8,128)(2,1)S(1)}, bf16[512,128]{1,0:T(8,128)(2,1)S(1)}, u32[]{:S(2)}, u32[]{:S(2)}) %collective-permute-start.5) | collective-permute-done | bytes 131104 | tf_op jit(solution)/shard_map/ppermute | solution.py:73
  61.7 0.7 %query.1 = bf16[256,256]{1,0:T(8,128)(2,1)} custom-call(f32[512,128]{1,0:T(8,128)S(1)} %get-tuple-element.28.part, bf16[512,128]{1,0:T(8,128)(2,1)S(1)} %collective-permute-done.5.dq_core), custom_call_target="tpu_custom_call" | custom-call | flops 134217728 | bytes 1048576 | tf_op jit(solution)/shard_map/query/pallas_call | solution.py:317
  62.4 1.2 %all-to-all-done.terms = bf16[16,16,256]{2,1,0:T(8,128)(2,1)S(1)} async-done(((bf16[16,16,256]{2,1,0:T(8,128)(2,1)}), bf16[16,16,256]{2,1,0:T(8,128)(2,1)S(1)}, u32[]{:S(2)}, u32[]{:S(2)}) %all-to-all-start) | async-done | bytes 131104 | tf_op jit(solution)/shard_map/all_to_all | solution.py:467
  63.7 0.6 key_value.1
  (3 shorter events, 0.1 us)
Async XLA Ops:
  1.9 17.1 %collective-permute-start = (bf16[1088,128]{1,0:T(8,128)(2,1)S(1)}, bf16[1088,128]{1,0:T(8,128)(2,1)S(1)}, u32[]{:S(2)}, u32[]{:S(2)}) collective-permute-start(bf16[1088,128]{1,0:T(8,128)(2,1)S(1)} %get-tuple-element.19.own.msg), channel_id=1, source_target_pairs={{4,0},{5,1},{6,2},{7,3},{0,4},{1,5},{2,6},{3,7},{12,8},{13,9},{14,... | collective-permute-start | bytes 835592 | tf_op jit(solution)/shard_map/ppermute | solution.py:73
  6.0 18.2 %collective-permute-start.2 = (bf16[256,256]{1,0:T(8,128)(2,1)S(1)}, bf16[256,256]{1,0:T(8,128)(2,1)S(1)}, u32[]{:S(2)}, u32[]{:S(2)}) collective-permute-start(bf16[256,256]{1,0:T(8,128)(2,1)S(1)} %get-tuple-element.20.kv), channel_id=1, source_target_pairs={{432,0},{467,1},{434,2},{465,3},{454,4},{421,5},{452,6},{423,7},{4... | collective-permute-start | bytes 393224 | tf_op jit(solution)/shard_map/ppermute | solution.py:73
  12.2 12.6 %collective-permute-start.1 = (bf16[256,256]{1,0:T(8,128)(2,1)S(1)}, bf16[256,256]{1,0:T(8,128)(2,1)S(1)}, u32[]{:S(2)}, u32[]{:S(2)}) collective-permute-start(bf16[256,256]{1,0:T(8,128)(2,1)S(1)} %get-tuple-element.20.kv), channel_id=1, source_target_pairs={{498,0},{401,1},{496,2},{403,3},{388,4},{487,5},{390,6},{485,7},{5... | collective-permute-start | bytes 393224 | tf_op jit(solution)/shard_map/ppermute | solution.py:73
  19.1 6.6 %collective-permute-start.3 = (bf16[2176,128]{1,0:T(8,128)(2,1)S(1)}, bf16[2176,128]{1,0:T(8,128)(2,1)S(1)}, u32[]{:S(2)}, u32[]{:S(2)}) collective-permute-start(bf16[2176,128]{1,0:T(8,128)(2,1)S(1)} %pad_maximum_fusion), channel_id=1, source_target_pairs={{1,0},{0,1},{3,2},{2,3},{5,4},{4,5},{7,6},{6,7},{9,8},{8,9},{11,10... | collective-permute-start | bytes 1671176 | tf_op jit(solution)/shard_map/ppermute | solution.py:73
  25.9 14.8 %collective-permute-start.6 = (bf16[256,256]{1,0:T(8,128)(2,1)S(1)}, bf16[256,256]{1,0:T(8,128)(2,1)S(1)}, u32[]{:S(2)}, u32[]{:S(2)}) collective-permute-start(bf16[256,256]{1,0:T(8,128)(2,1)S(1)} %get-tuple-element.31), channel_id=1, source_target_pairs={{0,432},{1,467},{2,434},{3,465},{4,454},{5,421},{6,452},{7,423},{8... | collective-permute-start | bytes 393224 | tf_op jit(solution)/shard_map/ppermute | solution.py:73
  36.0 6.9 %collective-permute-start.7 = (bf16[256,256]{1,0:T(8,128)(2,1)S(1)}, bf16[256,256]{1,0:T(8,128)(2,1)S(1)}, u32[]{:S(2)}, u32[]{:S(2)}) collective-permute-start(bf16[256,256]{1,0:T(8,128)(2,1)S(1)} %get-tuple-element.32), channel_id=1, source_target_pairs={{0,498},{1,401},{2,496},{3,403},{4,388},{5,487},{6,390},{7,485},{8... | collective-permute-start | bytes 393224 | tf_op jit(solution)/shard_map/ppermute | solution.py:73
  38.6 19.8 %collective-permute-start.4 = (bf16[1024,128]{1,0:T(8,128)(2,1)S(1)}, bf16[1024,128]{1,0:T(8,128)(2,1)S(1)}, u32[]{:S(2)}, u32[]{:S(2)}) collective-permute-start(bf16[1024,128]{1,0:T(8,128)(2,1)S(1)} %get-tuple-element.27), channel_id=1, source_target_pairs={{4,0},{5,1},{6,2},{7,3},{0,4},{1,5},{2,6},{3,7},{12,8},{13,9},{14,... | collective-permute-start | bytes 786440 | tf_op jit(solution)/shard_map/ppermute | solution.py:73
  43.6 20.1 %all-to-all-start = ((bf16[16,16,256]{2,1,0:T(8,128)(2,1)}), bf16[16,16,256]{2,1,0:T(8,128)(2,1)S(1)}, u32[]{:S(2)}, u32[]{:S(2)}) async-start(bf16[16,16,256]{2,1,0:T(8,128)(2,1)} %terms.1), calls=%async_computation | async-start | bytes 262144 | tf_op jit(solution)/shard_map/all_to_all | solution.py:467
  58.5 3.2 %collective-permute-start.5 = (bf16[512,128]{1,0:T(8,128)(2,1)S(1)}, bf16[512,128]{1,0:T(8,128)(2,1)S(1)}, u32[]{:S(2)}, u32[]{:S(2)}) collective-permute-start(bf16[512,128]{1,0:T(8,128)(2,1)S(1)} %get-tuple-element.29), channel_id=1, source_target_pairs={{1,0},{0,1},{3,2},{2,3},{5,4},{4,5},{7,6},{6,7},{9,8},{8,9},{11,10... | collective-permute-start | bytes 393224 | tf_op jit(solution)/shard_map/ppermute | solution.py:73

commit v9 on v8

--- a/solution.py
+++ b/solution.py
@@ -217,7 +217,9 @@
 def probs_and_dscores(key_block, value_block, msg, rate, visible):
     lse2, const = row_terms(msg)
     scores = nt(key_block, msg[: 2 * ROWS, :])
-    probs = jnp.where(visible, jnp.exp2(scores * (SCALE * LOG2E) - lse2), 0.0)
+    probs = jnp.exp2(scores * (SCALE * LOG2E) - lse2)
+    if visible is not None:
+        probs = jnp.where(visible, probs, 0.0)
     dprobs = nt(value_block, msg[2 * ROWS : 4 * ROWS, :])
     dscores = probs * (dprobs - const - scores * rate)
     return probs.astype(BF16), dscores.astype(BF16)
@@ -247,17 +249,22 @@
     return start - key_start, key_start + (ROWS - 1) >= jnp.min(start)
 
 
-def earlier_sums(table, messages, kv, aux, put):
-    reach, _ = block_place(table, aux[0:1, :])
-    key_at = lax.broadcasted_iota(jnp.int32, (ROWS, 2 * ROWS), 0).astype(F32)
-    return sums_of(
-        messages,
-        kv[:, :HD],
-        kv[:, HD:],
-        both(aux[1:2, :] * SCALE),
-        key_at >= both(reach),
-        put,
-    )
+def earlier_sums(table, messages, kv, aux, put, put_sums):
+    reach, seen = block_place(table, aux[0:1, :])
+    whole = jnp.max(reach) <= 0.0
+
+    def run(visible):
+        rate = both(aux[1:2, :] * SCALE)
+        put_sums(*sums_of(messages, kv[:, :HD], kv[:, HD:], rate, visible, put))
+
+    @pl.when(seen & whole)
+    def _():
+        run(None)
+
+    @pl.when(seen & jnp.logical_not(whole))
+    def _():
+        key_at = lax.broadcasted_iota(jnp.int32, (ROWS, 2 * ROWS), 0).astype(F32)
+        run(key_at >= both(reach))
 
 
 def early_kernel(own, y, kv_far, aux, far, dq):
@@ -268,14 +275,14 @@
         dq[...] = jnp.zeros_like(dq)
         far[...] = jnp.zeros_like(far)
 
-    @pl.when(seen)
-    def _():
-        def put(n, query_sum):
-            dq[n] = query_sum
-
-        key_sum, value_sum = earlier_sums(FAR, (own, y), kv_far, aux, put)
+    def put(n, query_sum):
+        dq[n] = query_sum
+
+    def put_sums(key_sum, value_sum):
         far[:, :HD] = key_sum
         far[:, HD:] = value_sum
+
+    earlier_sums(FAR, (own, y), kv_far, aux, put, put_sums)
 
 
 def late_kernel(own, y, kv_near, kv_far, other, aux, far_in, dq_in, far, near, dq):
@@ -289,27 +296,27 @@
         dq[2:] = jnp.zeros_like(dq[2:])
         near[...] = jnp.zeros_like(near)
 
-    @pl.when(near_seen)
-    def _():
-        def put(n, query_sum):
-            dq[n] = dq_in[n] + query_sum if n < 2 else query_sum
-
-        key_sum, value_sum = earlier_sums(NEAR, (own, y, core, cross), kv_near, aux, put)
+    def put_near(n, query_sum):
+        dq[n] = dq_in[n] + query_sum if n < 2 else query_sum
+
+    def put_near_sums(key_sum, value_sum):
         near[:, :HD] = key_sum.astype(BF16)
         near[:, HD:] = value_sum.astype(BF16)
+
+    earlier_sums(NEAR, (own, y, core, cross), kv_near, aux, put_near, put_near_sums)
 
     @pl.when(jnp.logical_not(far_seen))
     def _():
         far[...] = far_in[...].astype(BF16)
 
-    @pl.when(far_seen)
-    def _():
-        def put(n, query_sum):
-            dq[2 + n] += query_sum
-
-        key_sum, value_sum = earlier_sums(FAR, (core, cross), kv_far, aux, put)
+    def put_far(n, query_sum):
+        dq[2 + n] += query_sum
+
+    def put_far_sums(key_sum, value_sum):
         far[:, :HD] = (far_in[:, :HD] + key_sum).astype(BF16)
         far[:, HD:] = (far_in[:, HD:] + value_sum).astype(BF16)
+
+    earlier_sums(FAR, (core, cross), kv_far, aux, put_far, put_far_sums)
 
 
 def kernel_call(kernel, name, out_shape, flops, *arrays):

time: 65 us -> 65.5 us (level)
  waiting for transfers between devices: 5.74 us -> 4.4 us
  starting transfers between devices: 53.3 us -> 54.2 us
    all_to_all x1, starting transfers between devices: 14.8 us -> 17.5 us  [local(): terms = lax.all_to_all(terms, 'head', 0, 0, axis_index_groups=[HEAD_ORDER])]
    ppermute x8, starting transfers between devices: 38.5 us -> 36.8 us  [moved(): return lax.ppermute(value, ('blk', 'head'), pairs)]
    ppermute x8, waiting for transfers between devices: 4.5 us -> 3.16 us  [moved(): return lax.ppermute(value, ('blk', 'head'), pairs)]
where the time goes in v9:
time: 65.5 us; the launch traced here: 64.3 us
  starting transfers between devices  54.2 us (83%)
  Pallas kernels  4.79 us (7%)
  waiting for transfers between devices  4.4 us (7%)
  between operations  0.78 us (1%)
    ppermute x8, starting transfers between devices, moved(): return lax.ppermute(value, ('blk', 'head'), pairs)  36.8 us
    all_to_all x1, starting transfers between devices, local(): terms = lax.all_to_all(terms, 'head', 0, 0, axis_index_groups=[HEAD_ORDER])  17.5 us
    pallas_call x7, Pallas kernels, kernel_call(): pl.pallas_call(kernel, out_shape=out_shape, in_specs=[vmem] * len(arrays)...  3.52 us
    ppermute x8, waiting for transfers between devices, moved(): return lax.ppermute(value, ('blk', 'head'), pairs)  3.16 us
  transfers between devices with their start and end apart: 9, of which 5 were waited for; matrix products, arithmetic and copies ran while one was open for 0% of the time, Pallas kernels for 4%

profile of v9, /device:TPU:1, one launch (start us, length us, event | category | flops | bytes accessed | tf_op | source)
XLA Modules:
  0.0 64.3 jit_solution(5860004955645990863)
XLA Ops:
  0.6 1.3 %prep.1 = (bf16[1088,128]{1,0:T(8,128)(2,1)S(1)}, bf16[256,256]{1,0:T(8,128)(2,1)S(1)}, f32[8,256]{1,0:T(8,128)S(1)}) custom-call(bf16[256,256]{1,0:T(8,128)(2,1)} %q_in.1, bf16[256,256]{1,0:T(8,128)(2,1)} %k_in.1, bf16[256,256]{1,0:T(8,128)(2,1)} %v_in.1, bf16[256,256]{1,0:T(8,128)(2,1)} %o_in.1, bf16[256,256]{1,0:T(8,128)(2,1)} %do_in.1, f32[2,256]{1,0:T(2,128)} %lse_in.1, ...), custom_call_target="tpu_custom_call" | custom-call | tf_op jit(solution)/shard_map/prep/pallas_call | solution.py:182
  1.9 4.0 %collective-permute-start = (bf16[1088,128]{1,0:T(8,128)(2,1)S(1)}, bf16[1088,128]{1,0:T(8,128)(2,1)S(1)}, u32[]{:S(2)}, u32[]{:S(2)}) collective-permute-start(bf16[1088,128]{1,0:T(8,128)(2,1)S(1)} %get-tuple-element.19.own.msg), channel_id=1, source_target_pairs={{4,0},{5,1},{6,2},{7,3},{0,4},{1,5},{2,6},{3,7},{12,8},{13,9},{14,... | collective-permute-start | bytes 835592 | tf_op jit(solution)/shard_map/ppermute | solution.py:73
  6.0 6.3 %collective-permute-start.2 = (bf16[256,256]{1,0:T(8,128)(2,1)S(1)}, bf16[256,256]{1,0:T(8,128)(2,1)S(1)}, u32[]{:S(2)}, u32[]{:S(2)}) collective-permute-start(bf16[256,256]{1,0:T(8,128)(2,1)S(1)} %get-tuple-element.20.kv), channel_id=1, source_target_pairs={{432,0},{467,1},{434,2},{465,3},{454,4},{421,5},{452,6},{423,7},{4... | collective-permute-start | bytes 393224 | tf_op jit(solution)/shard_map/ppermute | solution.py:73
  12.2 6.8 %collective-permute-start.1 = (bf16[256,256]{1,0:T(8,128)(2,1)S(1)}, bf16[256,256]{1,0:T(8,128)(2,1)S(1)}, u32[]{:S(2)}, u32[]{:S(2)}) collective-permute-start(bf16[256,256]{1,0:T(8,128)(2,1)S(1)} %get-tuple-element.20.kv), channel_id=1, source_target_pairs={{498,0},{401,1},{496,2},{403,3},{388,4},{487,5},{390,6},{485,7},{5... | collective-permute-start | bytes 393224 | tf_op jit(solution)/shard_map/ppermute | solution.py:73
  19.0 0.0 collective-permute-done.y
  19.1 5.0 %collective-permute-start.3 = (bf16[2176,128]{1,0:T(8,128)(2,1)S(1)}, bf16[2176,128]{1,0:T(8,128)(2,1)S(1)}, u32[]{:S(2)}, u32[]{:S(2)}) collective-permute-start(bf16[2176,128]{1,0:T(8,128)(2,1)S(1)} %pad_maximum_fusion), channel_id=1, source_target_pairs={{1,0},{0,1},{3,2},{2,3},{5,4},{4,5},{7,6},{6,7},{9,8},{8,9},{11,10... | collective-permute-start | bytes 1671176 | tf_op jit(solution)/shard_map/ppermute | solution.py:73
  24.1 0.0 collective-permute-done.2.kv_far
  24.1 0.3 early.1
  24.4 0.4 collective-permute-done.1.kv_near
  24.8 0.9 %collective-permute-done.3.other = bf16[2176,128]{1,0:T(8,128)(2,1)S(1)} collective-permute-done((bf16[2176,128]{1,0:T(8,128)(2,1)S(1)}, bf16[2176,128]{1,0:T(8,128)(2,1)S(1)}, u32[]{:S(2)}, u32[]{:S(2)}) %collective-permute-start.3) | collective-permute-done | bytes 557088 | tf_op jit(solution)/shard_map/ppermute | solution.py:73
  25.7 0.5 late.1
  26.2 6.8 %collective-permute-start.6 = (bf16[256,256]{1,0:T(8,128)(2,1)S(1)}, bf16[256,256]{1,0:T(8,128)(2,1)S(1)}, u32[]{:S(2)}, u32[]{:S(2)}) collective-permute-start(bf16[256,256]{1,0:T(8,128)(2,1)S(1)} %get-tuple-element.31), channel_id=1, source_target_pairs={{0,432},{1,467},{2,434},{3,465},{4,454},{5,421},{6,452},{7,423},{8... | collective-permute-start | bytes 393224 | tf_op jit(solution)/shard_map/ppermute | solution.py:73
  33.0 3.6 %collective-permute-start.7 = (bf16[256,256]{1,0:T(8,128)(2,1)S(1)}, bf16[256,256]{1,0:T(8,128)(2,1)S(1)}, u32[]{:S(2)}, u32[]{:S(2)}) collective-permute-start(bf16[256,256]{1,0:T(8,128)(2,1)S(1)} %get-tuple-element.32), channel_id=1, source_target_pairs={{0,498},{1,401},{2,496},{3,403},{4,388},{5,487},{6,390},{7,485},{8... | collective-permute-start | bytes 393224 | tf_op jit(solution)/shard_map/ppermute | solution.py:73
  36.7 0.7 %own.1 = (f32[256,256]{1,0:T(8,128)S(1)}, f32[512,128]{1,0:T(8,128)S(1)}, f32[512,128]{1,0:T(8,128)S(1)}, bf16[1024,128]{1,0:T(8,128)(2,1)S(1)}) custom-call(bf16[1088,128]{1,0:T(8,128)(2,1)S(1)} %get-tuple-element.19.own.msg, bf16[256,256]{1,0:T(8,128)(2,1)S(1)} %get-tuple-element.20.kv, f32[8,256]{1,0:T(8,128)S(1)} %get-tuple-element.21.aux, ...), custom_call_target="tpu_custom_call" | custom-call | flops 268435456 | bytes 1048576 | tf_op jit(solution)/shard_map/own/pallas_call | solution.py:324
  37.3 1.9 %collective-permute-start.4 = (bf16[1024,128]{1,0:T(8,128)(2,1)S(1)}, bf16[1024,128]{1,0:T(8,128)(2,1)S(1)}, u32[]{:S(2)}, u32[]{:S(2)}) collective-permute-start(bf16[1024,128]{1,0:T(8,128)(2,1)S(1)} %get-tuple-element.27), channel_id=1, source_target_pairs={{4,0},{5,1},{6,2},{7,3},{0,4},{1,5},{2,6},{3,7},{12,8},{13,9},{14,... | collective-permute-start | bytes 786440 | tf_op jit(solution)/shard_map/ppermute | solution.py:73
  39.3 0.9 %collective-permute-done.7.near = bf16[256,256]{1,0:T(8,128)(2,1)S(1)} collective-permute-done((bf16[256,256]{1,0:T(8,128)(2,1)S(1)}, bf16[256,256]{1,0:T(8,128)(2,1)S(1)}, u32[]{:S(2)}, u32[]{:S(2)}) %collective-permute-start.7) | collective-permute-done | bytes 131104 | tf_op jit(solution)/shard_map/ppermute | solution.py:73
  40.2 0.7 %terms.1 = bf16[16,16,256]{2,1,0:T(8,128)(2,1)} custom-call(f32[256,256]{1,0:T(8,128)S(1)} %get-tuple-element.30.own, bf16[256,256]{1,0:T(8,128)(2,1)S(1)} %collective-permute-done.6.far, bf16[256,256]{1,0:T(8,128)(2,1)S(1)} %collective-permute-done.7.near), custom_call_target="tpu_custom_call" | custom-call | flops 17179869184 | bytes 1048576 | tf_op jit(solution)/shard_map/terms/pallas_call | solution.py:324
  40.9 17.5 %all-to-all-start = ((bf16[16,16,256]{2,1,0:T(8,128)(2,1)}), bf16[16,16,256]{2,1,0:T(8,128)(2,1)S(1)}, u32[]{:S(2)}, u32[]{:S(2)}) async-start(bf16[16,16,256]{2,1,0:T(8,128)(2,1)} %terms.1), calls=%async_computation | async-start | bytes 262144 | tf_op jit(solution)/shard_map/all_to_all | solution.py:474
  58.4 0.0 collective-permute-done.4.dq_y
  58.5 2.3 %collective-permute-start.5 = (bf16[512,128]{1,0:T(8,128)(2,1)S(1)}, bf16[512,128]{1,0:T(8,128)(2,1)S(1)}, u32[]{:S(2)}, u32[]{:S(2)}) collective-permute-start(bf16[512,128]{1,0:T(8,128)(2,1)S(1)} %get-tuple-element.29), channel_id=1, source_target_pairs={{1,0},{0,1},{3,2},{2,3},{5,4},{4,5},{7,6},{6,7},{9,8},{8,9},{11,10... | collective-permute-start | bytes 393224 | tf_op jit(solution)/shard_map/ppermute | solution.py:73
  60.7 1.0 %collective-permute-done.5.dq_core = bf16[512,128]{1,0:T(8,128)(2,1)S(1)} collective-permute-done((bf16[512,128]{1,0:T(8,128)(2,1)S(1)}, bf16[512,128]{1,0:T(8,128)(2,1)S(1)}, u32[]{:S(2)}, u32[]{:S(2)}) %collective-permute-start.5) | collective-permute-done | bytes 131104 | tf_op jit(solution)/shard_map/ppermute | solution.py:73
  61.7 0.7 %query.1 = bf16[256,256]{1,0:T(8,128)(2,1)} custom-call(f32[512,128]{1,0:T(8,128)S(1)} %get-tuple-element.28.part, bf16[512,128]{1,0:T(8,128)(2,1)S(1)} %collective-permute-done.5.dq_core), custom_call_target="tpu_custom_call" | custom-call | flops 134217728 | bytes 1048576 | tf_op jit(solution)/shard_map/query/pallas_call | solution.py:324
  62.4 1.2 %all-to-all-done.terms = bf16[16,16,256]{2,1,0:T(8,128)(2,1)S(1)} async-done(((bf16[16,16,256]{2,1,0:T(8,128)(2,1)}), bf16[16,16,256]{2,1,0:T(8,128)(2,1)S(1)}, u32[]{:S(2)}, u32[]{:S(2)}) %all-to-all-start) | async-done | bytes 131104 | tf_op jit(solution)/shard_map/all_to_all | solution.py:474
  63.6 0.6 key_value.1
  (3 shorter events, 0.1 us)
Async XLA Ops:
  1.9 17.1 %collective-permute-start = (bf16[1088,128]{1,0:T(8,128)(2,1)S(1)}, bf16[1088,128]{1,0:T(8,128)(2,1)S(1)}, u32[]{:S(2)}, u32[]{:S(2)}) collective-permute-start(bf16[1088,128]{1,0:T(8,128)(2,1)S(1)} %get-tuple-element.19.own.msg), channel_id=1, source_target_pairs={{4,0},{5,1},{6,2},{7,3},{0,4},{1,5},{2,6},{3,7},{12,8},{13,9},{14,... | collective-permute-start | bytes 835592 | tf_op jit(solution)/shard_map/ppermute | solution.py:73
  6.0 18.2 %collective-permute-start.2 = (bf16[256,256]{1,0:T(8,128)(2,1)S(1)}, bf16[256,256]{1,0:T(8,128)(2,1)S(1)}, u32[]{:S(2)}, u32[]{:S(2)}) collective-permute-start(bf16[256,256]{1,0:T(8,128)(2,1)S(1)} %get-tuple-element.20.kv), channel_id=1, source_target_pairs={{432,0},{467,1},{434,2},{465,3},{454,4},{421,5},{452,6},{423,7},{4... | collective-permute-start | bytes 393224 | tf_op jit(solution)/shard_map/ppermute | solution.py:73
  12.2 12.6 %collective-permute-start.1 = (bf16[256,256]{1,0:T(8,128)(2,1)S(1)}, bf16[256,256]{1,0:T(8,128)(2,1)S(1)}, u32[]{:S(2)}, u32[]{:S(2)}) collective-permute-start(bf16[256,256]{1,0:T(8,128)(2,1)S(1)} %get-tuple-element.20.kv), channel_id=1, source_target_pairs={{498,0},{401,1},{496,2},{403,3},{388,4},{487,5},{390,6},{485,7},{5... | collective-permute-start | bytes 393224 | tf_op jit(solution)/shard_map/ppermute | solution.py:73
  19.1 6.6 %collective-permute-start.3 = (bf16[2176,128]{1,0:T(8,128)(2,1)S(1)}, bf16[2176,128]{1,0:T(8,128)(2,1)S(1)}, u32[]{:S(2)}, u32[]{:S(2)}) collective-permute-start(bf16[2176,128]{1,0:T(8,128)(2,1)S(1)} %pad_maximum_fusion), channel_id=1, source_target_pairs={{1,0},{0,1},{3,2},{2,3},{5,4},{4,5},{7,6},{6,7},{9,8},{8,9},{11,10... | collective-permute-start | bytes 1671176 | tf_op jit(solution)/shard_map/ppermute | solution.py:73
  26.2 13.1 %collective-permute-start.6 = (bf16[256,256]{1,0:T(8,128)(2,1)S(1)}, bf16[256,256]{1,0:T(8,128)(2,1)S(1)}, u32[]{:S(2)}, u32[]{:S(2)}) collective-permute-start(bf16[256,256]{1,0:T(8,128)(2,1)S(1)} %get-tuple-element.31), channel_id=1, source_target_pairs={{0,432},{1,467},{2,434},{3,465},{4,454},{5,421},{6,452},{7,423},{8... | collective-permute-start | bytes 393224 | tf_op jit(solution)/shard_map/ppermute | solution.py:73
  33.0 7.2 %collective-permute-start.7 = (bf16[256,256]{1,0:T(8,128)(2,1)S(1)}, bf16[256,256]{1,0:T(8,128)(2,1)S(1)}, u32[]{:S(2)}, u32[]{:S(2)}) collective-permute-start(bf16[256,256]{1,0:T(8,128)(2,1)S(1)} %get-tuple-element.32), channel_id=1, source_target_pairs={{0,498},{1,401},{2,496},{3,403},{4,388},{5,487},{6,390},{7,485},{8... | collective-permute-start | bytes 393224 | tf_op jit(solution)/shard_map/ppermute | solution.py:73
  37.3 21.0 %collective-permute-start.4 = (bf16[1024,128]{1,0:T(8,128)(2,1)S(1)}, bf16[1024,128]{1,0:T(8,128)(2,1)S(1)}, u32[]{:S(2)}, u32[]{:S(2)}) collective-permute-start(bf16[1024,128]{1,0:T(8,128)(2,1)S(1)} %get-tuple-element.27), channel_id=1, source_target_pairs={{4,0},{5,1},{6,2},{7,3},{0,4},{1,5},{2,6},{3,7},{12,8},{13,9},{14,... | collective-permute-start | bytes 786440 | tf_op jit(solution)/shard_map/ppermute | solution.py:73
  40.9 22.7 %all-to-all-start = ((bf16[16,16,256]{2,1,0:T(8,128)(2,1)}), bf16[16,16,256]{2,1,0:T(8,128)(2,1)S(1)}, u32[]{:S(2)}, u32[]{:S(2)}) async-start(bf16[16,16,256]{2,1,0:T(8,128)(2,1)} %terms.1), calls=%async_computation | async-start | bytes 262144 | tf_op jit(solution)/shard_map/all_to_all | solution.py:474
  58.5 3.2 %collective-permute-start.5 = (bf16[512,128]{1,0:T(8,128)(2,1)S(1)}, bf16[512,128]{1,0:T(8,128)(2,1)S(1)}, u32[]{:S(2)}, u32[]{:S(2)}) collective-permute-start(bf16[512,128]{1,0:T(8,128)(2,1)S(1)} %get-tuple-element.29), channel_id=1, source_target_pairs={{1,0},{0,1},{3,2},{2,3},{5,4},{4,5},{7,6},{6,7},{9,8},{8,9},{11,10... | collective-permute-start | bytes 393224 | tf_op jit(solution)/shard_map/ppermute | solution.py:73

commit v10 on v8

--- a/solution.py
+++ b/solution.py
@@ -362,7 +362,7 @@
         grad_query[:, h * HD : (h + 1) * HD] = (total * SCALE).astype(BF16)
 
 
-def terms_kernel(own, far, near, terms):
+def terms_kernel(own, near, far, terms):
     share = terms.shape[1]
     for n, head in enumerate(HEAD_ORDER):
         at = slice(head * share, (head + 1) * share)
@@ -463,7 +463,7 @@
     )
     dq_core = moved(dq_core, to_core)
     share = jax.ShapeDtypeStruct((16, ROWS // 16, 2 * HD), BF16)
-    (terms,) = kernel_call(terms_kernel, "terms", (share,), TERMS_FLOPS, dkv_own, got_far, got_near)
+    (terms,) = kernel_call(terms_kernel, "terms", (share,), TERMS_FLOPS, dkv_own, got_near, got_far)
     terms = lax.all_to_all(terms, "head", 0, 0, axis_index_groups=[HEAD_ORDER])
     (grad_query,) = kernel_call(query_kernel, "query", (pair,), QUERY_FLOPS, dq_part, dq_core)
     result = jax.ShapeDtypeStruct((terms.shape[1], 2 * HD), BF16)

time: 65 us -> 68.3 us (1.051)
  the two profiles are of different devices: /device:TPU:1 before, /device:TPU:39 now
where the time goes in v10:
time: 68.3 us; the launch traced here: 68 us
  starting transfers between devices  55.3 us (81%)
  waiting for transfers between devices  7.46 us (11%)
  Pallas kernels  4.42 us (6%)
  between operations  0.79 us (1%)
    ppermute x8, starting transfers between devices, moved(): return lax.ppermute(value, ('blk', 'head'), pairs)  35.8 us
    all_to_all x1, starting transfers between devices, local(): terms = lax.all_to_all(terms, 'head', 0, 0, axis_index_groups=[HEAD_ORDER])  19.5 us
    all_to_all x1, waiting for transfers between devices, local(): terms = lax.all_to_all(terms, 'head', 0, 0, axis_index_groups=[HEAD_ORDER])  5.12 us
    pallas_call x7, Pallas kernels, kernel_call(): pl.pallas_call(kernel, out_shape=out_shape, in_specs=[vmem] * len(arrays)...  3.15 us
    ppermute x8, waiting for transfers between devices, moved(): return lax.ppermute(value, ('blk', 'head'), pairs)  2.34 us
  transfers between devices with their start and end apart: 9, of which 3 were waited for; matrix products, arithmetic and copies ran while one was open for 0% of the time, Pallas kernels for 3%

profile of v10, /device:TPU:39, one launch (start us, length us, event | category | flops | bytes accessed | tf_op | source)
XLA Modules:
  0.0 68.0 jit_solution(11797375423388477269)
XLA Ops:
  0.6 1.3 %prep.1 = (bf16[1088,128]{1,0:T(8,128)(2,1)S(1)}, bf16[256,256]{1,0:T(8,128)(2,1)S(1)}, f32[8,256]{1,0:T(8,128)S(1)}) custom-call(bf16[256,256]{1,0:T(8,128)(2,1)} %q_in.1, bf16[256,256]{1,0:T(8,128)(2,1)} %k_in.1, bf16[256,256]{1,0:T(8,128)(2,1)} %v_in.1, bf16[256,256]{1,0:T(8,128)(2,1)} %o_in.1, bf16[256,256]{1,0:T(8,128)(2,1)} %do_in.1, f32[2,256]{1,0:T(2,128)} %lse_in.1, ...), custom_call_target="tpu_custom_call" | custom-call | tf_op jit(solution)/shard_map/prep/pallas_call | solution.py:182
  1.9 3.2 %collective-permute-start = (bf16[1088,128]{1,0:T(8,128)(2,1)S(1)}, bf16[1088,128]{1,0:T(8,128)(2,1)S(1)}, u32[]{:S(2)}, u32[]{:S(2)}) collective-permute-start(bf16[1088,128]{1,0:T(8,128)(2,1)S(1)} %get-tuple-element.19.own.msg), channel_id=1, source_target_pairs={{4,0},{5,1},{6,2},{7,3},{0,4},{1,5},{2,6},{3,7},{12,8},{13,9},{14,... | collective-permute-start | bytes 835592 | tf_op jit(solution)/shard_map/ppermute | solution.py:73
  5.1 7.5 %collective-permute-start.2 = (bf16[256,256]{1,0:T(8,128)(2,1)S(1)}, bf16[256,256]{1,0:T(8,128)(2,1)S(1)}, u32[]{:S(2)}, u32[]{:S(2)}) collective-permute-start(bf16[256,256]{1,0:T(8,128)(2,1)S(1)} %get-tuple-element.20.kv), channel_id=1, source_target_pairs={{432,0},{467,1},{434,2},{465,3},{454,4},{421,5},{452,6},{423,7},{4... | collective-permute-start | bytes 393224 | tf_op jit(solution)/shard_map/ppermute | solution.py:73
  12.6 1.9 %collective-permute-start.1 = (bf16[256,256]{1,0:T(8,128)(2,1)S(1)}, bf16[256,256]{1,0:T(8,128)(2,1)S(1)}, u32[]{:S(2)}, u32[]{:S(2)}) collective-permute-start(bf16[256,256]{1,0:T(8,128)(2,1)S(1)} %get-tuple-element.20.kv), channel_id=1, source_target_pairs={{498,0},{401,1},{496,2},{403,3},{388,4},{487,5},{390,6},{485,7},{5... | collective-permute-start | bytes 393224 | tf_op jit(solution)/shard_map/ppermute | solution.py:73
  14.5 0.0 collective-permute-done.y
  14.6 7.8 %collective-permute-start.3 = (bf16[2176,128]{1,0:T(8,128)(2,1)S(1)}, bf16[2176,128]{1,0:T(8,128)(2,1)S(1)}, u32[]{:S(2)}, u32[]{:S(2)}) collective-permute-start(bf16[2176,128]{1,0:T(8,128)(2,1)S(1)} %pad_maximum_fusion), channel_id=1, source_target_pairs={{1,0},{0,1},{3,2},{2,3},{5,4},{4,5},{7,6},{6,7},{9,8},{8,9},{11,10... | collective-permute-start | bytes 1671176 | tf_op jit(solution)/shard_map/ppermute | solution.py:73
  22.4 0.0 collective-permute-done.2.kv_far
  22.4 0.2 early.1
  22.6 0.0 collective-permute-done.1.kv_near
  22.6 1.4 %collective-permute-done.3.other = bf16[2176,128]{1,0:T(8,128)(2,1)S(1)} collective-permute-done((bf16[2176,128]{1,0:T(8,128)(2,1)S(1)}, bf16[2176,128]{1,0:T(8,128)(2,1)S(1)}, u32[]{:S(2)}, u32[]{:S(2)}) %collective-permute-start.3) | collective-permute-done | bytes 557088 | tf_op jit(solution)/shard_map/ppermute | solution.py:73
  24.0 0.2 late.1
  24.2 4.5 %collective-permute-start.6 = (bf16[256,256]{1,0:T(8,128)(2,1)S(1)}, bf16[256,256]{1,0:T(8,128)(2,1)S(1)}, u32[]{:S(2)}, u32[]{:S(2)}) collective-permute-start(bf16[256,256]{1,0:T(8,128)(2,1)S(1)} %get-tuple-element.31), channel_id=1, source_target_pairs={{0,498},{1,401},{2,496},{3,403},{4,388},{5,487},{6,390},{7,485},{8... | collective-permute-start | bytes 393224 | tf_op jit(solution)/shard_map/ppermute | solution.py:73
  28.7 5.1 %collective-permute-start.7 = (bf16[256,256]{1,0:T(8,128)(2,1)S(1)}, bf16[256,256]{1,0:T(8,128)(2,1)S(1)}, u32[]{:S(2)}, u32[]{:S(2)}) collective-permute-start(bf16[256,256]{1,0:T(8,128)(2,1)S(1)} %get-tuple-element.32), channel_id=1, source_target_pairs={{0,432},{1,467},{2,434},{3,465},{4,454},{5,421},{6,452},{7,423},{8... | collective-permute-start | bytes 393224 | tf_op jit(solution)/shard_map/ppermute | solution.py:73
  33.7 0.7 %own.1 = (f32[256,256]{1,0:T(8,128)S(1)}, f32[512,128]{1,0:T(8,128)S(1)}, f32[512,128]{1,0:T(8,128)S(1)}, bf16[1024,128]{1,0:T(8,128)(2,1)S(1)}) custom-call(bf16[1088,128]{1,0:T(8,128)(2,1)S(1)} %get-tuple-element.19.own.msg, bf16[256,256]{1,0:T(8,128)(2,1)S(1)} %get-tuple-element.20.kv, f32[8,256]{1,0:T(8,128)S(1)} %get-tuple-element.21.aux, ...), custom_call_target="tpu_custom_call" | custom-call | flops 268435456 | bytes 1048576 | tf_op jit(solution)/shard_map/own/pallas_call | solution.py:317
  34.4 3.5 %collective-permute-start.4 = (bf16[1024,128]{1,0:T(8,128)(2,1)S(1)}, bf16[1024,128]{1,0:T(8,128)(2,1)S(1)}, u32[]{:S(2)}, u32[]{:S(2)}) collective-permute-start(bf16[1024,128]{1,0:T(8,128)(2,1)S(1)} %get-tuple-element.27), channel_id=1, source_target_pairs={{4,0},{5,1},{6,2},{7,3},{0,4},{1,5},{2,6},{3,7},{12,8},{13,9},{14,... | collective-permute-start | bytes 786440 | tf_op jit(solution)/shard_map/ppermute | solution.py:73
  38.0 0.0 collective-permute-done.7.far
  38.0 0.7 %terms.1 = bf16[16,16,256]{2,1,0:T(8,128)(2,1)} custom-call(f32[256,256]{1,0:T(8,128)S(1)} %get-tuple-element.30.own, bf16[256,256]{1,0:T(8,128)(2,1)S(1)} %collective-permute-done.6.near, bf16[256,256]{1,0:T(8,128)(2,1)S(1)} %collective-permute-done.7.far), custom_call_target="tpu_custom_call" | custom-call | flops 17179869184 | bytes 1048576 | tf_op jit(solution)/shard_map/terms/pallas_call | solution.py:317
  38.7 19.5 %all-to-all-start = ((bf16[16,16,256]{2,1,0:T(8,128)(2,1)}), bf16[16,16,256]{2,1,0:T(8,128)(2,1)S(1)}, u32[]{:S(2)}, u32[]{:S(2)}) async-start(bf16[16,16,256]{2,1,0:T(8,128)(2,1)} %terms.1), calls=%async_computation | async-start | bytes 262144 | tf_op jit(solution)/shard_map/all_to_all | solution.py:467
  58.3 0.0 collective-permute-done.4.dq_y
  58.3 2.3 %collective-permute-start.5 = (bf16[512,128]{1,0:T(8,128)(2,1)S(1)}, bf16[512,128]{1,0:T(8,128)(2,1)S(1)}, u32[]{:S(2)}, u32[]{:S(2)}) collective-permute-start(bf16[512,128]{1,0:T(8,128)(2,1)S(1)} %get-tuple-element.29), channel_id=1, source_target_pairs={{1,0},{0,1},{3,2},{2,3},{5,4},{4,5},{7,6},{6,7},{9,8},{8,9},{11,10... | collective-permute-start | bytes 393224 | tf_op jit(solution)/shard_map/ppermute | solution.py:73
  60.6 1.0 %collective-permute-done.5.dq_core = bf16[512,128]{1,0:T(8,128)(2,1)S(1)} collective-permute-done((bf16[512,128]{1,0:T(8,128)(2,1)S(1)}, bf16[512,128]{1,0:T(8,128)(2,1)S(1)}, u32[]{:S(2)}, u32[]{:S(2)}) %collective-permute-start.5) | collective-permute-done | bytes 131104 | tf_op jit(solution)/shard_map/ppermute | solution.py:73
  61.6 0.7 %query.1 = bf16[256,256]{1,0:T(8,128)(2,1)} custom-call(f32[512,128]{1,0:T(8,128)S(1)} %get-tuple-element.28.part, bf16[512,128]{1,0:T(8,128)(2,1)S(1)} %collective-permute-done.5.dq_core), custom_call_target="tpu_custom_call" | custom-call | flops 134217728 | bytes 1048576 | tf_op jit(solution)/shard_map/query/pallas_call | solution.py:317
  62.3 5.1 %all-to-all-done.terms = bf16[16,16,256]{2,1,0:T(8,128)(2,1)S(1)} async-done(((bf16[16,16,256]{2,1,0:T(8,128)(2,1)}), bf16[16,16,256]{2,1,0:T(8,128)(2,1)S(1)}, u32[]{:S(2)}, u32[]{:S(2)}) %all-to-all-start) | async-done | bytes 131104 | tf_op jit(solution)/shard_map/all_to_all | solution.py:467
  67.4 0.6 key_value.1
  (3 shorter events, 0.1 us)
Async XLA Ops:
  1.9 12.6 %collective-permute-start = (bf16[1088,128]{1,0:T(8,128)(2,1)S(1)}, bf16[1088,128]{1,0:T(8,128)(2,1)S(1)}, u32[]{:S(2)}, u32[]{:S(2)}) collective-permute-start(bf16[1088,128]{1,0:T(8,128)(2,1)S(1)} %get-tuple-element.19.own.msg), channel_id=1, source_target_pairs={{4,0},{5,1},{6,2},{7,3},{0,4},{1,5},{2,6},{3,7},{12,8},{13,9},{14,... | collective-permute-start | bytes 835592 | tf_op jit(solution)/shard_map/ppermute | solution.py:73
  5.1 17.3 %collective-permute-start.2 = (bf16[256,256]{1,0:T(8,128)(2,1)S(1)}, bf16[256,256]{1,0:T(8,128)(2,1)S(1)}, u32[]{:S(2)}, u32[]{:S(2)}) collective-permute-start(bf16[256,256]{1,0:T(8,128)(2,1)S(1)} %get-tuple-element.20.kv), channel_id=1, source_target_pairs={{432,0},{467,1},{434,2},{465,3},{454,4},{421,5},{452,6},{423,7},{4... | collective-permute-start | bytes 393224 | tf_op jit(solution)/shard_map/ppermute | solution.py:73
  12.6 10.0 %collective-permute-start.1 = (bf16[256,256]{1,0:T(8,128)(2,1)S(1)}, bf16[256,256]{1,0:T(8,128)(2,1)S(1)}, u32[]{:S(2)}, u32[]{:S(2)}) collective-permute-start(bf16[256,256]{1,0:T(8,128)(2,1)S(1)} %get-tuple-element.20.kv), channel_id=1, source_target_pairs={{498,0},{401,1},{496,2},{403,3},{388,4},{487,5},{390,6},{485,7},{5... | collective-permute-start | bytes 393224 | tf_op jit(solution)/shard_map/ppermute | solution.py:73
  14.6 9.4 %collective-permute-start.3 = (bf16[2176,128]{1,0:T(8,128)(2,1)S(1)}, bf16[2176,128]{1,0:T(8,128)(2,1)S(1)}, u32[]{:S(2)}, u32[]{:S(2)}) collective-permute-start(bf16[2176,128]{1,0:T(8,128)(2,1)S(1)} %pad_maximum_fusion), channel_id=1, source_target_pairs={{1,0},{0,1},{3,2},{2,3},{5,4},{4,5},{7,6},{6,7},{9,8},{8,9},{11,10... | collective-permute-start | bytes 1671176 | tf_op jit(solution)/shard_map/ppermute | solution.py:73
  24.2 13.8 %collective-permute-start.6 = (bf16[256,256]{1,0:T(8,128)(2,1)S(1)}, bf16[256,256]{1,0:T(8,128)(2,1)S(1)}, u32[]{:S(2)}, u32[]{:S(2)}) collective-permute-start(bf16[256,256]{1,0:T(8,128)(2,1)S(1)} %get-tuple-element.31), channel_id=1, source_target_pairs={{0,498},{1,401},{2,496},{3,403},{4,388},{5,487},{6,390},{7,485},{8... | collective-permute-start | bytes 393224 | tf_op jit(solution)/shard_map/ppermute | solution.py:73
  28.7 9.3 %collective-permute-start.7 = (bf16[256,256]{1,0:T(8,128)(2,1)S(1)}, bf16[256,256]{1,0:T(8,128)(2,1)S(1)}, u32[]{:S(2)}, u32[]{:S(2)}) collective-permute-start(bf16[256,256]{1,0:T(8,128)(2,1)S(1)} %get-tuple-element.32), channel_id=1, source_target_pairs={{0,432},{1,467},{2,434},{3,465},{4,454},{5,421},{6,452},{7,423},{8... | collective-permute-start | bytes 393224 | tf_op jit(solution)/shard_map/ppermute | solution.py:73
  34.4 23.8 %collective-permute-start.4 = (bf16[1024,128]{1,0:T(8,128)(2,1)S(1)}, bf16[1024,128]{1,0:T(8,128)(2,1)S(1)}, u32[]{:S(2)}, u32[]{:S(2)}) collective-permute-start(bf16[1024,128]{1,0:T(8,128)(2,1)S(1)} %get-tuple-element.27), channel_id=1, source_target_pairs={{4,0},{5,1},{6,2},{7,3},{0,4},{1,5},{2,6},{3,7},{12,8},{13,9},{14,... | collective-permute-start | bytes 786440 | tf_op jit(solution)/shard_map/ppermute | solution.py:73
  38.7 28.7 %all-to-all-start = ((bf16[16,16,256]{2,1,0:T(8,128)(2,1)}), bf16[16,16,256]{2,1,0:T(8,128)(2,1)S(1)}, u32[]{:S(2)}, u32[]{:S(2)}) async-start(bf16[16,16,256]{2,1,0:T(8,128)(2,1)} %terms.1), calls=%async_computation | async-start | bytes 262144 | tf_op jit(solution)/shard_map/all_to_all | solution.py:467
  58.3 3.2 %collective-permute-start.5 = (bf16[512,128]{1,0:T(8,128)(2,1)S(1)}, bf16[512,128]{1,0:T(8,128)(2,1)S(1)}, u32[]{:S(2)}, u32[]{:S(2)}) collective-permute-start(bf16[512,128]{1,0:T(8,128)(2,1)S(1)} %get-tuple-element.29), channel_id=1, source_target_pairs={{1,0},{0,1},{3,2},{2,3},{5,4},{4,5},{7,6},{6,7},{9,8},{8,9},{11,10... | collective-permute-start | bytes 393224 | tf_op jit(solution)/shard_map/ppermute | solution.py:73
